TPU v7x, 32 devices: a whole 2x2x4 slice. The times are simulated.
32 devices in a mesh: scen: 2 (over x), lx: 4 (over y, core), ly: 4 (over z).
Axes of the slice: x: 2, y: 2, z: 4, core: 2. Of those that a mesh axis runs over, the one named last changes fastest.
Arguments:
- density: float32 [2, 512, 2048], P('scen', 'lx', 'ly'), may hold values from 0.2 to 1.5
- trait: float32 [2, 512, 2048], P('scen', 'lx', 'ly'), may hold values from -4 to 4
- variance: float32 [2, 512, 2048], P('scen', 'lx', 'ly'), may hold values from 0.1 to 1
- optimum: float32 [2, 512, 2048], P('scen', 'lx', 'ly'), may hold values from -4 to 4
- observed: float32 [2, 512, 2048], P('scen', 'lx', 'ly'), may hold values from 0 to 1.5
- obs_step: int32 [2, 512], P('scen', 'lx'), may hold values from 1 to 2
- land_code: int32 [512, 2048], P('lx', 'ly'), may hold values 0 or 1
- maps: float32 [2, 512, 2048], P(None, 'lx', 'ly'), may hold values from -4 to 4
- first_moment: float32 [2, 512, 2048], P(None, 'lx', 'ly'), may hold values from -3 to 3
- second_moment: float32 [2, 512, 2048], P(None, 'lx', 'ly'), may hold values from 0.01 to 1
Outputs:
- new_maps: float32 [2, 512, 2048], P(None, 'lx', 'ly')
- new_first: float32 [2, 512, 2048], P(None, 'lx', 'ly')
- new_second: float32 [2, 512, 2048], P(None, 'lx', 'ly')
Inputs may be any that keep to these rules, and one draw needn't show every extreme that they name: `land_code`: 1 marks land, 0 sea.
All inputs are finite; a program needn't handle non-finite values. No bound on the sum of `land_code` on one device may be relied on, other than what follows from the above.
Results may differ from a plain program's by a relative error of at most 0.0003.
Values sent between devices are 32-bit elements; how exact they have to be, the bound alone decides.
No kernel may reach another device: no remote copies, remote signals or barrier semaphores. Data moves between devices by JAX's collectives and lax.ppermute only.
A program may use at most 64 MiB of HBM per device.

v0:
```python
import jax
import jax.numpy as jnp
from jax import lax
from jax.sharding import PartitionSpec as P

STEPS = 2
ADAM_STEP = 10


REACH_MAX = 0.2
PRIOR_WEIGHT = 0.1
GROWTH_RATE = 0.5
MUTATION_INPUT = 0.02
LEARN_RATE = 0.01
BETA_FIRST = 0.9
BETA_SECOND = 0.999
ADAM_EPS = 1e-08
LOSS_WEIGHT = 2.0


def extended(block, sides, width):
    for axis, dim in sides:
        count = lax.axis_size(axis)
        forward = [(i, i + 1) for i in range(count - 1)]
        backward = [(target, source) for source, target in forward]
        low = lax.ppermute(
            lax.slice_in_dim(block, block.shape[dim] - width, None, axis=dim), axis, forward
        )
        high = lax.ppermute(lax.slice_in_dim(block, 0, width, axis=dim), axis, backward)
        block = jnp.concatenate([low, block, high], axis=dim)
    return block


def interior(values):
    return values[..., 1:-1, 1:-1]


def advance(fields, raw_maps, optimum_map, land_frac):
    density_now, trait_now, variance_now = (fields[0], fields[1], fields[2])
    reach_map = REACH_MAX * jax.nn.sigmoid(raw_maps[0])
    selection = jax.nn.softplus(interior(raw_maps[1]))
    carried = density_now * trait_now
    moment_two = density_now * (variance_now + trait_now * trait_now)
    reach_mid = interior(reach_map)
    land_mid = interior(land_frac)
    cuts = (
        (slice(2, None), slice(1, -1)),
        (slice(None, -2), slice(1, -1)),
        (slice(1, -1), slice(2, None)),
        (slice(1, -1), slice(None, -2)),
    )
    spread_density = interior(density_now)
    spread_carried = interior(carried)
    spread_moment = interior(moment_two)
    for row_cut, col_cut in cuts:
        weight = (
            0.5 * (reach_mid + reach_map[row_cut, col_cut]) * land_mid * land_frac[row_cut, col_cut]
        )
        spread_density = spread_density + weight * (
            density_now[row_cut, col_cut] - interior(density_now)
        )
        spread_carried = spread_carried + weight * (carried[row_cut, col_cut] - interior(carried))
        spread_moment = spread_moment + weight * (
            moment_two[row_cut, col_cut] - interior(moment_two)
        )
    trait_mid = interior(trait_now)
    variance_mid = interior(variance_now)
    denominator = spread_density + PRIOR_WEIGHT
    trait_spread = (spread_carried + PRIOR_WEIGHT * trait_mid) / denominator
    second_spread = (
        spread_moment + PRIOR_WEIGHT * (variance_mid + trait_mid * trait_mid)
    ) / denominator
    variance_spread = second_spread - trait_spread * trait_spread
    offset = trait_spread - interior(optimum_map)
    growth = land_mid * (
        GROWTH_RATE * (1.0 - spread_density) - 0.5 * selection * (offset * offset + variance_spread)
    )
    density_new = spread_density * jnp.exp(growth)
    response = selection * variance_spread
    trait_new = trait_spread - response * offset / (1.0 + response)
    variance_new = variance_spread / (1.0 + response) + MUTATION_INPUT
    return jnp.stack([density_new, trait_new, variance_new])


def adam_update(raw_maps, first_now, second_now, gradient):
    first_new = BETA_FIRST * first_now + (1.0 - BETA_FIRST) * gradient
    second_new = BETA_SECOND * second_now + (1.0 - BETA_SECOND) * gradient * gradient
    first_hat = first_new / (1.0 - BETA_FIRST**ADAM_STEP)
    second_hat = second_new / (1.0 - BETA_SECOND**ADAM_STEP)
    maps_new = raw_maps - LEARN_RATE * first_hat / (jnp.sqrt(second_hat) + ADAM_EPS)
    return (maps_new, first_new, second_new)


def state_halo(fields):
    return extended(fields, (("lx", 1), ("ly", 2)), 2)


def adjoint_halo(adjoint_now):
    return extended(adjoint_now, (("lx", 1), ("ly", 2)), 1)


def shards(
    density,
    trait,
    variance,
    optimum,
    observed,
    obs_step,
    land_code,
    maps,
    first_moment,
    second_moment,
):
    land_frac = land_code.astype(jnp.float32)
    statics = jnp.concatenate([maps, optimum, land_frac[None]], axis=0)
    fields = jnp.concatenate([density, trait, variance], axis=0)
    padded_states = []
    later_states = []
    static_wide = extended(statics, (("lx", 1), ("ly", 2)), 2)
    raw_near = interior(static_wide[0:2])
    optimum_near = interior(static_wide[2])
    land_near = interior(static_wide[3])
    for step_index in range(STEPS):
        padded = state_halo(fields)
        padded_states.append(padded)
        fields = advance(interior(padded), raw_near, optimum_near, land_near)
        later_states.append(fields)
    raw_wide = static_wide[0:2]
    optimum_wide = static_wide[2]
    land_wide = static_wide[3]
    chosen_rows = obs_step[0]

    def forward_wide(field_block, raw_block):
        return advance(field_block, raw_block, optimum_wide, land_wide)

    adjoint_now = jnp.zeros_like(later_states[-1])
    gradient = jnp.zeros(maps.shape, jnp.float32)
    for step_index in reversed(range(STEPS)):
        chosen = (chosen_rows == step_index + 1).astype(jnp.float32)[:, None]
        source = (
            2.0 * LOSS_WEIGHT * chosen * land_frac * (later_states[step_index][0] - observed[0])
        )
        blank = jnp.zeros_like(source)
        adjoint_now = adjoint_now + jnp.stack([source, blank, blank])
        adjoint_wide = adjoint_halo(adjoint_now)
        outputs, pullback = jax.vjp(forward_wide, padded_states[step_index], raw_wide)
        cot_fields, cot_maps = pullback(adjoint_wide)
        adjoint_now = cot_fields[:, 2:-2, 2:-2]
        gradient = gradient + cot_maps[:, 2:-2, 2:-2]
    share = lax.psum_scatter(gradient, "scen", scatter_dimension=1, tiled=True)
    share_rows = share.shape[1]
    row_start = lax.axis_index("scen") * share_rows
    maps_own = lax.dynamic_slice_in_dim(maps, row_start, share_rows, 1)
    first_own = lax.dynamic_slice_in_dim(first_moment, row_start, share_rows, 1)
    second_own = lax.dynamic_slice_in_dim(second_moment, row_start, share_rows, 1)
    maps_part, first_part, second_part = adam_update(maps_own, first_own, second_own, share)
    new_maps, new_first, new_second = (
        lax.all_gather(maps_part, "scen", axis=1, tiled=True),
        lax.all_gather(first_part, "scen", axis=1, tiled=True),
        lax.all_gather(second_part, "scen", axis=1, tiled=True),
    )
    return (new_maps, new_first, new_second)


def solution(mesh):
    in_specs = (
        P("scen", "lx", "ly"),
        P("scen", "lx", "ly"),
        P("scen", "lx", "ly"),
        P("scen", "lx", "ly"),
        P("scen", "lx", "ly"),
        P("scen", "lx"),
        P("lx", "ly"),
        P(None, "lx", "ly"),
        P(None, "lx", "ly"),
        P(None, "lx", "ly"),
    )
    out_specs = (P(None, "lx", "ly"), P(None, "lx", "ly"), P(None, "lx", "ly"))
    return jax.shard_map(shards, mesh=mesh, in_specs=in_specs, out_specs=out_specs, check_vma=False)
```

profile of v0, /device:TPU:0, one launch (start us, length us, event | category | flops | bytes accessed | tf_op | source)
XLA Modules:
  0.0 169.7 jit_solution(1790507146723061573)
XLA Ops:
  7.2 1.0 constant_dynamic-update-slice_fusion.2
  10.3 2.4 %collective-permute-start = (f32[3,2,512]{2,1,0:T(2,128)S(1)}, f32[3,2,512]{2,1,0:T(2,128)S(1)}, u32[]{:S(2)}, u32[]{:S(2)}) collective-permute-start(f32[3,2,512]{2,1,0:T(2,128)S(1)} %get-tuple-element.119), channel_id=1, source_target_pairs={{0,4},{4,8},{8,12},{1,5},{5,9},{9,13},{2,6},{6,10},{10,14},{3,7},{... | collective-permute-start | bytes 36872 | tf_op jit(solution)/shard_map/ppermute | solution.py:26
  12.6 1.3 collective-permute-start.1
  14.0 5.2 %collective-permute-start.4 = (f32[4,2,512]{2,1,0:T(2,128)S(1)}, f32[4,2,512]{2,1,0:T(2,128)S(1)}, u32[]{:S(2)}, u32[]{:S(2)}) collective-permute-start(f32[4,2,512]{2,1,0:T(2,128)S(1)} %get-tuple-element.85), channel_id=1, source_target_pairs={{0,4},{4,8},{8,12},{1,5},{5,9},{9,13},{2,6},{6,10},{10,14},{3,7},{... | collective-permute-start | bytes 49160 | tf_op jit(solution)/shard_map/ppermute | solution.py:26
  19.2 1.3 collective-permute-start.5
  20.7 3.5 %collective-permute-start.2 = (f32[3,132,2]{2,1,0:T(8,128)S(1)}, f32[3,132,2]{2,1,0:T(8,128)S(1)}, u32[]{:S(2)}, u32[]{:S(2)}) collective-permute-start(f32[3,132,2]{2,1,0:T(8,128)S(1)} %get-tuple-element.109), channel_id=1, source_target_pairs={{0,1},{1,2},{2,3},{4,5},{5,6},{6,7},{8,9},{9,10},{10,11},{12,13},{... | collective-permute-start | bytes 9512 | tf_op jit(solution)/shard_map/ppermute | solution.py:26
  24.2 1.3 collective-permute-start.3
  25.5 2.8 %collective-permute-done.2 = f32[3,132,2]{2,1,0:T(8,128)S(1)} collective-permute-done((f32[3,132,2]{2,1,0:T(8,128)S(1)}, f32[3,132,2]{2,1,0:T(8,128)S(1)}, u32[]{:S(2)}, u32[]{:S(2)}) %collective-permute-start.2) | collective-permute-done | bytes 3200 | tf_op jit(solution)/shard_map/ppermute | solution.py:26
  28.2 4.7 %collective-permute-done.3 = f32[3,132,2]{2,1,0:T(8,128)S(1)} collective-permute-done((f32[3,132,2]{2,1,0:T(8,128)S(1)}, f32[3,132,2]{2,1,0:T(8,128)S(1)}, u32[]{:S(2)}, u32[]{:S(2)}) %collective-permute-start.3) | collective-permute-done | bytes 3200 | tf_op jit(solution)/shard_map/ppermute | solution.py:29
  33.9 3.5 %collective-permute-start.6 = (f32[4,132,2]{2,1,0:T(8,128)S(1)}, f32[4,132,2]{2,1,0:T(8,128)S(1)}, u32[]{:S(2)}, u32[]{:S(2)}) collective-permute-start(f32[4,132,2]{2,1,0:T(8,128)S(1)} %get-tuple-element.83), channel_id=1, source_target_pairs={{0,1},{1,2},{2,3},{4,5},{5,6},{6,7},{8,9},{9,10},{10,11},{12,13},{... | collective-permute-start | bytes 12680 | tf_op jit(solution)/shard_map/ppermute | solution.py:26
  37.4 1.3 collective-permute-start.7
  39.1 5.4 %collective-permute-done.6 = f32[4,132,2]{2,1,0:T(8,128)S(1)} collective-permute-done((f32[4,132,2]{2,1,0:T(8,128)S(1)}, f32[4,132,2]{2,1,0:T(8,128)S(1)}, u32[]{:S(2)}, u32[]{:S(2)}) %collective-permute-start.6) | collective-permute-done | bytes 4256 | tf_op jit(solution)/shard_map/ppermute | solution.py:26
  44.4 4.1 %collective-permute-done.7 = f32[4,132,2]{2,1,0:T(8,128)S(1)} collective-permute-done((f32[4,132,2]{2,1,0:T(8,128)S(1)}, f32[4,132,2]{2,1,0:T(8,128)S(1)}, u32[]{:S(2)}, u32[]{:S(2)}) %collective-permute-start.7) | collective-permute-done | bytes 4256 | tf_op jit(solution)/shard_map/ppermute | solution.py:29
  50.5 1.1 fusion.112
  52.0 1.7 %collective-permute-start.8 = (f32[3,2,512]{2,1,0:T(2,128)S(1)}, f32[3,2,512]{2,1,0:T(2,128)S(1)}, u32[]{:S(2)}, u32[]{:S(2)}) collective-permute-start(f32[3,2,512]{2,1,0:T(2,128)S(1)} %get-tuple-element.117), channel_id=1, source_target_pairs={{0,4},{4,8},{8,12},{1,5},{5,9},{9,13},{2,6},{6,10},{10,14},{3,7},{... | collective-permute-start | bytes 36872 | tf_op jit(solution)/shard_map/ppermute | solution.py:26
  53.7 1.3 collective-permute-start.9
  55.0 1.8 %collective-permute-done.9 = f32[3,2,512]{2,1,0:T(2,128)S(1)} collective-permute-done((f32[3,2,512]{2,1,0:T(2,128)S(1)}, f32[3,2,512]{2,1,0:T(2,128)S(1)}, u32[]{:S(2)}, u32[]{:S(2)}) %collective-permute-start.9) | collective-permute-done | bytes 12320 | tf_op jit(solution)/shard_map/ppermute | solution.py:29
  56.9 3.5 %collective-permute-start.10 = (f32[3,132,2]{2,1,0:T(8,128)S(1)}, f32[3,132,2]{2,1,0:T(8,128)S(1)}, u32[]{:S(2)}, u32[]{:S(2)}) collective-permute-start(f32[3,132,2]{2,1,0:T(8,128)S(1)} %get-tuple-element.107), channel_id=1, source_target_pairs={{0,1},{1,2},{2,3},{4,5},{5,6},{6,7},{8,9},{9,10},{10,11},{12,13},{... | collective-permute-start | bytes 9512 | tf_op jit(solution)/shard_map/ppermute | solution.py:26
  60.4 1.3 collective-permute-start.11
  61.8 2.6 %collective-permute-done.10 = f32[3,132,2]{2,1,0:T(8,128)S(1)} collective-permute-done((f32[3,132,2]{2,1,0:T(8,128)S(1)}, f32[3,132,2]{2,1,0:T(8,128)S(1)}, u32[]{:S(2)}, u32[]{:S(2)}) %collective-permute-start.10) | collective-permute-done | bytes 3200 | tf_op jit(solution)/shard_map/ppermute | solution.py:26
  64.4 4.7 %collective-permute-done.11 = f32[3,132,2]{2,1,0:T(8,128)S(1)} collective-permute-done((f32[3,132,2]{2,1,0:T(8,128)S(1)}, f32[3,132,2]{2,1,0:T(8,128)S(1)}, u32[]{:S(2)}, u32[]{:S(2)}) %collective-permute-start.11) | collective-permute-done | bytes 3200 | tf_op jit(solution)/shard_map/ppermute | solution.py:29
  70.3 1.4 fusion.110
  71.7 2.9 %collective-permute-start.12 = (f32[3,1,512]{2,1,0:T(1,128)S(1)}, f32[3,1,512]{2,1,0:T(1,128)S(1)}, u32[]{:S(2)}, u32[]{:S(2)}) collective-permute-start(f32[3,1,512]{2,1,0:T(1,128)S(1)} %get-tuple-element.147), channel_id=1, source_target_pairs={{0,4},{4,8},{8,12},{1,5},{5,9},{9,13},{2,6},{6,10},{10,14},{3,7},{... | collective-permute-start | bytes 18440 | tf_op jit(solution)/shard_map/ppermute | solution.py:26
  74.6 1.3 collective-permute-start.13
  76.2 1.5 collective-permute-done.13
  77.8 2.5 %collective-permute-start.14 = (f32[3,130,1]{2,1,0:T(8,128)S(1)}, f32[3,130,1]{2,1,0:T(8,128)S(1)}, u32[]{:S(2)}, u32[]{:S(2)}) collective-permute-start(f32[3,130,1]{2,1,0:T(8,128)S(1)} %get-tuple-element.113), channel_id=1, source_target_pairs={{0,1},{1,2},{2,3},{4,5},{5,6},{6,7},{8,9},{9,10},{10,11},{12,13},{... | collective-permute-start | bytes 4688 | tf_op jit(solution)/shard_map/ppermute | solution.py:26
  80.3 1.5 collective-permute-start.15
  81.9 3.0 %collective-permute-done.14 = f32[3,130,1]{2,1,0:T(8,128)S(1)} collective-permute-done((f32[3,130,1]{2,1,0:T(8,128)S(1)}, f32[3,130,1]{2,1,0:T(8,128)S(1)}, u32[]{:S(2)}, u32[]{:S(2)}) %collective-permute-start.14) | collective-permute-done | bytes 1592 | tf_op jit(solution)/shard_map/ppermute | solution.py:26
  84.9 4.7 %collective-permute-done.15 = f32[3,130,1]{2,1,0:T(8,128)S(1)} collective-permute-done((f32[3,130,1]{2,1,0:T(8,128)S(1)}, f32[3,130,1]{2,1,0:T(8,128)S(1)}, u32[]{:S(2)}, u32[]{:S(2)}) %collective-permute-start.15) | collective-permute-done | bytes 1592 | tf_op jit(solution)/shard_map/ppermute | solution.py:29
  90.1 2.4 %add_multiply_fusion.2 = (f32[130,514]{1,0:T(8,128)S(1)}, f32[130,514]{1,0:T(8,128)S(1)}, f32[130,514]{1,0:T(8,128)S(1)}, f32[130,514]{1,0:T(8,128)S(1)}, f32[13...) fusion(f32[132,516]{1,0:T(8,128)S(1)} %get-tuple-element.81, ...), kind=kLoop, calls=%fused_computation.139 | loop fusion | flops 7216560 | bytes 10958480 | tf_op jit(solution)/shard_map/transpose(jvp(jit(softplus)))/mul | solution.py:41
  92.5 2.3 %add_add_fusion.7 = (f32[130,514]{1,0:T(8,128)S(1)}, f32[130,514]{1,0:T(8,128)S(1)}, f32[130,514]{1,0:T(8,128)S(1)}, f32[130,514]{1,0:T(8,128)S(1)}, f32[130,514...) fusion(f32[132,516]{1,0:T(8,128)S(1)} %get-tuple-element.82, ...), kind=kLoop, calls=%fused_computation.131 | loop fusion | flops 7016100 | bytes 9889360 | tf_op jit(solution)/shard_map/transpose(jvp())/add_any | solution.py:57
  95.5 1.1 add_bitcast_fusion.1
  96.6 1.1 fusion.3
  99.0 2.3 %collective-permute-start.16 = (f32[3,1,512]{2,1,0:T(1,128)S(1)}, f32[3,1,512]{2,1,0:T(1,128)S(1)}, u32[]{:S(2)}, u32[]{:S(2)}) collective-permute-start(f32[3,1,512]{2,1,0:T(1,128)S(1)} %get-tuple-element.115), channel_id=1, source_target_pairs={{0,4},{4,8},{8,12},{1,5},{5,9},{9,13},{2,6},{6,10},{10,14},{3,7},{... | collective-permute-start | bytes 18440 | tf_op jit(solution)/shard_map/ppermute | solution.py:26
  101.4 1.3 collective-permute-start.17
  102.7 1.7 collective-permute-done.17
  104.6 1.9 %collective-permute-start.18 = (f32[3,130,1]{2,1,0:T(8,128)S(1)}, f32[3,130,1]{2,1,0:T(8,128)S(1)}, u32[]{:S(2)}, u32[]{:S(2)}) collective-permute-start(f32[3,130,1]{2,1,0:T(8,128)S(1)} %get-tuple-element.111), channel_id=1, source_target_pairs={{0,1},{1,2},{2,3},{4,5},{5,6},{6,7},{8,9},{9,10},{10,11},{12,13},{... | collective-permute-start | bytes 4688 | tf_op jit(solution)/shard_map/ppermute | solution.py:26
  106.5 1.5 collective-permute-start.19
  108.2 2.9 %collective-permute-done.18 = f32[3,130,1]{2,1,0:T(8,128)S(1)} collective-permute-done((f32[3,130,1]{2,1,0:T(8,128)S(1)}, f32[3,130,1]{2,1,0:T(8,128)S(1)}, u32[]{:S(2)}, u32[]{:S(2)}) %collective-permute-start.18) | collective-permute-done | bytes 1592 | tf_op jit(solution)/shard_map/ppermute | solution.py:26
  111.1 4.7 %collective-permute-done.19 = f32[3,130,1]{2,1,0:T(8,128)S(1)} collective-permute-done((f32[3,130,1]{2,1,0:T(8,128)S(1)}, f32[3,130,1]{2,1,0:T(8,128)S(1)}, u32[]{:S(2)}, u32[]{:S(2)}) %collective-permute-start.19) | collective-permute-done | bytes 1592 | tf_op jit(solution)/shard_map/ppermute | solution.py:29
  116.3 2.0 %add_multiply_fusion = (f32[130,514]{1,0:T(8,128)S(1)}, f32[130,514]{1,0:T(8,128)S(1)}, f32[130,514]{1,0:T(8,128)S(1)}, f32[130,514]{1,0:T(8,128)S(1)}, f32[130,514]{1,0:T(8,128)S(1)}) fusion(f32[132,516]{1,0:T(8,128)S(1)} %get-tuple-element.81, f32[3,130,514]{2,1,0:T(8,128)S(1)} %pad_maximum_fusion.4, f32[132,516]{1,0:T(8,128)S(1)} %get-tuple-element.82, ...), kind=kLoop, calls=%fused_computation.117 | loop fusion | flops 6147440 | bytes 8552960 | tf_op jit(solution)/shard_map/transpose(jvp(jit(softplus)))/mul | solution.py:41
  119.3 2.3 %add_add_fusion.5 = (f32[130,514]{1,0:T(8,128)S(1)}, f32[130,514]{1,0:T(8,128)S(1)}, f32[130,514]{1,0:T(8,128)S(1)}, f32[130,514]{1,0:T(8,128)S(1)}, f32[130,514]{1,0:T(8,128)S(1)}) fusion(f32[132,516]{1,0:T(8,128)S(1)} %get-tuple-element.82, f32[132,516]{1,0:T(8,128)S(1)} %get-tuple-element.91, f32[130,514]{1,0:T(8,128)S(1)} %get-tuple-element.75, ...), kind=kLoop, calls=%fused_computation.109 | loop fusion | flops 6882460 | bytes 9622080 | tf_op jit(solution)/shard_map/transpose(jvp())/add_any | solution.py:57
  122.5 1.2 fusion.1
  123.7 12.0 %reduce-scatter.2.cloned.1.call-done = f32[2,64,512]{2,1,0:T(8,128)} async-done(((f32[2,128,512]{2,1,0:T(8,128)}), f32[2,64,512]{2,1,0:T(8,128)}) %reduce-scatter.2.cloned.1.call-update) | async-done | bytes 262160 | tf_op jit(solution)/shard_map/reduce_scatter | solution.py:150
  135.8 1.1 divide_subtract_fusion
  136.9 8.7 %all_gather.9 = f32[2,128,512]{2,1,0:T(8,128)S(1)} all-gather(f32[2,64,512]{2,1,0:T(8,128)S(1)} %get-tuple-element.7), channel_id=1, replica_groups=mesh['scen'=2,'lx'=4,'ly'=4] {'scen'}, dimensions={1}, use_global_device_ids=true | all-gather | bytes 786432 | tf_op jit(solution)/shard_map/all_gather | solution.py:158
  145.6 7.8 %all_gather.10 = f32[2,128,512]{2,1,0:T(8,128)S(1)} all-gather(f32[2,64,512]{2,1,0:T(8,128)S(1)} %get-tuple-element.8), channel_id=1, replica_groups=mesh['scen'=2,'lx'=4,'ly'=4] {'scen'}, dimensions={1}, use_global_device_ids=true | all-gather | bytes 786432 | tf_op jit(solution)/shard_map/all_gather | solution.py:159
  153.5 7.0 %all_gather.11 = f32[2,128,512]{2,1,0:T(8,128)S(1)} all-gather(f32[2,64,512]{2,1,0:T(8,128)S(1)} %get-tuple-element.9), channel_id=1, replica_groups=mesh['scen'=2,'lx'=4,'ly'=4] {'scen'}, dimensions={1}, use_global_device_ids=true | all-gather | bytes 786432 | tf_op jit(solution)/shard_map/all_gather | solution.py:160
  (65 shorter events, 15.1 us)
Async XLA Ops:
  7.2 6.8 %copy-start.1 = (s32[128,512]{1,0:T(8,128)S(1)}, s32[128,512]{1,0:T(8,128)}, u32[]{:S(2)}) copy-start(s32[128,512]{1,0:T(8,128)} %param.17) | copy-start | bytes 786436
  7.2 6.8 %copy-start.2 = (f32[1,128,512]{2,1,0:T(8,128)S(1)}, f32[1,128,512]{2,1,0:T(8,128)}, u32[]{:S(2)}) copy-start(f32[1,128,512]{2,1,0:T(8,128)} %param.14) | copy-start | bytes 786436
  7.2 6.8 %copy-start = (f32[2,128,512]{2,1,0:T(8,128)S(1)}, f32[2,128,512]{2,1,0:T(8,128)}, u32[]{:S(2)}) copy-start(f32[2,128,512]{2,1,0:T(8,128)} %param.18) | copy-start | bytes 1572868
  7.2 128.6 %reduce-scatter.2.cloned.1.call-start = ((), (), s32[]{:S(2)}) async-start(), calls=%async_computation.1 | async-start | bytes 786432 | tf_op jit(solution)/shard_map/reduce_scatter | solution.py:150
  10.3 10.2 %collective-permute-start = (f32[3,2,512]{2,1,0:T(2,128)S(1)}, f32[3,2,512]{2,1,0:T(2,128)S(1)}, u32[]{:S(2)}, u32[]{:S(2)}) collective-permute-start(f32[3,2,512]{2,1,0:T(2,128)S(1)} %get-tuple-element.119), channel_id=1, source_target_pairs={{0,4},{4,8},{8,12},{1,5},{5,9},{9,13},{2,6},{6,10},{10,14},{3,7},{... | collective-permute-start | bytes 36872 | tf_op jit(solution)/shard_map/ppermute | solution.py:26
  12.6 12.8 %copy-start.6 = (s32[1,128]{1,0:T(1,128)S(1)}, s32[1,128]{1,0:T(1,128)}, u32[]{:S(2)}) copy-start(s32[1,128]{1,0:T(1,128)} %param.16) | copy-start | bytes 1540
  12.6 7.9 %collective-permute-start.1 = (f32[3,2,512]{2,1,0:T(2,128)S(1)}, f32[3,2,512]{2,1,0:T(2,128)S(1)}, u32[]{:S(2)}, u32[]{:S(2)}) collective-permute-start(f32[3,2,512]{2,1,0:T(2,128)S(1)} %get-tuple-element.120), channel_id=1, source_target_pairs={{4,0},{8,4},{12,8},{5,1},{9,5},{13,9},{6,2},{10,6},{14,10},{7,3},{... | collective-permute-start | bytes 36872 | tf_op jit(solution)/shard_map/ppermute | solution.py:29
  14.0 19.7 %collective-permute-start.4 = (f32[4,2,512]{2,1,0:T(2,128)S(1)}, f32[4,2,512]{2,1,0:T(2,128)S(1)}, u32[]{:S(2)}, u32[]{:S(2)}) collective-permute-start(f32[4,2,512]{2,1,0:T(2,128)S(1)} %get-tuple-element.85), channel_id=1, source_target_pairs={{0,4},{4,8},{8,12},{1,5},{5,9},{9,13},{2,6},{6,10},{10,14},{3,7},{... | collective-permute-start | bytes 49160 | tf_op jit(solution)/shard_map/ppermute | solution.py:26
  19.2 14.6 %collective-permute-start.5 = (f32[4,2,512]{2,1,0:T(2,128)S(1)}, f32[4,2,512]{2,1,0:T(2,128)S(1)}, u32[]{:S(2)}, u32[]{:S(2)}) collective-permute-start(f32[4,2,512]{2,1,0:T(2,128)S(1)} %get-tuple-element.86), channel_id=1, source_target_pairs={{4,0},{8,4},{12,8},{5,1},{9,5},{13,9},{6,2},{10,6},{14,10},{7,3},{... | collective-permute-start | bytes 49160 | tf_op jit(solution)/shard_map/ppermute | solution.py:29
  20.7 7.6 %collective-permute-start.2 = (f32[3,132,2]{2,1,0:T(8,128)S(1)}, f32[3,132,2]{2,1,0:T(8,128)S(1)}, u32[]{:S(2)}, u32[]{:S(2)}) collective-permute-start(f32[3,132,2]{2,1,0:T(8,128)S(1)} %get-tuple-element.109), channel_id=1, source_target_pairs={{0,1},{1,2},{2,3},{4,5},{5,6},{6,7},{8,9},{9,10},{10,11},{12,13},{... | collective-permute-start | bytes 9512 | tf_op jit(solution)/shard_map/ppermute | solution.py:26
  24.2 8.8 %collective-permute-start.3 = (f32[3,132,2]{2,1,0:T(8,128)S(1)}, f32[3,132,2]{2,1,0:T(8,128)S(1)}, u32[]{:S(2)}, u32[]{:S(2)}) collective-permute-start(f32[3,132,2]{2,1,0:T(8,128)S(1)} %get-tuple-element.110), channel_id=1, source_target_pairs={{1,0},{2,1},{3,2},{5,4},{6,5},{7,6},{9,8},{10,9},{11,10},{13,12},{... | collective-permute-start | bytes 9512 | tf_op jit(solution)/shard_map/ppermute | solution.py:29
  33.9 10.5 %collective-permute-start.6 = (f32[4,132,2]{2,1,0:T(8,128)S(1)}, f32[4,132,2]{2,1,0:T(8,128)S(1)}, u32[]{:S(2)}, u32[]{:S(2)}) collective-permute-start(f32[4,132,2]{2,1,0:T(8,128)S(1)} %get-tuple-element.83), channel_id=1, source_target_pairs={{0,1},{1,2},{2,3},{4,5},{5,6},{6,7},{8,9},{9,10},{10,11},{12,13},{... | collective-permute-start | bytes 12680 | tf_op jit(solution)/shard_map/ppermute | solution.py:26
  37.4 11.1 %collective-permute-start.7 = (f32[4,132,2]{2,1,0:T(8,128)S(1)}, f32[4,132,2]{2,1,0:T(8,128)S(1)}, u32[]{:S(2)}, u32[]{:S(2)}) collective-permute-start(f32[4,132,2]{2,1,0:T(8,128)S(1)} %get-tuple-element.84), channel_id=1, source_target_pairs={{1,0},{2,1},{3,2},{5,4},{6,5},{7,6},{9,8},{10,9},{11,10},{13,12},{... | collective-permute-start | bytes 12680 | tf_op jit(solution)/shard_map/ppermute | solution.py:29
  49.5 1.0 copy-start.3
  52.0 3.0 %collective-permute-start.8 = (f32[3,2,512]{2,1,0:T(2,128)S(1)}, f32[3,2,512]{2,1,0:T(2,128)S(1)}, u32[]{:S(2)}, u32[]{:S(2)}) collective-permute-start(f32[3,2,512]{2,1,0:T(2,128)S(1)} %get-tuple-element.117), channel_id=1, source_target_pairs={{0,4},{4,8},{8,12},{1,5},{5,9},{9,13},{2,6},{6,10},{10,14},{3,7},{... | collective-permute-start | bytes 36872 | tf_op jit(solution)/shard_map/ppermute | solution.py:26
  53.7 3.1 %collective-permute-start.9 = (f32[3,2,512]{2,1,0:T(2,128)S(1)}, f32[3,2,512]{2,1,0:T(2,128)S(1)}, u32[]{:S(2)}, u32[]{:S(2)}) collective-permute-start(f32[3,2,512]{2,1,0:T(2,128)S(1)} %get-tuple-element.118), channel_id=1, source_target_pairs={{4,0},{8,4},{12,8},{5,1},{9,5},{13,9},{6,2},{10,6},{14,10},{7,3},{... | collective-permute-start | bytes 36872 | tf_op jit(solution)/shard_map/ppermute | solution.py:29
  56.9 7.5 %collective-permute-start.10 = (f32[3,132,2]{2,1,0:T(8,128)S(1)}, f32[3,132,2]{2,1,0:T(8,128)S(1)}, u32[]{:S(2)}, u32[]{:S(2)}) collective-permute-start(f32[3,132,2]{2,1,0:T(8,128)S(1)} %get-tuple-element.107), channel_id=1, source_target_pairs={{0,1},{1,2},{2,3},{4,5},{5,6},{6,7},{8,9},{9,10},{10,11},{12,13},{... | collective-permute-start | bytes 9512 | tf_op jit(solution)/shard_map/ppermute | solution.py:26
  60.4 8.7 %collective-permute-start.11 = (f32[3,132,2]{2,1,0:T(8,128)S(1)}, f32[3,132,2]{2,1,0:T(8,128)S(1)}, u32[]{:S(2)}, u32[]{:S(2)}) collective-permute-start(f32[3,132,2]{2,1,0:T(8,128)S(1)} %get-tuple-element.108), channel_id=1, source_target_pairs={{1,0},{2,1},{3,2},{5,4},{6,5},{7,6},{9,8},{10,9},{11,10},{13,12},{... | collective-permute-start | bytes 9512 | tf_op jit(solution)/shard_map/ppermute | solution.py:29
  71.7 4.5 %collective-permute-start.12 = (f32[3,1,512]{2,1,0:T(1,128)S(1)}, f32[3,1,512]{2,1,0:T(1,128)S(1)}, u32[]{:S(2)}, u32[]{:S(2)}) collective-permute-start(f32[3,1,512]{2,1,0:T(1,128)S(1)} %get-tuple-element.147), channel_id=1, source_target_pairs={{0,4},{4,8},{8,12},{1,5},{5,9},{9,13},{2,6},{6,10},{10,14},{3,7},{... | collective-permute-start | bytes 18440 | tf_op jit(solution)/shard_map/ppermute | solution.py:26
  74.6 3.1 %collective-permute-start.13 = (f32[3,1,512]{2,1,0:T(1,128)S(1)}, f32[3,1,512]{2,1,0:T(1,128)S(1)}, u32[]{:S(2)}, u32[]{:S(2)}) collective-permute-start(f32[3,1,512]{2,1,0:T(1,128)S(1)} %get-tuple-element.148), channel_id=1, source_target_pairs={{4,0},{8,4},{12,8},{5,1},{9,5},{13,9},{6,2},{10,6},{14,10},{7,3},{... | collective-permute-start | bytes 18440 | tf_op jit(solution)/shard_map/ppermute | solution.py:29
  77.8 7.1 %collective-permute-start.14 = (f32[3,130,1]{2,1,0:T(8,128)S(1)}, f32[3,130,1]{2,1,0:T(8,128)S(1)}, u32[]{:S(2)}, u32[]{:S(2)}) collective-permute-start(f32[3,130,1]{2,1,0:T(8,128)S(1)} %get-tuple-element.113), channel_id=1, source_target_pairs={{0,1},{1,2},{2,3},{4,5},{5,6},{6,7},{8,9},{9,10},{10,11},{12,13},{... | collective-permute-start | bytes 4688 | tf_op jit(solution)/shard_map/ppermute | solution.py:26
  80.3 9.3 %collective-permute-start.15 = (f32[3,130,1]{2,1,0:T(8,128)S(1)}, f32[3,130,1]{2,1,0:T(8,128)S(1)}, u32[]{:S(2)}, u32[]{:S(2)}) collective-permute-start(f32[3,130,1]{2,1,0:T(8,128)S(1)} %get-tuple-element.114), channel_id=1, source_target_pairs={{1,0},{2,1},{3,2},{5,4},{6,5},{7,6},{9,8},{10,9},{11,10},{13,12},{... | collective-permute-start | bytes 4688 | tf_op jit(solution)/shard_map/ppermute | solution.py:29
  99.0 3.7 %collective-permute-start.16 = (f32[3,1,512]{2,1,0:T(1,128)S(1)}, f32[3,1,512]{2,1,0:T(1,128)S(1)}, u32[]{:S(2)}, u32[]{:S(2)}) collective-permute-start(f32[3,1,512]{2,1,0:T(1,128)S(1)} %get-tuple-element.115), channel_id=1, source_target_pairs={{0,4},{4,8},{8,12},{1,5},{5,9},{9,13},{2,6},{6,10},{10,14},{3,7},{... | collective-permute-start | bytes 18440 | tf_op jit(solution)/shard_map/ppermute | solution.py:26
  101.4 3.1 %collective-permute-start.17 = (f32[3,1,512]{2,1,0:T(1,128)S(1)}, f32[3,1,512]{2,1,0:T(1,128)S(1)}, u32[]{:S(2)}, u32[]{:S(2)}) collective-permute-start(f32[3,1,512]{2,1,0:T(1,128)S(1)} %get-tuple-element.116), channel_id=1, source_target_pairs={{4,0},{8,4},{12,8},{5,1},{9,5},{13,9},{6,2},{10,6},{14,10},{7,3},{... | collective-permute-start | bytes 18440 | tf_op jit(solution)/shard_map/ppermute | solution.py:29
  104.6 6.5 %collective-permute-start.18 = (f32[3,130,1]{2,1,0:T(8,128)S(1)}, f32[3,130,1]{2,1,0:T(8,128)S(1)}, u32[]{:S(2)}, u32[]{:S(2)}) collective-permute-start(f32[3,130,1]{2,1,0:T(8,128)S(1)} %get-tuple-element.111), channel_id=1, source_target_pairs={{0,1},{1,2},{2,3},{4,5},{5,6},{6,7},{8,9},{9,10},{10,11},{12,13},{... | collective-permute-start | bytes 4688 | tf_op jit(solution)/shard_map/ppermute | solution.py:26
  106.5 9.3 %collective-permute-start.19 = (f32[3,130,1]{2,1,0:T(8,128)S(1)}, f32[3,130,1]{2,1,0:T(8,128)S(1)}, u32[]{:S(2)}, u32[]{:S(2)}) collective-permute-start(f32[3,130,1]{2,1,0:T(8,128)S(1)} %get-tuple-element.112), channel_id=1, source_target_pairs={{1,0},{2,1},{3,2},{5,4},{6,5},{7,6},{9,8},{10,9},{11,10},{13,12},{... | collective-permute-start | bytes 4688 | tf_op jit(solution)/shard_map/ppermute | solution.py:29
  122.5 13.2 %copy-start.4 = (f32[2,128,512]{2,1,0:T(8,128)S(1)}, f32[2,128,512]{2,1,0:T(8,128)}, u32[]{:S(2)}) copy-start(f32[2,128,512]{2,1,0:T(8,128)} %param.19) | copy-start | bytes 1572868
  122.5 13.2 %copy-start.5 = (f32[2,128,512]{2,1,0:T(8,128)S(1)}, f32[2,128,512]{2,1,0:T(8,128)}, u32[]{:S(2)}) copy-start(f32[2,128,512]{2,1,0:T(8,128)} %param.20) | copy-start | bytes 1572868
Sparse Core Ops, SparseCore 0:
  123.8 11.8 reduce-scatter.1
where the time goes:
time: 170 us
  waiting for transfers between devices  56.7 us (33%)
  starting transfers between devices  42.7 us (25%)
  other arithmetic  25.3 us (15%)
  blocking collectives  23.6 us (14%)
  between operations  14.6 us (9%)
  local copies, waits for them, and re-layouts  6.76 us (4%)
    ppermute x10, starting transfers between devices, extended(): lax.ppermute(lax.slice_in_dim(block, block.shape[dim] - width, None, axis...  29.4 us
    ppermute x10, waiting for transfers between devices, extended(): lax.ppermute(lax.slice_in_dim(block, 0, width, axis=dim), axis, backward)  28 us
    ppermute x10, waiting for transfers between devices, extended(): lax.ppermute(lax.slice_in_dim(block, block.shape[dim] - width, None, axis...  16.7 us
    ppermute x10, starting transfers between devices, extended(): lax.ppermute(lax.slice_in_dim(block, 0, width, axis=dim), axis, backward)  13.3 us
    reduce_scatter x1, waiting for transfers between devices, shards(): share = lax.psum_scatter(gradient, 'scen', scatter_dimension=1, tiled=True)  12 us
    all_gather x1, blocking collectives, shards(): lax.all_gather(maps_part, 'scen', axis=1, tiled=True)  8.72 us
    all_gather x1, blocking collectives, shards(): lax.all_gather(first_part, 'scen', axis=1, tiled=True)  7.84 us
    all_gather x1, blocking collectives, shards(): lax.all_gather(second_part, 'scen', axis=1, tiled=True)  7.04 us
  transfers between devices with their start and end apart: 21, of which 14 were waited for; matrix products, arithmetic and copies ran while one was open for 1% of the time, Pallas kernels for 0%

commit v1 on v0

v1 whole, which is shorter than its diff:
```python
import functools

import jax
import jax.numpy as jnp
from jax import lax
from jax.experimental import pallas as pl
from jax.experimental.pallas import tpu as pltpu
from jax.sharding import PartitionSpec as P

STEPS = 2
ADAM_STEP = 10
REACH_MAX = 0.2
PRIOR_WEIGHT = 0.1
GROWTH_RATE = 0.5
MUTATION_INPUT = 0.02
LEARN_RATE = 0.01
BETA_FIRST = 0.9
BETA_SECOND = 0.999
ADAM_EPS = 1e-08
LOSS_WEIGHT = 2.0

F32 = jnp.float32
LANES = 128
EDGE = 8
HALO = 4
DENSITY, TRAIT, VARIANCE, DISPERSAL, SELECTION, OPTIMUM, LAND, OBSERVED = range(8)
FIELDS = 8
VMEM_BYTES = 48 * 1024 * 1024
SAVED = (
    "half",
    "land",
    "select",
    "n0",
    "q0",
    "m0",
    "wd",
    "wr",
    "lr",
    "dr0n",
    "dr0q",
    "dr0m",
    "e",
    "d",
    "vs",
    "p",
    "zs",
    "r",
    "n1",
    "q1",
    "m1",
    "z1",
    "u1",
    "dr1n",
    "dr1q",
    "dr1m",
    "a2n",
    "a2q",
    "a2m",
    "gsel",
    "gd",
    "gr",
    "a1n",
    "a1q",
    "a1m",
)


def reciprocal(value):
    guess = pl.reciprocal(value, approx=True)
    return guess * (2.0 - value * guess)


def sigmoid(value):
    return 0.5 + 0.5 * jnp.tanh(0.5 * value)


def dynamics(slabs, tiles, load, steps_at, keep, put):
    shape = (tiles, 8, LANES)
    lane = lax.broadcasted_iota(jnp.int32, shape, 2)
    at_last, at_first = lane == LANES - 1, lane == 0

    def right(value):
        turned = pltpu.roll(value, LANES - 1, 2)
        beside = jnp.concatenate([turned[1:], turned[:1]], 0) if tiles > 1 else turned
        return jnp.where(at_last, beside, turned)

    def left(value):
        turned = pltpu.roll(value, 1, 2)
        beside = jnp.concatenate([turned[-1:], turned[:-1]], 0) if tiles > 1 else turned
        return jnp.where(at_first, beside, turned)

    def down(name, k):
        if k + 1 < slabs:
            return keep[name][k + 1]
        return pltpu.roll(keep[name][0], 7, 1)

    def wrapped(values):
        return [pltpu.roll(value, 1, 1) for value in values]

    def row_fluxes(names, k):
        weight = keep["wd"][k]
        gaps = [down(name, k) - keep[name][k] for name in names]
        return gaps, [weight * gap for gap in gaps]

    def spread(names, k, above):
        row_gaps, row_flux = row_fluxes(names, k)
        weight = keep["wr"][k]
        out, col_gaps = [], []
        for name, flux, before in zip(names, row_flux, above):
            value = keep[name][k]
            gap = right(value) - value
            col_flux = weight * gap
            out.append(value + (flux - before) + (col_flux - left(col_flux)))
            col_gaps.append(gap)
        return out, row_gaps, col_gaps, row_flux

    for k in range(slabs):
        keep["half"][k] = 0.5 * REACH_MAX * sigmoid(load(DISPERSAL, k))
        keep["land"][k] = load(LAND, k)
        raw = load(SELECTION, k)
        keep["select"][k] = jnp.maximum(raw, 0.0) + jnp.log(1.0 + jnp.exp(-jnp.abs(raw)))
        n, z, v = load(DENSITY, k), load(TRAIT, k), load(VARIANCE, k)
        keep["n0"][k] = n
        keep["q0"][k] = n * z
        keep["m0"][k] = n * (v + z * z)

    for k in range(slabs):
        half, land = keep["half"][k], keep["land"][k]
        keep["wd"][k] = (half + down("half", k)) * (land * down("land", k))
        pair = land * right(land)
        keep["lr"][k] = pair
        keep["wr"][k] = (half + right(half)) * pair

    names = ("n0", "q0", "m0")
    above = wrapped(row_fluxes(names, slabs - 1)[1])
    for k in range(slabs):
        (ns, qs, ms), _, col_gaps, above = spread(names, k, above)
        for name, gap in zip(("dr0n", "dr0q", "dr0m"), col_gaps):
            keep[name][k] = gap
        z, v = load(TRAIT, k), load(VARIANCE, k)
        optimum, select, land = load(OPTIMUM, k), keep["select"][k], keep["land"][k]
        r = reciprocal(ns + PRIOR_WEIGHT)
        zs = (qs + PRIOR_WEIGHT * z) * r
        vs = (ms + PRIOR_WEIGHT * (v + z * z)) * r - zs * zs
        d = zs - optimum
        p = reciprocal(1.0 + select * vs)
        e = jnp.exp(land * (GROWTH_RATE * (1.0 - ns) - 0.5 * select * (d * d + vs)))
        n1 = ns * e
        z1 = optimum + p * d
        u1 = vs * p + MUTATION_INPUT + z1 * z1
        for name, value in zip(
            ("e", "d", "vs", "p", "zs", "r", "n1", "q1", "m1", "z1", "u1"),
            (e, d, vs, p, zs, r, n1, n1 * z1, n1 * u1, z1, u1),
        ):
            keep[name][k] = value

    names = ("n1", "q1", "m1")
    above = wrapped(row_fluxes(names, slabs - 1)[1])
    for k in range(slabs):
        (ns, qs, ms), _, col_gaps, above = spread(names, k, above)
        for name, gap in zip(("dr1n", "dr1q", "dr1m"), col_gaps):
            keep[name][k] = gap
        optimum, select, land = load(OPTIMUM, k), keep["select"][k], keep["land"][k]
        r = reciprocal(ns + PRIOR_WEIGHT)
        zs = (qs + PRIOR_WEIGHT * keep["z1"][k]) * r
        es = (ms + PRIOR_WEIGHT * keep["u1"][k]) * r
        vs = es - zs * zs
        d = zs - optimum
        misfit = d * d + vs
        e = jnp.exp(land * (GROWTH_RATE * (1.0 - ns) - 0.5 * select * misfit))
        n2 = ns * e
        weight = jnp.where(steps_at(k) == 2.0, 2.0 * LOSS_WEIGHT * land, 0.0)
        an = weight * (n2 - load(OBSERVED, k))
        b = 0.5 * an * n2
        av = -b * select
        am = av * r
        aq = -2.0 * optimum * am
        keep["gsel"][k] = -b * misfit
        keep["a2n"][k] = an * e - b - (aq * zs + am * es)
        keep["a2q"][k] = aq
        keep["a2m"][k] = am

    names = ("a2n", "a2q", "a2m")
    above = wrapped(row_fluxes(names, slabs - 1)[1])
    for k in range(slabs):
        (an, aq, am), row_gaps, col_gaps, above = spread(names, k, above)
        fields = ("n1", "q1", "m1")
        keep["gd"][k] = sum((down(f, k) - keep[f][k]) * gap for f, gap in zip(fields, row_gaps))
        keep["gr"][k] = sum(keep[f][k] * gap for f, gap in zip(("dr1n", "dr1q", "dr1m"), col_gaps))
        n1, z1, land, select = keep["n1"][k], keep["z1"][k], keep["land"][k], keep["select"][k]
        e, d, vs, p, zs, r = (keep[name][k] for name in ("e", "d", "vs", "p", "zs", "r"))
        av = PRIOR_WEIGHT * keep["a2m"][k] + am * n1
        az = PRIOR_WEIGHT * keep["a2q"][k] + aq * n1 + 2.0 * z1 * av
        weight = jnp.where(steps_at(k) == 1.0, 2.0 * LOSS_WEIGHT * land, 0.0)
        an = an + aq * z1 + am * keep["u1"][k] + weight * (n1 - load(OBSERVED, k))
        b = 0.5 * an * n1 * land
        at = -(az * d + av * vs) * (p * p)
        gsel = keep["gsel"][k] + at * vs - b * (d * d + vs)
        avs = av * p + select * (at - b)
        azs = az * p - 2.0 * (b * select * d + zs * avs)
        aqs, ams = azs * r, avs * r
        keep["a1n"][k] = an * e - b - (aqs * zs + ams * (vs + zs * zs))
        keep["a1q"][k] = aqs
        keep["a1m"][k] = ams
        put(1, k, gsel * sigmoid(load(SELECTION, k)))

    def row_share(k):
        gaps = [down(name, k) - keep[name][k] for name in ("a1n", "a1q", "a1m")]
        fields = [down(name, k) - keep[name][k] for name in ("n0", "q0", "m0")]
        total = keep["gd"][k] + sum(gap * field for gap, field in zip(gaps, fields))
        return total * (keep["land"][k] * down("land", k))

    (above,) = wrapped([row_share(slabs - 1)])
    for k in range(slabs):
        here = row_share(k)
        total = keep["gr"][k]
        for name, field in zip(("a1n", "a1q", "a1m"), ("dr0n", "dr0q", "dr0m")):
            value = keep[name][k]
            total = total + (right(value) - value) * keep[field][k]
        total = total * keep["lr"][k]
        half = keep["half"][k]
        put(0, k, half * (10.0 * half - 1.0) * (here + above + total + left(total)))
        above = here


def step_rows(line):
    return jnp.transpose(jnp.concatenate([line] * (LANES // 8), 0))


def interior_kernel(first, rows, out_first, out_rows, tiles, *refs):
    sources, step_ref, out_ref = refs[:7], refs[7], refs[8]
    fields, codes, step_tile, grads, kept, sems = refs[9:15]
    slabs = rows // 8
    copies = []

    def bring(field, source, target):
        group = [
            pltpu.make_async_copy(
                source.at[pl.ds(first, rows), pl.ds(t * LANES, LANES)], target.at[t], sems.at[field, t]
            )
            for t in range(tiles)
        ]
        for copy in group:
            copy.start()
        copies.extend(group)

    density, trait, variance, optimum, observed, land_code, maps = sources
    bring(DISPERSAL, maps.at[0], fields.at[DISPERSAL])
    bring(LAND, land_code, codes)
    bring(SELECTION, maps.at[1], fields.at[SELECTION])
    bring(DENSITY, density.at[0], fields.at[DENSITY])
    bring(TRAIT, trait.at[0], fields.at[TRAIT])
    bring(VARIANCE, variance.at[0], fields.at[VARIANCE])
    bring(OPTIMUM, optimum.at[0], fields.at[OPTIMUM])
    bring(OBSERVED, observed.at[0], fields.at[OBSERVED])
    line = jnp.broadcast_to(step_ref[0:1, :].astype(F32), (8, LANES))
    step_tile[...] = step_rows(line)
    for copy in copies:
        copy.wait()

    def load(field, k):
        source = codes if field == LAND else fields.at[field]
        parts = [source[t, pl.ds(k, 8, stride=slabs), :] for t in range(tiles)]
        return jnp.stack(parts).astype(F32)

    def steps_at(k):
        part = step_tile[pl.ds(first + k, 8, stride=slabs), :]
        return jnp.broadcast_to(part[None], (tiles, 8, LANES))

    def put(which, k, value):
        for t in range(tiles):
            grads[which, t, pl.ds(k, 8, stride=slabs), :] = value[t]

    keep = {name: kept.at[index] for index, name in enumerate(SAVED)}
    dynamics(slabs, tiles, load, steps_at, keep, put)
    skip = out_first - first
    for which in range(2):
        for t in range(tiles):
            out_ref[which, :, t * LANES : (t + 1) * LANES] = grads[which, t, skip : skip + out_rows, :]


def interior(first, rows, out_first, out_rows, sources, steps):
    columns = sources[0].shape[-1]
    tiles = columns // LANES
    kernel = functools.partial(interior_kernel, first, rows, out_first, out_rows, tiles)
    return pl.pallas_call(
        kernel,
        out_shape=jax.ShapeDtypeStruct((2, out_rows, columns), F32),
        in_specs=[pl.BlockSpec(memory_space=pl.ANY)] * 7 + [pl.BlockSpec(memory_space=pltpu.VMEM)],
        out_specs=pl.BlockSpec(memory_space=pltpu.VMEM),
        scratch_shapes=[
            pltpu.VMEM((FIELDS, tiles, rows, LANES), F32),
            pltpu.VMEM((tiles, rows, LANES), jnp.int32),
            pltpu.VMEM((LANES, LANES), F32),
            pltpu.VMEM((2, tiles, rows, LANES), F32),
            pltpu.VMEM((len(SAVED), rows // 8, tiles, 8, LANES), F32),
            pltpu.SemaphoreType.DMA((FIELDS, tiles)),
        ],
        compiler_params=pltpu.CompilerParams(vmem_limit_bytes=VMEM_BYTES),
        name=f"interior_{out_first}",
    )(*sources, steps)


def field_blocks(refs):
    density, trait, variance, optimum, observed, land_code, maps = refs
    return [
        density[0],
        trait[0],
        variance[0],
        maps[0],
        maps[1],
        optimum[0],
        land_code[...].astype(F32),
        observed[0],
    ]


def columns_kernel(*refs):
    firsts, lasts, left_ref, right_ref = refs[:7], refs[7:14], refs[14], refs[15]
    rows = left_ref.shape[-1]
    lane = lax.broadcasted_iota(jnp.int32, (rows, LANES), 1)
    packed = jnp.zeros((rows, LANES), F32)
    for field, (first, last) in enumerate(zip(field_blocks(firsts), field_blocks(lasts))):
        both = jnp.where(lane < EDGE, first, last)
        turned = pltpu.roll(both, 16 * field, 1) if field else both
        place = (lane - 16 * field + EDGE) % LANES
        packed = jnp.where(place < 2 * EDGE, turned, packed)
    flipped = jnp.transpose(packed)
    for field in range(FIELDS):
        left_ref[field] = flipped[16 * field : 16 * field + EDGE]
        start = (16 * field - EDGE) % LANES
        right_ref[field] = flipped[start : start + EDGE]


def block_specs(sources, rows, columns, at):
    specs = []
    for source in sources:
        if source.ndim == 2:
            specs.append(pl.BlockSpec((rows, columns), lambda i, at=at: at))
        else:
            specs.append(pl.BlockSpec((source.shape[0], rows, columns), lambda i, at=at: (0, *at)))
    return specs


def whole_spec(array):
    return pl.BlockSpec(array.shape, lambda i: (0,) * array.ndim)


def pack_columns(sources):
    rows, columns = sources[0].shape[1:]
    specs = block_specs(sources, rows, LANES, (0, 0))
    specs += block_specs(sources, rows, LANES, (0, columns // LANES - 1))
    shape = jax.ShapeDtypeStruct((FIELDS, EDGE, rows), F32)
    return pl.pallas_call(
        columns_kernel,
        grid=(1,),
        out_shape=[shape, shape],
        in_specs=specs,
        out_specs=[whole_spec(shape)] * 2,
        compiler_params=pltpu.CompilerParams(vmem_limit_bytes=VMEM_BYTES),
        name="pack_columns",
    )(*sources, *sources)


def rows_kernel(tiles, *refs):
    tops, bottoms = refs[:7], refs[7:14]
    own_left, own_right, from_left, from_right, step_ref, up_ref, down_ref = refs[14:]
    sub = lax.broadcasted_iota(jnp.int32, (8, tiles * LANES), 0)
    top, bottom = field_blocks(tops), field_blocks(bottoms)
    for pair in range(FIELDS // 2):
        upward = jnp.where(sub < HALO, top[2 * pair], pltpu.roll(top[2 * pair + 1], HALO, 0))
        downward = jnp.where(sub < HALO, pltpu.roll(bottom[2 * pair + 1], HALO, 0), bottom[2 * pair])
        for t in range(tiles):
            up_ref[pair * tiles + t] = upward[:, t * LANES : (t + 1) * LANES]
            down_ref[pair * tiles + t] = downward[:, t * LANES : (t + 1) * LANES]
    lane = lax.broadcasted_iota(jnp.int32, (8, LANES), 1)
    base = FIELDS // 2 * tiles
    for index, strip in enumerate((from_left, own_left, own_right, from_right)):
        packed = jnp.zeros((8, LANES), F32)
        for field in range(FIELDS):
            turned = pltpu.roll(strip[field], 8 * field, 1) if field else strip[field]
            place = (lane - 8 * field + HALO) % LANES
            packed = jnp.where(place < 2 * HALO, turned, packed)
        up_ref[base + index] = packed
        down_ref[base + index] = packed
    line = jnp.broadcast_to(step_ref[0:1, :].astype(F32), (8, LANES))
    up_ref[base + 4] = line
    down_ref[base + 4] = line


def pack_rows(sources, strips, steps):
    rows, columns = sources[0].shape[1:]
    tiles = columns // LANES
    specs = block_specs(sources, EDGE, columns, (0, 0))
    specs += block_specs(sources, EDGE, columns, (rows // EDGE - 1, 0))
    specs += [whole_spec(strip) for strip in strips] + [whole_spec(steps)]
    shape = jax.ShapeDtypeStruct((FIELDS // 2 * tiles + 5, 8, LANES), F32)
    return pl.pallas_call(
        functools.partial(rows_kernel, tiles),
        grid=(1,),
        out_shape=[shape, shape],
        in_specs=specs,
        out_specs=[whole_spec(shape)] * 2,
        compiler_params=pltpu.CompilerParams(vmem_limit_bytes=VMEM_BYTES),
        name="pack_rows",
    )(*sources, *sources, *strips, steps)


def edges_kernel(tiles, place_ref, *refs):
    tops, bottoms = refs[:7], refs[7:14]
    own_left, own_right, from_left, from_right, step_ref, from_above, from_below, out_ref = refs[14:22]
    row_strip, col_strip, row_step, row_grad, col_grad, row_keep, col_keep = refs[22:]
    base = FIELDS // 2 * tiles
    has_above, has_below, has_left, has_right = (place_ref[i] for i in range(4))
    top, bottom = field_blocks(tops), field_blocks(bottoms)
    lane = lax.broadcasted_iota(jnp.int32, (8, LANES), 1)
    sub = lax.broadcasted_iota(jnp.int32, (8, LANES), 0)

    corners = [
        jnp.where((lane % 8) < HALO, from_below[base + index], from_above[base + index]) for index in range(4)
    ]
    beside = [[None] * 4 for _ in range(FIELDS)]
    for field in range(FIELDS):
        for index, strip in enumerate((from_left, own_left, own_right, from_right)):
            value = strip[field]
            outer = pltpu.roll(corners[index], (LANES - 8 * field) % LANES, 1) if field else corners[index]
            if field == LAND:
                outer = outer * jnp.where(lane < LANES // 2, has_below, has_above)
                if index == 0:
                    value, outer = value * has_left, outer * has_left
                if index == 3:
                    value, outer = value * has_right, outer * has_right
            col_strip[field, 0, 8 * index : 8 * index + 8, :] = value
            col_strip[field, 1, 8 * index : 8 * index + 8, :] = outer
            beside[field][index] = (value, outer)

    def lined(value, outer):
        out = jnp.where(lane < 8, pltpu.roll(outer, 8, 1), pltpu.roll(value, 8, 1))
        out = jnp.where(lane < 16, out, pltpu.roll(value, 24, 1))
        return jnp.where(lane < 24, out, pltpu.roll(outer, 24, 1))

    zeros = jnp.zeros((8, LANES), F32)
    stack = []
    for index in range(LANES // 8):
        here = lined(*beside[index][3]) if index < FIELDS else zeros
        following = (index + 1) % (LANES // 8)
        after = lined(*beside[following][0]) if following < FIELDS else zeros
        stack.append(jnp.where(sub < HALO, here, after))
    flipped = jnp.transpose(jnp.concatenate(stack, 0))[:32]
    own_step = jnp.broadcast_to(step_ref[0:1, :].astype(F32), (8, LANES))
    outer_step = jnp.where(lane < LANES // 2, from_below[base + 4], from_above[base + 4])
    row_step[...] = step_rows(lined(own_step, outer_step))[:32]
    for field in range(FIELDS):
        for t in range(tiles):
            above, below = from_above[field // 2 * tiles + t], from_below[field // 2 * tiles + t]
            if field % 2:
                above, below = pltpu.roll(above, HALO, 0), pltpu.roll(below, HALO, 0)
            if field == LAND:
                above, below = above * has_above, below * has_below
            own = slice(t * LANES, (t + 1) * LANES)
            for index, value in enumerate((above, top[field][:, own], bottom[field][:, own], below)):
                row_strip[field, t, 8 * index : 8 * index + 8, :] = value
        row_strip[field, tiles] = pltpu.roll(flipped, (LANES - 8 * field) % LANES, 1) if field else flipped

    slabs = 3
    for strip, grad, kept, count in (
        (row_strip, row_grad, row_keep, tiles + 1),
        (col_strip, col_grad, col_keep, 2),
    ):
        on_rows = strip is row_strip

        def load(field, k):
            parts = [strip[field, t, pl.ds(HALO + k, 8, stride=slabs), :] for t in range(count)]
            return jnp.stack(parts)

        def steps_at(k):
            if on_rows:
                part = row_step[pl.ds(HALO + k, 8, stride=slabs), :]
                return jnp.broadcast_to(part[None], (count, 8, LANES))
            return jnp.stack([own_step, outer_step])

        def put(which, k, value):
            for t in range(count):
                grad[which, t, pl.ds(HALO + k, 8, stride=slabs), :] = value[t]

        keep = {name: kept.at[index] for index, name in enumerate(SAVED)}
        dynamics(slabs, count, load, steps_at, keep, put)
    for which in range(2):
        for t in range(tiles):
            out_ref[which, :, t * LANES : (t + 1) * LANES] = jnp.where(
                sub < HALO, row_grad[which, t, 8:16, :], row_grad[which, t, 16:24, :]
            )
        out_ref[which, :, tiles * LANES :] = jnp.where(
            sub < HALO, col_grad[which, 0, 8:16, :], col_grad[which, 0, 16:24, :]
        )


def edges(place, sources, strips, steps, from_above, from_below):
    rows, columns = sources[0].shape[1:]
    tiles = columns // LANES
    specs = [pl.BlockSpec(memory_space=pltpu.SMEM)]
    specs += block_specs(sources, EDGE, columns, (0, 0))
    specs += block_specs(sources, EDGE, columns, (rows // EDGE - 1, 0))
    rest = [*strips, steps, from_above, from_below]
    specs += [whole_spec(array) for array in rest]
    shape = jax.ShapeDtypeStruct((2, EDGE, columns + LANES), F32)
    return pl.pallas_call(
        functools.partial(edges_kernel, tiles),
        grid=(1,),
        out_shape=shape,
        in_specs=specs,
        out_specs=whole_spec(shape),
        scratch_shapes=[
            pltpu.VMEM((FIELDS, tiles + 1, 32, LANES), F32),
            pltpu.VMEM((FIELDS, 2, 32, LANES), F32),
            pltpu.VMEM((32, LANES), F32),
            pltpu.VMEM((2, tiles + 1, 32, LANES), F32),
            pltpu.VMEM((2, 2, 32, LANES), F32),
            pltpu.VMEM((len(SAVED), 3, tiles + 1, 8, LANES), F32),
            pltpu.VMEM((len(SAVED), 3, 2, 8, LANES), F32),
        ],
        compiler_params=pltpu.CompilerParams(vmem_limit_bytes=VMEM_BYTES),
        name="edges",
    )(place, *sources, *sources, *rest)


def update_kernel(parts, terms, maps_ref, first_ref, second_ref, *refs):
    grads, edge_refs = refs[: parts * terms], refs[parts * terms : (parts + 1) * terms]
    new_maps, new_first, new_second = refs[(parts + 1) * terms :]
    rows, columns = maps_ref.shape[1:]
    tiles = columns // LANES
    lane = lax.broadcasted_iota(jnp.int32, (rows, LANES), 1)
    sub = lax.broadcasted_iota(jnp.int32, (EDGE, LANES), 0)
    edge = sum(ref[...] for ref in edge_refs)
    strips = [edge[which, :, columns:] for which in range(2)]
    blank = jnp.zeros((LANES - 2 * EDGE, LANES), F32)
    flipped = jnp.transpose(jnp.concatenate([*strips, blank], 0))
    height = rows // parts
    for which in range(2):
        for t in range(tiles):
            own = slice(t * LANES, (t + 1) * LANES)
            grad = jnp.concatenate(
                [sum(ref[which, :, own] for ref in grads[part * terms : (part + 1) * terms]) for part in range(parts)],
                0,
            )
            outer = edge[which, :, own]
            grad = jnp.concatenate(
                [
                    jnp.where(sub < HALO, outer, grad[:EDGE]),
                    grad[EDGE:-EDGE],
                    jnp.where(sub < HALO, grad[-EDGE:], outer),
                ],
                0,
            )
            if t == 0:
                beside = pltpu.roll(flipped, LANES - EDGE * which, 1) if which else flipped
                grad = jnp.where(lane < HALO, beside, grad)
            if t == tiles - 1:
                beside = pltpu.roll(flipped, LANES - EDGE * (which + 1), 1)
                grad = jnp.where(lane >= LANES - HALO, beside, grad)
            first = BETA_FIRST * first_ref[which, :, own] + (1.0 - BETA_FIRST) * grad
            second = BETA_SECOND * second_ref[which, :, own] + (1.0 - BETA_SECOND) * grad * grad
            new_first[which, :, own] = first
            new_second[which, :, own] = second
            scale = jnp.sqrt(second * (1.0 / (1.0 - BETA_SECOND**ADAM_STEP))) + ADAM_EPS
            change = (LEARN_RATE / (1.0 - BETA_FIRST**ADAM_STEP)) * first
            new_maps[which, :, own] = maps_ref[which, :, own] - change * reciprocal(scale)


def update(maps, first_moment, second_moment, grads, edge_grads):
    parts, terms = len(grads), len(edge_grads)
    flat = [term for grad in grads for term in grad]
    shape = jax.ShapeDtypeStruct(maps.shape, F32)
    operands = [maps, first_moment, second_moment, *flat, *edge_grads]
    return pl.pallas_call(
        functools.partial(update_kernel, parts, terms),
        out_shape=[shape] * 3,
        in_specs=[pl.BlockSpec(memory_space=pltpu.VMEM)] * len(operands),
        out_specs=[pl.BlockSpec(memory_space=pltpu.VMEM)] * 3,
        compiler_params=pltpu.CompilerParams(vmem_limit_bytes=VMEM_BYTES),
        name="update",
    )(*operands)


def shifts(axis):
    count = lax.axis_size(axis)
    forward = [(i, (i + 1) % count) for i in range(count)]
    return forward, [(target, source) for source, target in forward]


def both_scenarios(value):
    count = lax.axis_size("scen")
    if count == 2:
        return [value, lax.ppermute(value, "scen", [(0, 1), (1, 0)])]
    return [lax.psum(value, "scen")]


def shards(
    density,
    trait,
    variance,
    optimum,
    observed,
    obs_step,
    land_code,
    maps,
    first_moment,
    second_moment,
):
    sources = (density, trait, variance, optimum, observed, land_code, maps)
    rows = maps.shape[1]
    middle = rows // 2
    upper = interior(0, middle + EDGE, 0, middle, sources, obs_step)
    upper_terms = both_scenarios(upper)
    own_left, own_right = pack_columns(sources)
    rightward, leftward = shifts("ly")
    from_left = lax.ppermute(own_right, "ly", rightward)
    from_right = lax.ppermute(own_left, "ly", leftward)
    lower = interior(middle - EDGE, middle + EDGE, middle, middle, sources, obs_step)
    lower_terms = both_scenarios(lower)
    strips = (own_left, own_right, from_left, from_right)
    up, down = pack_rows(sources, strips, obs_step)
    downward, upward = shifts("lx")
    from_above = lax.ppermute(down, "lx", downward)
    from_below = lax.ppermute(up, "lx", upward)
    row, column = lax.axis_index("lx"), lax.axis_index("ly")
    place = jnp.stack(
        [row > 0, row < lax.axis_size("lx") - 1, column > 0, column < lax.axis_size("ly") - 1]
    ).astype(F32)
    outer = edges(place, sources, strips, obs_step, from_above, from_below)
    outer_terms = both_scenarios(outer)
    return tuple(update(maps, first_moment, second_moment, [upper_terms, lower_terms], outer_terms))


def solution(mesh):
    in_specs = (
        P("scen", "lx", "ly"),
        P("scen", "lx", "ly"),
        P("scen", "lx", "ly"),
        P("scen", "lx", "ly"),
        P("scen", "lx", "ly"),
        P("scen", "lx"),
        P("lx", "ly"),
        P(None, "lx", "ly"),
        P(None, "lx", "ly"),
        P(None, "lx", "ly"),
    )
    out_specs = (P(None, "lx", "ly"), P(None, "lx", "ly"), P(None, "lx", "ly"))
    return jax.shard_map(shards, mesh=mesh, in_specs=in_specs, out_specs=out_specs, check_vma=False)
```

time: 170 us -> 49.3 us (0.29)
  waiting for transfers between devices: 56.7 us -> 10.3 us
  starting transfers between devices: 42.7 us -> 10.6 us
  other arithmetic: 25.3 us -> 0.08 us
  blocking collectives: 23.6 us -> 0 us
  Pallas kernels: 0 us -> 19.7 us
  between operations: 14.6 us -> 0.79 us
    ppermute x20 -> x7, waiting for transfers between devices: 44.7 us -> 10.3 us  [the longest x1 4.11 us: shards(): from_left = lax.ppermute(own_right, 'ly', rightward)]
    ppermute x20 -> x7, starting transfers between devices: 42.7 us -> 10.6 us  [the longest x3 4.65 us: both_scenarios(): return [value, lax.ppermute(value, 'scen', [(0, 1), (1, 0)])]]
    all_gather x3 -> x0, blocking collectives: 23.6 us -> none  [the longest x1 8.72 us: shards(): lax.all_gather(maps_part, 'scen', axis=1, tiled=True)]
    pallas_call x0 -> x6, Pallas kernels: none -> 19.7 us  [the longest x2 14.8 us: interior(): pl.pallas_call(kernel, out_shape=jax.ShapeDtypeStruct((2, out_rows, colum...]
    reduce_scatter x1 -> x0, waiting for transfers between devices: 12 us -> none  [shards(): share = lax.psum_scatter(gradient, 'scen', scatter_dimension=1, tiled=True)]
    mul x7 -> x0, other arithmetic: 5.33 us -> none  [the longest x2 4.42 us: advance(): selection = jax.nn.softplus(interior(raw_maps[1]))]
    add_any x2 -> x0, other arithmetic: 4.63 us -> none  [advance(): reach_mid + reach_map[row_cut, col_cut]]
    broadcast_in_dim x5 -> x0, other arithmetic: 4.08 us -> none  [the longest x3 3.18 us: advance(): density_now, trait_now, variance_now = (fields[0], fields[1], fields[2])]
  transfers between devices with their start and end apart: 21 -> 7, of which waited for: 14 -> 4; matrix products, arithmetic and copies ran while one was open for 1% -> 0% of each run, Pallas kernels for 0% -> 22%
where the time goes in v1:
time: 49.3 us; the launch traced here: 48.9 us
  Pallas kernels  19.7 us (40%)
  starting transfers between devices  10.6 us (22%)
  waiting for transfers between devices  10.3 us (21%)
  local copies, waits for them, and re-layouts  7.44 us (15%)
  between operations  0.79 us (2%)
    pallas_call x2, Pallas kernels, interior(): pl.pallas_call(kernel, out_shape=jax.ShapeDtypeStruct((2, out_rows, colum...  14.8 us
    unnamed x36, local copies, waits for them, and re-layouts  7.44 us
    ppermute x3, starting transfers between devices, both_scenarios(): return [value, lax.ppermute(value, 'scen', [(0, 1), (1, 0)])]  4.65 us
    ppermute x1, starting transfers between devices, shards(): from_right = lax.ppermute(own_left, 'ly', leftward)  4.17 us
    ppermute x1, waiting for transfers between devices, shards(): from_left = lax.ppermute(own_right, 'ly', rightward)  4.11 us
    pallas_call x1, Pallas kernels, edges(): pl.pallas_call(functools.partial(edges_kernel, tiles), grid=(1,), out_sha...  3.03 us
    ppermute x3, waiting for transfers between devices, both_scenarios(): return [value, lax.ppermute(value, 'scen', [(0, 1), (1, 0)])]  2.52 us
    ppermute x1, waiting for transfers between devices, shards(): from_above = lax.ppermute(down, 'lx', downward)  2.08 us
  transfers between devices with their start and end apart: 7, of which 4 were waited for; matrix products, arithmetic and copies ran while one was open for 0% of the time, Pallas kernels for 22%

profile of v1, /device:TPU:0, one launch (start us, length us, event | category | flops | bytes accessed | tf_op | source)
XLA Modules:
  0.0 48.9 jit_solution(11314091643091708935)
XLA Ops:
  0.6 0.0 copy-start
  0.6 1.0 %copy-done = f32[2,128,512]{2,1,0:T(8,128)S(1)} copy-done((f32[2,128,512]{2,1,0:T(8,128)S(1)}, f32[2,128,512]{2,1,0:T(8,128)}, u32[]{:S(2)}) %copy-start) | copy-done | bytes 524312
  1.7 0.0 copy-start.2
  1.7 0.9 %copy-done.2 = f32[1,128,512]{2,1,0:T(8,128)S(1)} copy-done((f32[1,128,512]{2,1,0:T(8,128)S(1)}, f32[1,128,512]{2,1,0:T(8,128)}, u32[]{:S(2)}) %copy-start.2) | copy-done | bytes 262168
  2.6 0.9 %copy-done.4 = f32[1,128,512]{2,1,0:T(8,128)S(1)} copy-done((f32[1,128,512]{2,1,0:T(8,128)S(1)}, f32[1,128,512]{2,1,0:T(8,128)}, u32[]{:S(2)}) %copy-start.4) | copy-done | bytes 262168
  3.6 0.9 %copy-done.6 = f32[1,128,512]{2,1,0:T(8,128)S(1)} copy-done((f32[1,128,512]{2,1,0:T(8,128)S(1)}, f32[1,128,512]{2,1,0:T(8,128)}, u32[]{:S(2)}) %copy-start.6) | copy-done | bytes 262168
  4.5 0.9 %copy-done.8 = f32[1,128,512]{2,1,0:T(8,128)S(1)} copy-done((f32[1,128,512]{2,1,0:T(8,128)S(1)}, f32[1,128,512]{2,1,0:T(8,128)}, u32[]{:S(2)}) %copy-start.8) | copy-done | bytes 262168
  5.5 0.9 %copy-done.10 = f32[1,128,512]{2,1,0:T(8,128)S(1)} copy-done((f32[1,128,512]{2,1,0:T(8,128)S(1)}, f32[1,128,512]{2,1,0:T(8,128)}, u32[]{:S(2)}) %copy-start.10) | copy-done | bytes 262168
  6.4 0.9 %copy-done.12 = s32[128,512]{1,0:T(8,128)S(1)} copy-done((s32[128,512]{1,0:T(8,128)S(1)}, s32[128,512]{1,0:T(8,128)}, u32[]{:S(2)}) %copy-start.12) | copy-done | bytes 262168
  7.4 0.7 %copy-done.16 = s32[1,128]{1,0:T(1,128)S(1)} copy-done((s32[1,128]{1,0:T(1,128)S(1)}, s32[1,128]{1,0:T(1,128)}, u32[]{:S(2)}) %copy-start.16) | copy-done | bytes 536
  8.0 7.4 %interior_0.1.refs_0_ = f32[2,64,512]{2,1,0:T(8,128)S(1)} custom-call(f32[1,128,512]{2,1,0:T(8,128)S(1)} %copy-done.2, f32[1,128,512]{2,1,0:T(8,128)S(1)} %copy-done.4, f32[1,128,512]{2,1,0:T(8,128)S(1)} %copy-done.6, f32[1,128,512]{2,1,0:T(8,128)S(1)} %copy-done.8, f32[1,128,512]{2,1,0:T(8,128)S(1)} %copy-done.10, s32[128,512]{1,0:T(8,128)S(1)} %copy-done.12, ...), custom_call_target="tpu_custom_call" | custom-call | tf_op jit(solution)/shard_map/interior_0/pallas_call | solution.py:286
  15.4 3.0 %collective-permute-start = (f32[2,64,512]{2,1,0:T(8,128)S(1)}, f32[2,64,512]{2,1,0:T(8,128)S(1)}, u32[]{:S(2)}, u32[]{:S(2)}) collective-permute-start(f32[2,64,512]{2,1,0:T(8,128)S(1)} %interior_0.1.refs_0_), channel_id=1, source_target_pairs={{0,16},{16,0},{1,17},{17,1},{2,18},{18,2},{3,19},{19,3},{4,20},{20... | collective-permute-start | bytes 786440 | tf_op jit(solution)/shard_map/ppermute | solution.py:594
  18.4 7.4 %interior_64.1.refs_2_ = f32[2,64,512]{2,1,0:T(8,128)S(1)} custom-call(f32[1,128,512]{2,1,0:T(8,128)S(1)} %copy-done.2, f32[1,128,512]{2,1,0:T(8,128)S(1)} %copy-done.4, f32[1,128,512]{2,1,0:T(8,128)S(1)} %copy-done.6, f32[1,128,512]{2,1,0:T(8,128)S(1)} %copy-done.8, f32[1,128,512]{2,1,0:T(8,128)S(1)} %copy-done.10, s32[128,512]{1,0:T(8,128)S(1)} %copy-done.12, ...), custom_call_target="tpu_custom_call" | custom-call | tf_op jit(solution)/shard_map/interior_64/pallas_call | solution.py:286
  25.9 0.0 copy-start.1
  25.9 0.0 copy-start.3
  25.9 0.0 copy-start.5
  25.9 0.0 copy-start.7
  25.9 0.0 copy-start.9
  25.9 0.0 copy-start.11
  25.9 0.0 copy-start.13
  25.9 0.1 collective-permute-start.1
  26.0 0.2 pack_columns.1
  26.3 4.2 %collective-permute-start.3 = (f32[8,8,128]{2,1,0:T(8,128)S(1)}, f32[8,8,128]{2,1,0:T(8,128)S(1)}, u32[]{:S(2)}, u32[]{:S(2)}) collective-permute-start(f32[8,8,128]{2,1,0:T(8,128)S(1)} %get-tuple-element.7.refs_14_), channel_id=1, source_target_pairs={{1,0},{2,1},{3,2},{0,3},{5,4},{6,5},{7,6},{4,7},{9,8},{10,9},{11,1... | collective-permute-start | bytes 98312 | tf_op jit(solution)/shard_map/ppermute | solution.py:618
  30.4 0.0 collective-permute-start.2
  30.4 1.6 %collective-permute-done.3.refs_17_ = f32[8,8,128]{2,1,0:T(8,128)S(1)} collective-permute-done((f32[8,8,128]{2,1,0:T(8,128)S(1)}, f32[8,8,128]{2,1,0:T(8,128)S(1)}, u32[]{:S(2)}, u32[]{:S(2)}) %collective-permute-start.3) | collective-permute-done | bytes 32800 | tf_op jit(solution)/shard_map/ppermute | solution.py:618
  32.0 4.1 %collective-permute-done.2.refs_16_ = f32[8,8,128]{2,1,0:T(8,128)S(1)} collective-permute-done((f32[8,8,128]{2,1,0:T(8,128)S(1)}, f32[8,8,128]{2,1,0:T(8,128)S(1)}, u32[]{:S(2)}, u32[]{:S(2)}) %collective-permute-start.2) | collective-permute-done | bytes 32800 | tf_op jit(solution)/shard_map/ppermute | solution.py:617
  36.2 0.0 copy-done.1
  36.2 0.0 copy-done.3
  36.2 0.0 copy-done.5
  36.2 0.0 copy-done.7
  36.2 0.0 copy-done.9
  36.2 0.0 copy-done.11
  36.2 0.0 copy-done.13
  36.2 0.0 copy-done.17
  36.2 0.1 pack_rows.1
  36.3 0.1 collective-permute-start.4
  36.4 1.7 %collective-permute-start.5 = (f32[21,8,128]{2,1,0:T(8,128)S(1)}, f32[21,8,128]{2,1,0:T(8,128)S(1)}, u32[]{:S(2)}, u32[]{:S(2)}) collective-permute-start(f32[21,8,128]{2,1,0:T(8,128)S(1)} %get-tuple-element.10), channel_id=1, source_target_pairs={{4,0},{8,4},{12,8},{0,12},{5,1},{9,5},{13,9},{1,13},{6,2},{10,6},{... | collective-permute-start | bytes 258056 | tf_op jit(solution)/shard_map/ppermute | solution.py:625
  38.1 0.1 add_convert_fusion.place_ref
  38.2 2.1 %collective-permute-done.4.refs_19_ = f32[21,8,128]{2,1,0:T(8,128)S(1)} collective-permute-done((f32[21,8,128]{2,1,0:T(8,128)S(1)}, f32[21,8,128]{2,1,0:T(8,128)S(1)}, u32[]{:S(2)}, u32[]{:S(2)}) %collective-permute-start.4) | collective-permute-done | bytes 86048 | tf_op jit(solution)/shard_map/ppermute | solution.py:624
  40.3 0.0 collective-permute-done.5.refs_20_
  40.3 3.0 %edges.1.refs_4_ = f32[2,8,640]{2,1,0:T(8,128)S(1)} custom-call(f32[4]{0:T(128)S(1)} %add_convert_fusion.place_ref, f32[1,128,512]{2,1,0:T(8,128)S(1)} %copy-done.3, f32[1,128,512]{2,1,0:T(8,128)S(1)} %copy-done.5, f32[1,128,512]{2,1,0:T(8,128)S(1)} %copy-done.7, f32[1,128,512]{2,1,0:T(8,128)S(1)} %copy-done.9, f32[1,128,512]{2,1,0:T(8,128)S(1)} %copy-done.11, ...), custom_call_target="tpu_custom_call" | custom-call | tf_op jit(solution)/shard_map/edges/pallas_call | solution.py:507
  43.3 1.6 %collective-permute-start.6 = (f32[2,8,640]{2,1,0:T(8,128)S(1)}, f32[2,8,640]{2,1,0:T(8,128)S(1)}, u32[]{:S(2)}, u32[]{:S(2)}) collective-permute-start(f32[2,8,640]{2,1,0:T(8,128)S(1)} %edges.1.refs_4_), channel_id=1, source_target_pairs={{0,16},{16,0},{1,17},{17,1},{2,18},{18,2},{3,19},{19,3},{4,20},{20... | collective-permute-start | bytes 122888 | tf_op jit(solution)/shard_map/ppermute | solution.py:594
  44.9 2.5 %collective-permute-done.6.refs_5_ = f32[2,8,640]{2,1,0:T(8,128)S(1)} collective-permute-done((f32[2,8,640]{2,1,0:T(8,128)S(1)}, f32[2,8,640]{2,1,0:T(8,128)S(1)}, u32[]{:S(2)}, u32[]{:S(2)}) %collective-permute-start.6) | collective-permute-done | bytes 40992 | tf_op jit(solution)/shard_map/ppermute | solution.py:594
  47.4 0.0 collective-permute-done.refs_1_
  47.4 0.0 collective-permute-done.1.refs_3_
  47.4 0.0 copy-done.14
  47.4 0.0 copy-done.15
  47.4 1.5 %update.1 = (f32[2,128,512]{2,1,0:T(8,128)}, f32[2,128,512]{2,1,0:T(8,128)}, f32[2,128,512]{2,1,0:T(8,128)}) custom-call(f32[2,128,512]{2,1,0:T(8,128)S(1)} %copy-done.1, f32[2,128,512]{2,1,0:T(8,128)S(1)} %copy-done.14, f32[2,128,512]{2,1,0:T(8,128)S(1)} %copy-done.15, f32[2,64,512]{2,1,0:T(8,128)S(1)} %interior_0.1.refs_0_, ...), custom_call_target="tpu_custom_call" | custom-call | tf_op jit(solution)/shard_map/update/pallas_call | solution.py:575
  (9 shorter events, 0.0 us)
Async XLA Ops:
  0.6 1.0 %copy-start = (f32[2,128,512]{2,1,0:T(8,128)S(1)}, f32[2,128,512]{2,1,0:T(8,128)}, u32[]{:S(2)}) copy-start(f32[2,128,512]{2,1,0:T(8,128)} %maps_ref.1) | copy-start | bytes 1572868
  1.7 0.9 %copy-start.2 = (f32[1,128,512]{2,1,0:T(8,128)S(1)}, f32[1,128,512]{2,1,0:T(8,128)}, u32[]{:S(2)}) copy-start(f32[1,128,512]{2,1,0:T(8,128)} %refs_7_.9) | copy-start | bytes 786436
  2.6 0.9 %copy-start.4 = (f32[1,128,512]{2,1,0:T(8,128)S(1)}, f32[1,128,512]{2,1,0:T(8,128)}, u32[]{:S(2)}) copy-start(f32[1,128,512]{2,1,0:T(8,128)} %refs_8_.5) | copy-start | bytes 786436
  3.6 0.9 %copy-start.6 = (f32[1,128,512]{2,1,0:T(8,128)S(1)}, f32[1,128,512]{2,1,0:T(8,128)}, u32[]{:S(2)}) copy-start(f32[1,128,512]{2,1,0:T(8,128)} %refs_9_.5) | copy-start | bytes 786436
  4.5 0.9 %copy-start.8 = (f32[1,128,512]{2,1,0:T(8,128)S(1)}, f32[1,128,512]{2,1,0:T(8,128)}, u32[]{:S(2)}) copy-start(f32[1,128,512]{2,1,0:T(8,128)} %refs_10_.5) | copy-start | bytes 786436
  5.5 0.9 %copy-start.10 = (f32[1,128,512]{2,1,0:T(8,128)S(1)}, f32[1,128,512]{2,1,0:T(8,128)}, u32[]{:S(2)}) copy-start(f32[1,128,512]{2,1,0:T(8,128)} %refs_11_.5) | copy-start | bytes 786436
  6.4 0.9 %copy-start.12 = (s32[128,512]{1,0:T(8,128)S(1)}, s32[128,512]{1,0:T(8,128)}, u32[]{:S(2)}) copy-start(s32[128,512]{1,0:T(8,128)} %refs_12_.5) | copy-start | bytes 786436
  7.4 0.7 %copy-start.16 = (s32[1,128]{1,0:T(1,128)S(1)}, s32[1,128]{1,0:T(1,128)}, u32[]{:S(2)}) copy-start(s32[1,128]{1,0:T(1,128)} %refs_18_.3) | copy-start | bytes 1540
  15.4 31.9 %collective-permute-start = (f32[2,64,512]{2,1,0:T(8,128)S(1)}, f32[2,64,512]{2,1,0:T(8,128)S(1)}, u32[]{:S(2)}, u32[]{:S(2)}) collective-permute-start(f32[2,64,512]{2,1,0:T(8,128)S(1)} %interior_0.1.refs_0_), channel_id=1, source_target_pairs={{0,16},{16,0},{1,17},{17,1},{2,18},{18,2},{3,19},{19,3},{4,20},{20... | collective-permute-start | bytes 786440 | tf_op jit(solution)/shard_map/ppermute | solution.py:594
  25.9 10.3 %copy-start.1 = (f32[2,128,512]{2,1,0:T(8,128)S(1)}, f32[2,128,512]{2,1,0:T(8,128)}, u32[]{:S(2)}) copy-start(f32[2,128,512]{2,1,0:T(8,128)} %maps_ref.1) | copy-start | bytes 1572868
  25.9 10.3 %copy-start.3 = (f32[1,128,512]{2,1,0:T(8,128)S(1)}, f32[1,128,512]{2,1,0:T(8,128)}, u32[]{:S(2)}) copy-start(f32[1,128,512]{2,1,0:T(8,128)} %refs_7_.9) | copy-start | bytes 786436
  25.9 10.3 %copy-start.5 = (f32[1,128,512]{2,1,0:T(8,128)S(1)}, f32[1,128,512]{2,1,0:T(8,128)}, u32[]{:S(2)}) copy-start(f32[1,128,512]{2,1,0:T(8,128)} %refs_8_.5) | copy-start | bytes 786436
  25.9 10.3 %copy-start.7 = (f32[1,128,512]{2,1,0:T(8,128)S(1)}, f32[1,128,512]{2,1,0:T(8,128)}, u32[]{:S(2)}) copy-start(f32[1,128,512]{2,1,0:T(8,128)} %refs_9_.5) | copy-start | bytes 786436
  25.9 10.3 %copy-start.9 = (f32[1,128,512]{2,1,0:T(8,128)S(1)}, f32[1,128,512]{2,1,0:T(8,128)}, u32[]{:S(2)}) copy-start(f32[1,128,512]{2,1,0:T(8,128)} %refs_10_.5) | copy-start | bytes 786436
  25.9 10.3 %copy-start.11 = (f32[1,128,512]{2,1,0:T(8,128)S(1)}, f32[1,128,512]{2,1,0:T(8,128)}, u32[]{:S(2)}) copy-start(f32[1,128,512]{2,1,0:T(8,128)} %refs_11_.5) | copy-start | bytes 786436
  25.9 10.3 %copy-start.13 = (s32[128,512]{1,0:T(8,128)S(1)}, s32[128,512]{1,0:T(8,128)}, u32[]{:S(2)}) copy-start(s32[128,512]{1,0:T(8,128)} %refs_12_.5) | copy-start | bytes 786436
  25.9 21.5 %collective-permute-start.1 = (f32[2,64,512]{2,1,0:T(8,128)S(1)}, f32[2,64,512]{2,1,0:T(8,128)S(1)}, u32[]{:S(2)}, u32[]{:S(2)}) collective-permute-start(f32[2,64,512]{2,1,0:T(8,128)S(1)} %interior_64.1.refs_2_), channel_id=1, source_target_pairs={{0,16},{16,0},{1,17},{17,1},{2,18},{18,2},{3,19},{19,3},{4,20},{20... | collective-permute-start | bytes 786440 | tf_op jit(solution)/shard_map/ppermute | solution.py:594
  26.3 5.8 %collective-permute-start.3 = (f32[8,8,128]{2,1,0:T(8,128)S(1)}, f32[8,8,128]{2,1,0:T(8,128)S(1)}, u32[]{:S(2)}, u32[]{:S(2)}) collective-permute-start(f32[8,8,128]{2,1,0:T(8,128)S(1)} %get-tuple-element.7.refs_14_), channel_id=1, source_target_pairs={{1,0},{2,1},{3,2},{0,3},{5,4},{6,5},{7,6},{4,7},{9,8},{10,9},{11,1... | collective-permute-start | bytes 98312 | tf_op jit(solution)/shard_map/ppermute | solution.py:618
  30.4 5.7 %collective-permute-start.2 = (f32[8,8,128]{2,1,0:T(8,128)S(1)}, f32[8,8,128]{2,1,0:T(8,128)S(1)}, u32[]{:S(2)}, u32[]{:S(2)}) collective-permute-start(f32[8,8,128]{2,1,0:T(8,128)S(1)} %get-tuple-element.8.refs_15_), channel_id=1, source_target_pairs={{0,1},{1,2},{2,3},{3,0},{4,5},{5,6},{6,7},{7,4},{8,9},{9,10},{10,1... | collective-permute-start | bytes 98312 | tf_op jit(solution)/shard_map/ppermute | solution.py:617
  30.4 5.8 %copy-start.17 = (s32[1,128]{1,0:T(1,128)S(1)}, s32[1,128]{1,0:T(1,128)}, u32[]{:S(2)}) copy-start(s32[1,128]{1,0:T(1,128)} %refs_18_.3) | copy-start | bytes 1540
  36.3 4.0 %collective-permute-start.4 = (f32[21,8,128]{2,1,0:T(8,128)S(1)}, f32[21,8,128]{2,1,0:T(8,128)S(1)}, u32[]{:S(2)}, u32[]{:S(2)}) collective-permute-start(f32[21,8,128]{2,1,0:T(8,128)S(1)} %get-tuple-element.9), channel_id=1, source_target_pairs={{0,4},{4,8},{8,12},{12,0},{1,5},{5,9},{9,13},{13,1},{2,6},{6,10},{... | collective-permute-start | bytes 258056 | tf_op jit(solution)/shard_map/ppermute | solution.py:624
  36.4 3.9 %collective-permute-start.5 = (f32[21,8,128]{2,1,0:T(8,128)S(1)}, f32[21,8,128]{2,1,0:T(8,128)S(1)}, u32[]{:S(2)}, u32[]{:S(2)}) collective-permute-start(f32[21,8,128]{2,1,0:T(8,128)S(1)} %get-tuple-element.10), channel_id=1, source_target_pairs={{4,0},{8,4},{12,8},{0,12},{5,1},{9,5},{13,9},{1,13},{6,2},{10,6},{... | collective-permute-start | bytes 258056 | tf_op jit(solution)/shard_map/ppermute | solution.py:625
  38.2 9.2 %copy-start.14 = (f32[2,128,512]{2,1,0:T(8,128)S(1)}, f32[2,128,512]{2,1,0:T(8,128)}, u32[]{:S(2)}) copy-start(f32[2,128,512]{2,1,0:T(8,128)} %first_ref.1) | copy-start | bytes 1572868
  38.2 9.2 %copy-start.15 = (f32[2,128,512]{2,1,0:T(8,128)S(1)}, f32[2,128,512]{2,1,0:T(8,128)}, u32[]{:S(2)}) copy-start(f32[2,128,512]{2,1,0:T(8,128)} %second_ref.1) | copy-start | bytes 1572868
  43.3 4.1 %collective-permute-start.6 = (f32[2,8,640]{2,1,0:T(8,128)S(1)}, f32[2,8,640]{2,1,0:T(8,128)S(1)}, u32[]{:S(2)}, u32[]{:S(2)}) collective-permute-start(f32[2,8,640]{2,1,0:T(8,128)S(1)} %edges.1.refs_4_), channel_id=1, source_target_pairs={{0,16},{16,0},{1,17},{17,1},{2,18},{18,2},{3,19},{19,3},{4,20},{20... | collective-permute-start | bytes 122888 | tf_op jit(solution)/shard_map/ppermute | solution.py:594

commit v2 on v1

v2 whole, which is shorter than its diff:
```python
import functools

import jax
import jax.numpy as jnp
from jax import lax
from jax.experimental import pallas as pl
from jax.experimental.pallas import tpu as pltpu
from jax.sharding import PartitionSpec as P

STEPS = 2
ADAM_STEP = 10
REACH_MAX = 0.2
PRIOR_WEIGHT = 0.1
GROWTH_RATE = 0.5
MUTATION_INPUT = 0.02
LEARN_RATE = 0.01
BETA_FIRST = 0.9
BETA_SECOND = 0.999
ADAM_EPS = 1e-08
LOSS_WEIGHT = 2.0

F32 = jnp.float32
LANES = 128
EDGE = 8
HALO = 4
DENSITY, TRAIT, VARIANCE, DISPERSAL, SELECTION, OPTIMUM, LAND, OBSERVED = range(8)
FIELDS = 8
GROUP = 3
WINDOW_US, EDGES_US = 4, 20
VMEM_BYTES = 16 * 1024 * 1024
SAVED = (
    "half",
    "land",
    "select",
    "n0",
    "q0",
    "m0",
    "wd",
    "wr",
    "lr",
    "dr0n",
    "dr0q",
    "dr0m",
    "e",
    "d",
    "vs",
    "p",
    "zs",
    "r",
    "n1",
    "q1",
    "m1",
    "z1",
    "u1",
    "dr1n",
    "dr1q",
    "dr1m",
    "a2n",
    "a2q",
    "a2m",
    "gsel",
    "gd",
    "gr",
    "a1n",
    "a1q",
    "a1m",
)


def cost(microseconds):
    return pl.CostEstimate(flops=int(microseconds * 1e9), transcendentals=0, bytes_accessed=int(microseconds * 3.6e6))


def reciprocal(value):
    guess = pl.reciprocal(value, approx=True)
    return guess * (2.0 - value * guess)


def sigmoid(value):
    return 0.5 + 0.5 * jnp.tanh(0.5 * value)


def dynamics(slabs, group, tiles, load, steps_at, keep, put):
    shape = (tiles, 8, LANES)
    lane = lax.broadcasted_iota(jnp.int32, shape, 2)
    at_last, at_first = lane == LANES - 1, lane == 0

    def right(value):
        turned = pltpu.roll(value, LANES - 1, 2)
        beside = jnp.concatenate([turned[1:], turned[:1]], 0) if tiles > 1 else turned
        return jnp.where(at_last, beside, turned)

    def left(value):
        turned = pltpu.roll(value, 1, 2)
        beside = jnp.concatenate([turned[-1:], turned[:-1]], 0) if tiles > 1 else turned
        return jnp.where(at_first, beside, turned)

    def each_slab(body, carry=()):
        def step(index, carry):
            for offset in range(group):
                carry = body(index * group + offset, carry)
            return carry

        if group == slabs:
            return step(0, carry)
        return lax.fori_loop(0, slabs // group, step, carry)

    def close(names):
        for name in names:
            keep[name][slabs] = pltpu.roll(keep[name][0], 7, 1)

    def wrapped(values):
        return tuple(pltpu.roll(value, 1, 1) for value in values)

    def down_gap(name, k):
        return keep[name][k + 1] - keep[name][k]

    def row_fluxes(names, k):
        weight = keep["wd"][k]
        gaps = [down_gap(name, k) for name in names]
        return gaps, tuple(weight * gap for gap in gaps)

    def spread(names, k, above):
        row_gaps, row_flux = row_fluxes(names, k)
        weight = keep["wr"][k]
        out, col_gaps = [], []
        for name, flux, before in zip(names, row_flux, above):
            value = keep[name][k]
            gap = right(value) - value
            col_flux = weight * gap
            out.append(value + (flux - before) + (col_flux - left(col_flux)))
            col_gaps.append(gap)
        return out, row_gaps, col_gaps, row_flux

    def begin(k, _):
        keep["half"][k] = 0.5 * REACH_MAX * sigmoid(load(DISPERSAL, k))
        keep["land"][k] = load(LAND, k)
        raw = load(SELECTION, k)
        keep["select"][k] = jnp.maximum(raw, 0.0) + jnp.log(1.0 + jnp.exp(-jnp.abs(raw)))
        n, z, v = load(DENSITY, k), load(TRAIT, k), load(VARIANCE, k)
        keep["n0"][k] = n
        keep["q0"][k] = n * z
        keep["m0"][k] = n * (v + z * z)
        return ()

    each_slab(begin)
    close(("half", "land", "n0", "q0", "m0"))

    def weigh(k, _):
        half, land = keep["half"][k], keep["land"][k]
        keep["wd"][k] = (half + keep["half"][k + 1]) * (land * keep["land"][k + 1])
        pair = land * right(land)
        keep["lr"][k] = pair
        keep["wr"][k] = (half + right(half)) * pair
        return ()

    each_slab(weigh)
    first_names, second_names = ("n0", "q0", "m0"), ("n1", "q1", "m1")

    def first_step(k, above):
        (ns, qs, ms), _, col_gaps, above = spread(first_names, k, above)
        for name, gap in zip(("dr0n", "dr0q", "dr0m"), col_gaps):
            keep[name][k] = gap
        z, v = load(TRAIT, k), load(VARIANCE, k)
        optimum, select, land = load(OPTIMUM, k), keep["select"][k], keep["land"][k]
        r = reciprocal(ns + PRIOR_WEIGHT)
        zs = (qs + PRIOR_WEIGHT * z) * r
        vs = (ms + PRIOR_WEIGHT * (v + z * z)) * r - zs * zs
        d = zs - optimum
        p = reciprocal(1.0 + select * vs)
        e = jnp.exp(land * (GROWTH_RATE * (1.0 - ns) - 0.5 * select * (d * d + vs)))
        n1 = ns * e
        z1 = optimum + p * d
        u1 = vs * p + MUTATION_INPUT + z1 * z1
        for name, value in zip(
            ("e", "d", "vs", "p", "zs", "r", "n1", "q1", "m1", "z1", "u1"),
            (e, d, vs, p, zs, r, n1, n1 * z1, n1 * u1, z1, u1),
        ):
            keep[name][k] = value
        return above

    each_slab(first_step, wrapped(row_fluxes(first_names, slabs - 1)[1]))
    close(second_names)

    def second_step(k, above):
        (ns, qs, ms), _, col_gaps, above = spread(second_names, k, above)
        for name, gap in zip(("dr1n", "dr1q", "dr1m"), col_gaps):
            keep[name][k] = gap
        optimum, select, land = load(OPTIMUM, k), keep["select"][k], keep["land"][k]
        r = reciprocal(ns + PRIOR_WEIGHT)
        zs = (qs + PRIOR_WEIGHT * keep["z1"][k]) * r
        es = (ms + PRIOR_WEIGHT * keep["u1"][k]) * r
        vs = es - zs * zs
        d = zs - optimum
        misfit = d * d + vs
        e = jnp.exp(land * (GROWTH_RATE * (1.0 - ns) - 0.5 * select * misfit))
        n2 = ns * e
        weight = jnp.where(steps_at(k) == 2.0, 2.0 * LOSS_WEIGHT * land, 0.0)
        an = weight * (n2 - load(OBSERVED, k))
        b = 0.5 * an * n2
        av = -b * select
        am = av * r
        aq = -2.0 * optimum * am
        keep["gsel"][k] = -b * misfit
        keep["a2n"][k] = an * e - b - (aq * zs + am * es)
        keep["a2q"][k] = aq
        keep["a2m"][k] = am
        return above

    each_slab(second_step, wrapped(row_fluxes(second_names, slabs - 1)[1]))
    second_back, first_back = ("a2n", "a2q", "a2m"), ("a1n", "a1q", "a1m")
    close(second_back)

    def back(k, above):
        (an, aq, am), row_gaps, col_gaps, above = spread(second_back, k, above)
        n_gap, q_gap, m_gap = [down_gap(name, k) * gap for name, gap in zip(second_names, row_gaps)]
        keep["gd"][k] = n_gap + q_gap + m_gap
        n_gap, q_gap, m_gap = [keep[f][k] * gap for f, gap in zip(("dr1n", "dr1q", "dr1m"), col_gaps)]
        keep["gr"][k] = n_gap + q_gap + m_gap
        n1, z1, land, select = keep["n1"][k], keep["z1"][k], keep["land"][k], keep["select"][k]
        e, d, vs, p, zs, r = (keep[name][k] for name in ("e", "d", "vs", "p", "zs", "r"))
        av = PRIOR_WEIGHT * keep["a2m"][k] + am * n1
        az = PRIOR_WEIGHT * keep["a2q"][k] + aq * n1 + 2.0 * z1 * av
        weight = jnp.where(steps_at(k) == 1.0, 2.0 * LOSS_WEIGHT * land, 0.0)
        an = an + aq * z1 + am * keep["u1"][k] + weight * (n1 - load(OBSERVED, k))
        b = 0.5 * an * n1 * land
        at = -(az * d + av * vs) * (p * p)
        gsel = keep["gsel"][k] + at * vs - b * (d * d + vs)
        avs = av * p + select * (at - b)
        azs = az * p - 2.0 * (b * select * d + zs * avs)
        aqs, ams = azs * r, avs * r
        keep["a1n"][k] = an * e - b - (aqs * zs + ams * (vs + zs * zs))
        keep["a1q"][k] = aqs
        keep["a1m"][k] = ams
        put(1, k, gsel * sigmoid(load(SELECTION, k)))
        return above

    each_slab(back, wrapped(row_fluxes(second_back, slabs - 1)[1]))
    close(first_back)

    def row_share(k):
        n_gap, q_gap, m_gap = [down_gap(a, k) * down_gap(f, k) for a, f in zip(first_back, first_names)]
        return (keep["gd"][k] + n_gap + q_gap + m_gap) * (keep["land"][k] * keep["land"][k + 1])

    def finish(k, above):
        here = row_share(k)
        total = keep["gr"][k]
        for name, field in zip(first_back, ("dr0n", "dr0q", "dr0m")):
            value = keep[name][k]
            total = total + (right(value) - value) * keep[field][k]
        total = total * keep["lr"][k]
        half = keep["half"][k]
        put(0, k, half * (10.0 * half - 1.0) * (here + above[0] + total + left(total)))
        return (here,)

    each_slab(finish, wrapped((row_share(slabs - 1),)))


def step_rows(line):
    return jnp.transpose(jnp.concatenate([line] * (LANES // 8), 0))


def fill_kernel(tiles, sources, step_ref, fields, steps, codes, sems):
    density, trait, variance, optimum, observed, land_code, maps = sources
    copies = []
    for field, (source, target) in enumerate(
        (
            (density.at[0], fields.at[DENSITY]),
            (trait.at[0], fields.at[TRAIT]),
            (variance.at[0], fields.at[VARIANCE]),
            (maps.at[0], fields.at[DISPERSAL]),
            (maps.at[1], fields.at[SELECTION]),
            (optimum.at[0], fields.at[OPTIMUM]),
            (land_code, codes),
            (observed.at[0], fields.at[OBSERVED]),
        )
    ):
        for t in range(tiles):
            copies.append(
                pltpu.make_async_copy(source.at[:, pl.ds(t * LANES, LANES)], target.at[t], sems.at[field, t])
            )
    for copy in copies:
        copy.start()
    line = jnp.broadcast_to(step_ref[0:1, :].astype(F32), (8, LANES))
    steps[0] = step_rows(line)
    steps[1] = jnp.broadcast_to(line[0:1], (LANES, LANES))
    for copy in copies:
        copy.wait()
    fields[LAND] = codes[...].astype(F32)


def window_kernel(first, rows, skip, fields, steps, *refs):
    out_ref, grads, kept = refs[-3:]
    tiles = fields.shape[1]
    out_rows = out_ref.shape[1]
    slabs = rows // 8

    def load(field, k):
        return jnp.stack([fields[field, t, pl.ds(first + k, 8, stride=slabs), :] for t in range(tiles)])

    def steps_at(k):
        part = steps[0, pl.ds(first + k, 8, stride=slabs), :]
        return jnp.broadcast_to(part[None], (tiles, 8, LANES))

    def put(which, k, value):
        for t in range(tiles):
            grads[which, t, pl.ds(k, 8, stride=slabs), :] = value[t]

    keep = {name: kept.at[index] for index, name in enumerate(SAVED)}
    dynamics(slabs, GROUP, tiles, load, steps_at, keep, put)
    for which in range(2):
        for t in range(tiles):
            out_ref[which, :, t * LANES : (t + 1) * LANES] = grads[which, t, skip : skip + out_rows, :]


def load_kernel(tiles, *refs):
    sources, step_ref, fields, steps, left_ref, right_ref, codes, sems = refs[:7], *refs[7:]
    fill_kernel(tiles, sources, step_ref, fields, steps, codes, sems)
    columns_kernel(fields, left_ref, right_ref)


def load_tile(sources, obs_step):
    height, columns = sources[0].shape[1:]
    tiles = columns // LANES
    strip = jax.ShapeDtypeStruct((FIELDS, EDGE, height), F32)
    return pl.pallas_call(
        functools.partial(load_kernel, tiles),
        out_shape=[
            jax.ShapeDtypeStruct((FIELDS, tiles, height, LANES), F32),
            jax.ShapeDtypeStruct((2, LANES, LANES), F32),
            strip,
            strip,
        ],
        in_specs=[pl.BlockSpec(memory_space=pltpu.HBM)] * 7 + [pl.BlockSpec(memory_space=pltpu.VMEM)],
        out_specs=[pl.BlockSpec(memory_space=pltpu.VMEM)] * 4,
        scratch_shapes=[
            pltpu.VMEM((tiles, height, LANES), jnp.int32),
            pltpu.SemaphoreType.DMA((FIELDS, tiles)),
        ],
        compiler_params=pltpu.CompilerParams(vmem_limit_bytes=VMEM_BYTES),
        name="load_tile",
    )(*(pltpu.with_memory_space_constraint(source, pltpu.HBM) for source in sources), obs_step)


def window(first, rows, out_first, out_rows, fields, steps, *after):
    tiles = fields.shape[1]
    return pl.pallas_call(
        functools.partial(window_kernel, first, rows, out_first - first),
        out_shape=jax.ShapeDtypeStruct((2, out_rows, tiles * LANES), F32),
        in_specs=[pl.BlockSpec(memory_space=pltpu.VMEM)] * 2 + [pl.BlockSpec(memory_space=pltpu.VMEM)] * len(after),
        out_specs=pl.BlockSpec(memory_space=pltpu.VMEM),
        scratch_shapes=[
            pltpu.VMEM((2, tiles, rows, LANES), F32),
            pltpu.VMEM((len(SAVED), rows // 8 + 1, tiles, 8, LANES), F32),
        ],
        cost_estimate=cost(WINDOW_US),
        compiler_params=pltpu.CompilerParams(vmem_limit_bytes=VMEM_BYTES),
        name=f"window_{out_first}",
    )(fields, steps, *after)


def columns_kernel(fields, left_ref, right_ref):
    tiles, rows = fields.shape[1:3]
    lane = lax.broadcasted_iota(jnp.int32, (rows, LANES), 1)
    packed = jnp.zeros((rows, LANES), F32)
    for field in range(FIELDS):
        both = jnp.where(lane < EDGE, fields[field, 0], fields[field, tiles - 1])
        turned = pltpu.roll(both, 16 * field, 1) if field else both
        place = (lane - 16 * field + EDGE) % LANES
        packed = jnp.where(place < 2 * EDGE, turned, packed)
    flipped = jnp.transpose(packed)
    for field in range(FIELDS):
        left_ref[field] = flipped[16 * field : 16 * field + EDGE]
        start = (16 * field - EDGE) % LANES
        right_ref[field] = flipped[start : start + EDGE]


def in_vmem(kernel, name, out_shape, scratch=()):
    def call(*operands):
        many = isinstance(out_shape, (list, tuple))
        space = pl.BlockSpec(memory_space=pltpu.VMEM)
        return pl.pallas_call(
            kernel,
            out_shape=out_shape,
            in_specs=[space] * len(operands),
            out_specs=[space] * len(out_shape) if many else space,
            scratch_shapes=list(scratch),
            compiler_params=pltpu.CompilerParams(vmem_limit_bytes=VMEM_BYTES),
            name=name,
        )(*operands)

    return call


def rows_kernel(fields, steps, own_left, own_right, from_left, from_right, up_ref, down_ref):
    tiles = fields.shape[1]
    sub = lax.broadcasted_iota(jnp.int32, (8, LANES), 0)
    for pair in range(FIELDS // 2):
        for t in range(tiles):
            even, odd = fields.at[2 * pair, t], fields.at[2 * pair + 1, t]
            up_ref[pair * tiles + t] = jnp.where(sub < HALO, even[:EDGE], pltpu.roll(odd[:EDGE], HALO, 0))
            down_ref[pair * tiles + t] = jnp.where(sub < HALO, pltpu.roll(odd[-EDGE:], HALO, 0), even[-EDGE:])
    lane = lax.broadcasted_iota(jnp.int32, (8, LANES), 1)
    base = FIELDS // 2 * tiles
    for index, strip in enumerate((from_left, own_left, own_right, from_right)):
        packed = jnp.zeros((8, LANES), F32)
        for field in range(FIELDS):
            turned = pltpu.roll(strip[field], 8 * field, 1) if field else strip[field]
            place = (lane - 8 * field + HALO) % LANES
            packed = jnp.where(place < 2 * HALO, turned, packed)
        up_ref[base + index] = packed
        down_ref[base + index] = packed
    up_ref[base + 4] = steps[1, :8]
    down_ref[base + 4] = steps[1, :8]


def pack_rows(fields, steps, strips):
    shape = jax.ShapeDtypeStruct((FIELDS // 2 * fields.shape[1] + 5, 8, LANES), F32)
    return in_vmem(rows_kernel, "pack_rows", [shape, shape])(fields, steps, *strips)


def edges_kernel(place_ref, fields, steps, *refs):
    own_left, own_right, from_left, from_right, from_above, from_below, out_ref = refs[:7]
    row_strip, col_strip, row_step, row_grad, col_grad, row_keep, col_keep = refs[7:]
    tiles = fields.shape[1]
    base = FIELDS // 2 * tiles
    has_above, has_below, has_left, has_right = (place_ref[i] for i in range(4))
    lane = lax.broadcasted_iota(jnp.int32, (8, LANES), 1)
    sub = lax.broadcasted_iota(jnp.int32, (8, LANES), 0)

    corners = [
        jnp.where((lane % 8) < HALO, from_below[base + index], from_above[base + index]) for index in range(4)
    ]
    beside = [[None] * 4 for _ in range(FIELDS)]
    for field in range(FIELDS):
        for index, strip in enumerate((from_left, own_left, own_right, from_right)):
            value = strip[field]
            outer = pltpu.roll(corners[index], (LANES - 8 * field) % LANES, 1) if field else corners[index]
            if field == LAND:
                outer = outer * jnp.where(lane < LANES // 2, has_below, has_above)
                if index == 0:
                    value, outer = value * has_left, outer * has_left
                if index == 3:
                    value, outer = value * has_right, outer * has_right
            col_strip[field, 0, 8 * index : 8 * index + 8, :] = value
            col_strip[field, 1, 8 * index : 8 * index + 8, :] = outer
            beside[field][index] = (value, outer)

    def lined(value, outer):
        out = jnp.where(lane < 8, pltpu.roll(outer, 8, 1), pltpu.roll(value, 8, 1))
        out = jnp.where(lane < 16, out, pltpu.roll(value, 24, 1))
        return jnp.where(lane < 24, out, pltpu.roll(outer, 24, 1))

    zeros = jnp.zeros((8, LANES), F32)
    stack = []
    for index in range(LANES // 8):
        here = lined(*beside[index][3]) if index < FIELDS else zeros
        following = (index + 1) % (LANES // 8)
        after = lined(*beside[following][0]) if following < FIELDS else zeros
        stack.append(jnp.where(sub < HALO, here, after))
    flipped = jnp.transpose(jnp.concatenate(stack, 0))[:32]
    own_step = steps[1, :8]
    outer_step = jnp.where(lane < LANES // 2, from_below[base + 4], from_above[base + 4])
    row_step[...] = step_rows(lined(own_step, outer_step))[:32]
    for field in range(FIELDS):
        for t in range(tiles):
            above, below = from_above[field // 2 * tiles + t], from_below[field // 2 * tiles + t]
            if field % 2:
                above, below = pltpu.roll(above, HALO, 0), pltpu.roll(below, HALO, 0)
            if field == LAND:
                above, below = above * has_above, below * has_below
            own = fields.at[field, t]
            for index, value in enumerate((above, own[:EDGE], own[-EDGE:], below)):
                row_strip[field, t, 8 * index : 8 * index + 8, :] = value
        row_strip[field, tiles] = pltpu.roll(flipped, (LANES - 8 * field) % LANES, 1) if field else flipped

    slabs = 3
    for strip, grad, kept, count in (
        (row_strip, row_grad, row_keep, tiles + 1),
        (col_strip, col_grad, col_keep, 2),
    ):
        on_rows = strip is row_strip

        def load(field, k):
            parts = [strip[field, t, pl.ds(HALO + k, 8, stride=slabs), :] for t in range(count)]
            return jnp.stack(parts)

        def steps_at(k):
            if on_rows:
                part = row_step[pl.ds(HALO + k, 8, stride=slabs), :]
                return jnp.broadcast_to(part[None], (count, 8, LANES))
            return jnp.stack([own_step, outer_step])

        def put(which, k, value):
            for t in range(count):
                grad[which, t, pl.ds(HALO + k, 8, stride=slabs), :] = value[t]

        keep = {name: kept.at[index] for index, name in enumerate(SAVED)}
        dynamics(slabs, slabs, count, load, steps_at, keep, put)
    for which in range(2):
        for t in range(tiles):
            out_ref[which, :, t * LANES : (t + 1) * LANES] = jnp.where(
                sub < HALO, row_grad[which, t, 8:16, :], row_grad[which, t, 16:24, :]
            )
        out_ref[which, :, tiles * LANES :] = jnp.where(
            sub < HALO, col_grad[which, 0, 8:16, :], col_grad[which, 0, 16:24, :]
        )


def edges(place, fields, steps, strips, from_above, from_below):
    tiles = fields.shape[1]
    scratch = [
        pltpu.VMEM((FIELDS, tiles + 1, 32, LANES), F32),
        pltpu.VMEM((FIELDS, 2, 32, LANES), F32),
        pltpu.VMEM((32, LANES), F32),
        pltpu.VMEM((2, tiles + 1, 32, LANES), F32),
        pltpu.VMEM((2, 2, 32, LANES), F32),
        pltpu.VMEM((len(SAVED), 4, tiles + 1, 8, LANES), F32),
        pltpu.VMEM((len(SAVED), 4, 2, 8, LANES), F32),
    ]
    operands = [place, fields, steps, *strips, from_above, from_below]
    space = pl.BlockSpec(memory_space=pltpu.VMEM)
    return pl.pallas_call(
        edges_kernel,
        out_shape=jax.ShapeDtypeStruct((2, EDGE, (tiles + 1) * LANES), F32),
        in_specs=[pl.BlockSpec(memory_space=pltpu.SMEM)] + [space] * (len(operands) - 1),
        out_specs=space,
        scratch_shapes=scratch,
        cost_estimate=cost(EDGES_US),
        compiler_params=pltpu.CompilerParams(vmem_limit_bytes=VMEM_BYTES),
        name="edges",
    )(*operands)


def update_kernel(parts, terms, maps_ref, first_ref, second_ref, *refs):
    grads, edge_refs = refs[: parts * terms], refs[parts * terms : (parts + 1) * terms]
    new_maps, new_first, new_second = refs[(parts + 1) * terms :]
    rows, columns = maps_ref.shape[1:]
    tiles = columns // LANES
    lane = lax.broadcasted_iota(jnp.int32, (rows, LANES), 1)
    sub = lax.broadcasted_iota(jnp.int32, (EDGE, LANES), 0)
    edge = sum(ref[...] for ref in edge_refs)
    strips = [edge[which, :, columns:] for which in range(2)]
    blank = jnp.zeros((LANES - 2 * EDGE, LANES), F32)
    flipped = jnp.transpose(jnp.concatenate([*strips, blank], 0))
    height = rows // parts
    for which in range(2):
        for t in range(tiles):
            own = slice(t * LANES, (t + 1) * LANES)
            grad = jnp.concatenate(
                [sum(ref[which, :, own] for ref in grads[part * terms : (part + 1) * terms]) for part in range(parts)],
                0,
            )
            outer = edge[which, :, own]
            grad = jnp.concatenate(
                [
                    jnp.where(sub < HALO, outer, grad[:EDGE]),
                    grad[EDGE:-EDGE],
                    jnp.where(sub < HALO, grad[-EDGE:], outer),
                ],
                0,
            )
            if t == 0:
                beside = pltpu.roll(flipped, LANES - EDGE * which, 1) if which else flipped
                grad = jnp.where(lane < HALO, beside, grad)
            if t == tiles - 1:
                beside = pltpu.roll(flipped, LANES - EDGE * (which + 1), 1)
                grad = jnp.where(lane >= LANES - HALO, beside, grad)
            first = BETA_FIRST * first_ref[which, :, own] + (1.0 - BETA_FIRST) * grad
            second = BETA_SECOND * second_ref[which, :, own] + (1.0 - BETA_SECOND) * grad * grad
            new_first[which, :, own] = first
            new_second[which, :, own] = second
            scale = jnp.sqrt(second * (1.0 / (1.0 - BETA_SECOND**ADAM_STEP))) + ADAM_EPS
            change = (LEARN_RATE / (1.0 - BETA_FIRST**ADAM_STEP)) * first
            new_maps[which, :, own] = maps_ref[which, :, own] - change * reciprocal(scale)


def update(maps, first_moment, second_moment, grads, edge_grads):
    parts, terms = len(grads), len(edge_grads)
    flat = [term for grad in grads for term in grad]
    shape = jax.ShapeDtypeStruct(maps.shape, F32)
    kernel = functools.partial(update_kernel, parts, terms)
    return in_vmem(kernel, "update", [shape] * 3)(maps, first_moment, second_moment, *flat, *edge_grads)


def shifts(axis):
    count = lax.axis_size(axis)
    forward = [(i, (i + 1) % count) for i in range(count)]
    return forward, [(target, source) for source, target in forward]


def both_scenarios(value):
    count = lax.axis_size("scen")
    if count == 2:
        return [value, lax.ppermute(value, "scen", [(0, 1), (1, 0)])]
    return [lax.psum(value, "scen")]


def shards(
    density,
    trait,
    variance,
    optimum,
    observed,
    obs_step,
    land_code,
    maps,
    first_moment,
    second_moment,
):
    sources = (density, trait, variance, optimum, observed, land_code, maps)
    rows = maps.shape[1]
    middle = rows // 2
    fields, steps, own_left, own_right = load_tile(sources, obs_step)
    rightward, leftward = shifts("ly")
    from_left = lax.ppermute(own_right, "ly", rightward)
    from_right = lax.ppermute(own_left, "ly", leftward)
    upper_terms = both_scenarios(window(0, middle + EDGE, 0, middle, fields, steps))
    strips = (own_left, own_right, from_left, from_right)
    up, down = pack_rows(fields, steps, strips)
    downward, upward = shifts("lx")
    from_above = lax.ppermute(down, "lx", downward)
    from_below = lax.ppermute(up, "lx", upward)
    lower = window(middle - EDGE, middle + EDGE, middle, middle, fields, steps, *strips, up, down)
    lower_terms = both_scenarios(lower)
    row, column = lax.axis_index("lx"), lax.axis_index("ly")
    place = jnp.stack(
        [row > 0, row < lax.axis_size("lx") - 1, column > 0, column < lax.axis_size("ly") - 1]
    ).astype(F32)
    outer = edges(place, fields, steps, strips, from_above, from_below)
    outer_terms = both_scenarios(outer)
    return tuple(update(maps, first_moment, second_moment, [upper_terms, lower_terms], outer_terms))


def solution(mesh):
    in_specs = (
        P("scen", "lx", "ly"),
        P("scen", "lx", "ly"),
        P("scen", "lx", "ly"),
        P("scen", "lx", "ly"),
        P("scen", "lx", "ly"),
        P("scen", "lx"),
        P("lx", "ly"),
        P(None, "lx", "ly"),
        P(None, "lx", "ly"),
        P(None, "lx", "ly"),
    )
    out_specs = (P(None, "lx", "ly"), P(None, "lx", "ly"), P(None, "lx", "ly"))
    return jax.shard_map(shards, mesh=mesh, in_specs=in_specs, out_specs=out_specs, check_vma=False)
```

time: 49.3 us -> 29.8 us (0.60)
  local copies, waits for them, and re-layouts: 7.44 us -> 0.67 us
  Pallas kernels: 19.7 us -> 13.2 us
  waiting for transfers between devices: 10.3 us -> 5.05 us
  starting transfers between devices: 10.6 us -> 9.86 us
    unnamed x36 -> x8, local copies, waits for them, and re-layouts: 7.44 us -> 0.67 us
    pallas_call x6, Pallas kernels: 19.7 us -> 13.2 us  [the longest x2 6.47 us: window(): pl.pallas_call(functools.partial(window_kernel, first, rows, out_first -...]
    ppermute x1, waiting for transfers between devices: 4.11 us -> 0.83 us  [shards(): from_left = lax.ppermute(own_right, 'ly', rightward)]
    ppermute x1, waiting for transfers between devices: 2.08 us -> 0.01 us  [shards(): from_above = lax.ppermute(down, 'lx', downward)]
    ppermute x3, waiting for transfers between devices: 2.52 us -> 4.22 us  [both_scenarios(): return [value, lax.ppermute(value, 'scen', [(0, 1), (1, 0)])]]
    ppermute x1, starting transfers between devices: 1.73 us -> 0.06 us  [shards(): from_below = lax.ppermute(up, 'lx', upward)]
    ppermute x1, waiting for transfers between devices: 1.59 us -> 0.01 us  [shards(): from_right = lax.ppermute(own_left, 'ly', leftward)]
    ppermute x1, starting transfers between devices: 4.17 us -> 5.1 us  [shards(): from_right = lax.ppermute(own_left, 'ly', leftward)]
  transfers between devices with their start and end apart: 7 -> 7, of which waited for: 4 -> 2; matrix products, arithmetic and copies ran while one was open for 0% -> 0% of each run, Pallas kernels for 22% -> 32%
where the time goes in v2:
time: 29.8 us; the launch traced here: 29.6 us
  Pallas kernels  13.2 us (44%)
  starting transfers between devices  9.86 us (33%)
  waiting for transfers between devices  5.05 us (17%)
  between operations  0.73 us (2%)
  local copies, waits for them, and re-layouts  0.67 us (2%)
    pallas_call x2, Pallas kernels, window(): pl.pallas_call(functools.partial(window_kernel, first, rows, out_first -...  6.47 us
    ppermute x1, starting transfers between devices, shards(): from_right = lax.ppermute(own_left, 'ly', leftward)  5.1 us
    ppermute x3, waiting for transfers between devices, both_scenarios(): return [value, lax.ppermute(value, 'scen', [(0, 1), (1, 0)])]  4.22 us
    ppermute x3, starting transfers between devices, both_scenarios(): return [value, lax.ppermute(value, 'scen', [(0, 1), (1, 0)])]  4.2 us
    pallas_call x1, Pallas kernels, edges(): pl.pallas_call(edges_kernel, out_shape=jax.ShapeDtypeStruct((2, EDGE, (ti...  3.03 us
    pallas_call x1, Pallas kernels, load_tile(): pl.pallas_call(functools.partial(load_kernel, tiles), out_shape=[jax.Shap...  2.13 us
    pallas_call x2, Pallas kernels, call(): pl.pallas_call(kernel, out_shape=out_shape, in_specs=[space] * len(operan...  1.62 us
    ppermute x1, waiting for transfers between devices, shards(): from_left = lax.ppermute(own_right, 'ly', rightward)  0.83 us
  transfers between devices with their start and end apart: 7, of which 2 were waited for; matrix products, arithmetic and copies ran while one was open for 0% of the time, Pallas kernels for 32%

profile of v2, /device:TPU:0, one launch (start us, length us, event | category | flops | bytes accessed | tf_op | source)
XLA Modules:
  0.0 29.6 jit_solution(10616227326030851116)
XLA Ops:
  0.6 0.0 copy-start.3
  0.6 0.6 %copy-done.3 = s32[1,128]{1,0:T(1,128)S(1)} copy-done((s32[1,128]{1,0:T(1,128)S(1)}, s32[1,128]{1,0:T(1,128)}, u32[]{:S(2)}) %copy-start.3) | copy-done | bytes 536
  1.3 2.1 %load_tile.1 = (f32[8,4,128,128]{3,2,1,0:T(8,128)S(1)}, f32[2,128,128]{2,1,0:T(8,128)S(1)}, f32[8,8,128]{2,1,0:T(8,128)S(1)}, f32[8,8,128]{2,1,0:T(8,128)S(1)}) custom-call(f32[1,128,512]{2,1,0:T(8,128)} %refs_0_.1, f32[1,128,512]{2,1,0:T(8,128)} %refs_1_.1, f32[1,128,512]{2,1,0:T(8,128)} %refs_2_.1, f32[1,128,512]{2,1,0:T(8,128)} %refs_3_.1, ...), custom_call_target="tpu_custom_call" | custom-call | tf_op jit(solution)/shard_map/load_tile/pallas_call | solution.py:326
  3.4 5.1 %collective-permute-start.2 = (f32[8,8,128]{2,1,0:T(8,128)S(1)}, f32[8,8,128]{2,1,0:T(8,128)S(1)}, u32[]{:S(2)}, u32[]{:S(2)}) collective-permute-start(f32[8,8,128]{2,1,0:T(8,128)S(1)} %get-tuple-element.11.own_left.refs_0_), channel_id=1, source_target_pairs={{1,0},{2,1},{3,2},{0,3},{5,4},{6,5},{7,6},{4,7},{9,8},{10,9},{11,1... | collective-permute-start | bytes 98312 | tf_op jit(solution)/shard_map/ppermute | solution.py:617
  8.5 0.0 collective-permute-start.1
  8.5 3.2 %window_0.1.refs_0_ = f32[2,64,512]{2,1,0:T(8,128)S(1)} custom-call(f32[8,4,128,128]{3,2,1,0:T(8,128)S(1)} %get-tuple-element.9.fields, f32[2,128,128]{2,1,0:T(8,128)S(1)} %get-tuple-element.10.steps), custom_call_target="tpu_custom_call" | custom-call | flops 4000000000 | bytes 14400000 | tf_op jit(solution)/shard_map/window_0/pallas_call | solution.py:347
  11.8 1.6 %collective-permute-start = (f32[2,64,512]{2,1,0:T(8,128)S(1)}, f32[2,64,512]{2,1,0:T(8,128)S(1)}, u32[]{:S(2)}, u32[]{:S(2)}) collective-permute-start(f32[2,64,512]{2,1,0:T(8,128)S(1)} %window_0.1.refs_0_), channel_id=1, source_target_pairs={{0,16},{16,0},{1,17},{17,1},{2,18},{18,2},{3,19},{19,3},{4,20},{20... | collective-permute-start | bytes 786440 | tf_op jit(solution)/shard_map/ppermute | solution.py:595
  13.3 0.1 add_convert_fusion.place_ref
  13.4 0.0 collective-permute-done.2.from_right.refs_3_
  13.4 0.8 %collective-permute-done.1.from_left.refs_2_ = f32[8,8,128]{2,1,0:T(8,128)S(1)} collective-permute-done((f32[8,8,128]{2,1,0:T(8,128)S(1)}, f32[8,8,128]{2,1,0:T(8,128)S(1)}, u32[]{:S(2)}, u32[]{:S(2)}) %collective-permute-start.1) | collective-permute-done | bytes 32800 | tf_op jit(solution)/shard_map/ppermute | solution.py:616
  14.2 0.1 pack_rows.1
  14.3 0.1 collective-permute-start.5
  14.4 0.5 %collective-permute-start.4 = (f32[21,8,128]{2,1,0:T(8,128)S(1)}, f32[21,8,128]{2,1,0:T(8,128)S(1)}, u32[]{:S(2)}, u32[]{:S(2)}) collective-permute-start(f32[21,8,128]{2,1,0:T(8,128)S(1)} %get-tuple-element.14.refs_5_), channel_id=1, source_target_pairs={{0,4},{4,8},{8,12},{12,0},{1,5},{5,9},{9,13},{13,1},{2,6},{6,10},{... | collective-permute-start | bytes 258056 | tf_op jit(solution)/shard_map/ppermute | solution.py:622
  14.9 3.2 %window_64.1.refs_2_ = f32[2,64,512]{2,1,0:T(8,128)S(1)} custom-call(f32[8,4,128,128]{3,2,1,0:T(8,128)S(1)} %get-tuple-element.9.fields, f32[2,128,128]{2,1,0:T(8,128)S(1)} %get-tuple-element.10.steps, f32[8,8,128]{2,1,0:T(8,128)S(1)} %get-tuple-element.11.own_left.refs_0_, f32[8,8,128]{2,1,0:T(8,128)S(1)} %get-tuple-element.12.own_right.refs_1_, ...), custom_call_target="tpu_custom_call" | custom-call | flops 4000000000 | bytes 14400000 | tf_op jit(solution)/shard_map/window_64/pallas_call | solution.py:347
  18.1 0.0 copy-start
  18.2 0.0 copy-start.1
  18.2 0.0 copy-start.2
  18.2 1.6 %collective-permute-start.3 = (f32[2,64,512]{2,1,0:T(8,128)S(1)}, f32[2,64,512]{2,1,0:T(8,128)S(1)}, u32[]{:S(2)}, u32[]{:S(2)}) collective-permute-start(f32[2,64,512]{2,1,0:T(8,128)S(1)} %window_64.1.refs_2_), channel_id=1, source_target_pairs={{0,16},{16,0},{1,17},{17,1},{2,18},{18,2},{3,19},{19,3},{4,20},{20... | collective-permute-start | bytes 786440 | tf_op jit(solution)/shard_map/ppermute | solution.py:595
  19.7 0.0 collective-permute-done.5.refs_5_
  19.7 0.0 collective-permute-done.4.refs_4_
  19.7 3.0 %edges.1.refs_4_ = f32[2,8,640]{2,1,0:T(8,128)S(1)} custom-call(f32[4]{0:T(128)S(1)} %add_convert_fusion.place_ref, f32[8,4,128,128]{3,2,1,0:T(8,128)S(1)} %get-tuple-element.9.fields, f32[2,128,128]{2,1,0:T(8,128)S(1)} %get-tuple-element.10.steps, f32[8,8,128]{2,1,0:T(8,128)S(1)} %get-tuple-element.11.own_left.refs_0_, ...), custom_call_target="tpu_custom_call" | custom-call | flops 20000000000 | bytes 72000000 | tf_op jit(solution)/shard_map/edges/pallas_call | solution.py:523
  22.8 1.1 %collective-permute-start.6 = (f32[2,8,640]{2,1,0:T(8,128)S(1)}, f32[2,8,640]{2,1,0:T(8,128)S(1)}, u32[]{:S(2)}, u32[]{:S(2)}) collective-permute-start(f32[2,8,640]{2,1,0:T(8,128)S(1)} %edges.1.refs_4_), channel_id=1, source_target_pairs={{0,16},{16,0},{1,17},{17,1},{2,18},{18,2},{3,19},{19,3},{4,20},{20... | collective-permute-start | bytes 122888 | tf_op jit(solution)/shard_map/ppermute | solution.py:595
  23.9 4.2 %collective-permute-done.6.refs_5_ = f32[2,8,640]{2,1,0:T(8,128)S(1)} collective-permute-done((f32[2,8,640]{2,1,0:T(8,128)S(1)}, f32[2,8,640]{2,1,0:T(8,128)S(1)}, u32[]{:S(2)}, u32[]{:S(2)}) %collective-permute-start.6) | collective-permute-done | bytes 40992 | tf_op jit(solution)/shard_map/ppermute | solution.py:595
  28.1 0.0 collective-permute-done.refs_1_
  28.1 0.0 collective-permute-done.3.refs_3_
  28.1 0.0 copy-done
  28.1 0.0 copy-done.1
  28.1 0.0 copy-done.2
  28.1 1.5 %update.1 = (f32[2,128,512]{2,1,0:T(8,128)}, f32[2,128,512]{2,1,0:T(8,128)}, f32[2,128,512]{2,1,0:T(8,128)}) custom-call(f32[2,128,512]{2,1,0:T(8,128)S(1)} %copy-done, f32[2,128,512]{2,1,0:T(8,128)S(1)} %copy-done.1, f32[2,128,512]{2,1,0:T(8,128)S(1)} %copy-done.2, f32[2,64,512]{2,1,0:T(8,128)S(1)} %window_0.1.refs_0_, ...), custom_call_target="tpu_custom_call" | custom-call | tf_op jit(solution)/shard_map/update/pallas_call | solution.py:382
Async XLA Ops:
  0.6 0.7 %copy-start.3 = (s32[1,128]{1,0:T(1,128)S(1)}, s32[1,128]{1,0:T(1,128)}, u32[]{:S(2)}) copy-start(s32[1,128]{1,0:T(1,128)} %refs_7_.1) | copy-start | bytes 1540
  3.4 10.0 %collective-permute-start.2 = (f32[8,8,128]{2,1,0:T(8,128)S(1)}, f32[8,8,128]{2,1,0:T(8,128)S(1)}, u32[]{:S(2)}, u32[]{:S(2)}) collective-permute-start(f32[8,8,128]{2,1,0:T(8,128)S(1)} %get-tuple-element.11.own_left.refs_0_), channel_id=1, source_target_pairs={{1,0},{2,1},{3,2},{0,3},{5,4},{6,5},{7,6},{4,7},{9,8},{10,9},{11,1... | collective-permute-start | bytes 98312 | tf_op jit(solution)/shard_map/ppermute | solution.py:617
  8.5 5.7 %collective-permute-start.1 = (f32[8,8,128]{2,1,0:T(8,128)S(1)}, f32[8,8,128]{2,1,0:T(8,128)S(1)}, u32[]{:S(2)}, u32[]{:S(2)}) collective-permute-start(f32[8,8,128]{2,1,0:T(8,128)S(1)} %get-tuple-element.12.own_right.refs_1_), channel_id=1, source_target_pairs={{0,1},{1,2},{2,3},{3,0},{4,5},{5,6},{6,7},{7,4},{8,9},{9,10},{10,1... | collective-permute-start | bytes 98312 | tf_op jit(solution)/shard_map/ppermute | solution.py:616
  11.8 16.3 %collective-permute-start = (f32[2,64,512]{2,1,0:T(8,128)S(1)}, f32[2,64,512]{2,1,0:T(8,128)S(1)}, u32[]{:S(2)}, u32[]{:S(2)}) collective-permute-start(f32[2,64,512]{2,1,0:T(8,128)S(1)} %window_0.1.refs_0_), channel_id=1, source_target_pairs={{0,16},{16,0},{1,17},{17,1},{2,18},{18,2},{3,19},{19,3},{4,20},{20... | collective-permute-start | bytes 786440 | tf_op jit(solution)/shard_map/ppermute | solution.py:595
  14.3 5.4 %collective-permute-start.5 = (f32[21,8,128]{2,1,0:T(8,128)S(1)}, f32[21,8,128]{2,1,0:T(8,128)S(1)}, u32[]{:S(2)}, u32[]{:S(2)}) collective-permute-start(f32[21,8,128]{2,1,0:T(8,128)S(1)} %get-tuple-element.13.refs_4_), channel_id=1, source_target_pairs={{4,0},{8,4},{12,8},{0,12},{5,1},{9,5},{13,9},{1,13},{6,2},{10,6},{... | collective-permute-start | bytes 258056 | tf_op jit(solution)/shard_map/ppermute | solution.py:623
  14.4 5.3 %collective-permute-start.4 = (f32[21,8,128]{2,1,0:T(8,128)S(1)}, f32[21,8,128]{2,1,0:T(8,128)S(1)}, u32[]{:S(2)}, u32[]{:S(2)}) collective-permute-start(f32[21,8,128]{2,1,0:T(8,128)S(1)} %get-tuple-element.14.refs_5_), channel_id=1, source_target_pairs={{0,4},{4,8},{8,12},{12,0},{1,5},{5,9},{9,13},{13,1},{2,6},{6,10},{... | collective-permute-start | bytes 258056 | tf_op jit(solution)/shard_map/ppermute | solution.py:622
  18.1 9.9 %copy-start = (f32[2,128,512]{2,1,0:T(8,128)S(1)}, f32[2,128,512]{2,1,0:T(8,128)}, u32[]{:S(2)}) copy-start(f32[2,128,512]{2,1,0:T(8,128)} %maps_ref.1) | copy-start | bytes 1572868
  18.2 9.9 %copy-start.1 = (f32[2,128,512]{2,1,0:T(8,128)S(1)}, f32[2,128,512]{2,1,0:T(8,128)}, u32[]{:S(2)}) copy-start(f32[2,128,512]{2,1,0:T(8,128)} %first_ref.1) | copy-start | bytes 1572868
  18.2 9.9 %copy-start.2 = (f32[2,128,512]{2,1,0:T(8,128)S(1)}, f32[2,128,512]{2,1,0:T(8,128)}, u32[]{:S(2)}) copy-start(f32[2,128,512]{2,1,0:T(8,128)} %second_ref.1) | copy-start | bytes 1572868
  18.2 9.9 %collective-permute-start.3 = (f32[2,64,512]{2,1,0:T(8,128)S(1)}, f32[2,64,512]{2,1,0:T(8,128)S(1)}, u32[]{:S(2)}, u32[]{:S(2)}) collective-permute-start(f32[2,64,512]{2,1,0:T(8,128)S(1)} %window_64.1.refs_2_), channel_id=1, source_target_pairs={{0,16},{16,0},{1,17},{17,1},{2,18},{18,2},{3,19},{19,3},{4,20},{20... | collective-permute-start | bytes 786440 | tf_op jit(solution)/shard_map/ppermute | solution.py:595
  22.8 5.3 %collective-permute-start.6 = (f32[2,8,640]{2,1,0:T(8,128)S(1)}, f32[2,8,640]{2,1,0:T(8,128)S(1)}, u32[]{:S(2)}, u32[]{:S(2)}) collective-permute-start(f32[2,8,640]{2,1,0:T(8,128)S(1)} %edges.1.refs_4_), channel_id=1, source_target_pairs={{0,16},{16,0},{1,17},{17,1},{2,18},{18,2},{3,19},{19,3},{4,20},{20... | collective-permute-start | bytes 122888 | tf_op jit(solution)/shard_map/ppermute | solution.py:595

commit v3 on v2

--- a/solution.py
+++ b/solution.py
@@ -25,7 +25,9 @@
 HALO = 4
 DENSITY, TRAIT, VARIANCE, DISPERSAL, SELECTION, OPTIMUM, LAND, OBSERVED = range(8)
 FIELDS = 8
-GROUP = 3
+RINGS = True, False
+GROUPS = {5: (5, 5, 5, 5, 5, 5), 9: (9, 9, 3, 3, 3, 9)}
+CUTS = (32, 96)
 WINDOW_US, EDGES_US = 4, 20
 VMEM_BYTES = 16 * 1024 * 1024
 SAVED = (
@@ -80,22 +82,29 @@
     return 0.5 + 0.5 * jnp.tanh(0.5 * value)
 
 
-def dynamics(slabs, group, tiles, load, steps_at, keep, put):
-    shape = (tiles, 8, LANES)
-    lane = lax.broadcasted_iota(jnp.int32, shape, 2)
+def dynamics(slabs, groups, cycles, load, steps_at, keep, put):
+    lane = lax.broadcasted_iota(jnp.int32, (sum(cycles), 8, LANES), 2)
     at_last, at_first = lane == LANES - 1, lane == 0
+
+    def turn_tiles(value, by):
+        parts, start = [], 0
+        for count in cycles:
+            cut = start + by % count
+            parts += [value[cut : start + count], value[start:cut]]
+            start += count
+        return jnp.concatenate([part for part in parts if part.shape[0]], 0)
 
     def right(value):
         turned = pltpu.roll(value, LANES - 1, 2)
-        beside = jnp.concatenate([turned[1:], turned[:1]], 0) if tiles > 1 else turned
-        return jnp.where(at_last, beside, turned)
+        return jnp.where(at_last, turn_tiles(turned, 1), turned)
 
     def left(value):
         turned = pltpu.roll(value, 1, 2)
-        beside = jnp.concatenate([turned[-1:], turned[:-1]], 0) if tiles > 1 else turned
-        return jnp.where(at_first, beside, turned)
-
-    def each_slab(body, carry=()):
+        return jnp.where(at_first, turn_tiles(turned, -1), turned)
+
+    def each_slab(stage, body, carry=()):
+        group = groups[stage]
+
         def step(index, carry):
             for offset in range(group):
                 carry = body(index * group + offset, carry)
@@ -143,7 +152,7 @@
         keep["m0"][k] = n * (v + z * z)
         return ()
 
-    each_slab(begin)
+    each_slab(0, begin)
     close(("half", "land", "n0", "q0", "m0"))
 
     def weigh(k, _):
@@ -154,7 +163,7 @@
         keep["wr"][k] = (half + right(half)) * pair
         return ()
 
-    each_slab(weigh)
+    each_slab(1, weigh)
     first_names, second_names = ("n0", "q0", "m0"), ("n1", "q1", "m1")
 
     def first_step(k, above):
@@ -179,7 +188,7 @@
             keep[name][k] = value
         return above
 
-    each_slab(first_step, wrapped(row_fluxes(first_names, slabs - 1)[1]))
+    each_slab(2, first_step, wrapped(row_fluxes(first_names, slabs - 1)[1]))
     close(second_names)
 
     def second_step(k, above):
@@ -207,7 +216,7 @@
         keep["a2m"][k] = am
         return above
 
-    each_slab(second_step, wrapped(row_fluxes(second_names, slabs - 1)[1]))
+    each_slab(3, second_step, wrapped(row_fluxes(second_names, slabs - 1)[1]))
     second_back, first_back = ("a2n", "a2q", "a2m"), ("a1n", "a1q", "a1m")
     close(second_back)
 
@@ -235,7 +244,7 @@
         put(1, k, gsel * sigmoid(load(SELECTION, k)))
         return above
 
-    each_slab(back, wrapped(row_fluxes(second_back, slabs - 1)[1]))
+    each_slab(4, back, wrapped(row_fluxes(second_back, slabs - 1)[1]))
     close(first_back)
 
     def row_share(k):
@@ -253,40 +262,35 @@
         put(0, k, half * (10.0 * half - 1.0) * (here + above[0] + total + left(total)))
         return (here,)
 
-    each_slab(finish, wrapped((row_share(slabs - 1),)))
+    each_slab(5, finish, wrapped((row_share(slabs - 1),)))
 
 
 def step_rows(line):
     return jnp.transpose(jnp.concatenate([line] * (LANES // 8), 0))
 
 
-def fill_kernel(tiles, sources, step_ref, fields, steps, codes, sems):
+def tile_copies(tiles, first, rows, sources, fields, codes, sems):
     density, trait, variance, optimum, observed, land_code, maps = sources
+    moves = (
+        (maps, fields.at[DISPERSAL : SELECTION + 1]),
+        (land_code, codes),
+        (density.at[0], fields.at[DENSITY]),
+        (trait.at[0], fields.at[TRAIT]),
+        (variance.at[0], fields.at[VARIANCE]),
+        (optimum.at[0], fields.at[OPTIMUM]),
+        (observed.at[0], fields.at[OBSERVED]),
+    )
+    part = pl.ds(first, rows)
     copies = []
-    for field, (source, target) in enumerate(
-        (
-            (density.at[0], fields.at[DENSITY]),
-            (trait.at[0], fields.at[TRAIT]),
-            (variance.at[0], fields.at[VARIANCE]),
-            (maps.at[0], fields.at[DISPERSAL]),
-            (maps.at[1], fields.at[SELECTION]),
-            (optimum.at[0], fields.at[OPTIMUM]),
-            (land_code, codes),
-            (observed.at[0], fields.at[OBSERVED]),
-        )
-    ):
+    for index, (source, target) in enumerate(moves):
         for t in range(tiles):
-            copies.append(
-                pltpu.make_async_copy(source.at[:, pl.ds(t * LANES, LANES)], target.at[t], sems.at[field, t])
-            )
-    for copy in copies:
-        copy.start()
-    line = jnp.broadcast_to(step_ref[0:1, :].astype(F32), (8, LANES))
-    steps[0] = step_rows(line)
-    steps[1] = jnp.broadcast_to(line[0:1], (LANES, LANES))
-    for copy in copies:
-        copy.wait()
-    fields[LAND] = codes[...].astype(F32)
+            lanes = pl.ds(t * LANES, LANES)
+            if source is maps:
+                ends = source.at[:, part, lanes], target.at[:, t, part]
+            else:
+                ends = source.at[part, lanes], target.at[t, part]
+            copies.append(pltpu.make_async_copy(*ends, sems.at[index, t]))
+    return copies
 
 
 def window_kernel(first, rows, skip, fields, steps, *refs):
@@ -307,39 +311,61 @@
             grads[which, t, pl.ds(k, 8, stride=slabs), :] = value[t]
 
     keep = {name: kept.at[index] for index, name in enumerate(SAVED)}
-    dynamics(slabs, GROUP, tiles, load, steps_at, keep, put)
+    dynamics(slabs, GROUPS[slabs], (tiles,), load, steps_at, keep, put)
     for which in range(2):
         for t in range(tiles):
             out_ref[which, :, t * LANES : (t + 1) * LANES] = grads[which, t, skip : skip + out_rows, :]
 
 
-def load_kernel(tiles, *refs):
-    sources, step_ref, fields, steps, left_ref, right_ref, codes, sems = refs[:7], *refs[7:]
-    fill_kernel(tiles, sources, step_ref, fields, steps, codes, sems)
-    columns_kernel(fields, left_ref, right_ref)
-
-
-def load_tile(sources, obs_step):
+def first_kernel(tiles, rows, *refs):
+    sources, step_ref = refs[:7], refs[7]
+    out_ref, fields, steps, pair_ref, other_ref, codes, line, grads, kept, sems, late_sems = refs[8:]
+    height = fields.shape[2]
+    early = tile_copies(tiles, 0, rows, sources, fields, codes, sems)
+    late = tile_copies(tiles, rows, height - rows, sources, fields, codes, late_sems)
+    early.append(pltpu.make_async_copy(step_ref, line, sems.at[7, 0]))
+    for copy in early + late:
+        copy.start()
+    for copy in early:
+        copy.wait()
+    fields[LAND, :, :rows] = codes[:, :rows].astype(F32)
+    wide = jnp.broadcast_to(line[0:1, :].astype(F32), (8, LANES))
+    steps[0] = step_rows(wide)
+    steps[1] = jnp.broadcast_to(wide[0:1], (LANES, LANES))
+    window_kernel(0, rows, 0, fields, steps, out_ref, grads, kept)
+    for copy in late:
+        copy.wait()
+    fields[LAND, :, rows:] = codes[:, rows:].astype(F32)
+    columns_kernel(fields, pair_ref, other_ref)
+
+
+def first_window(rows, out_rows, sources, obs_step):
     height, columns = sources[0].shape[1:]
     tiles = columns // LANES
     strip = jax.ShapeDtypeStruct((FIELDS, EDGE, height), F32)
     return pl.pallas_call(
-        functools.partial(load_kernel, tiles),
+        functools.partial(first_kernel, tiles, rows),
         out_shape=[
+            jax.ShapeDtypeStruct((2, out_rows, columns), F32),
             jax.ShapeDtypeStruct((FIELDS, tiles, height, LANES), F32),
             jax.ShapeDtypeStruct((2, LANES, LANES), F32),
             strip,
             strip,
         ],
-        in_specs=[pl.BlockSpec(memory_space=pltpu.HBM)] * 7 + [pl.BlockSpec(memory_space=pltpu.VMEM)],
-        out_specs=[pl.BlockSpec(memory_space=pltpu.VMEM)] * 4,
+        in_specs=[pl.BlockSpec(memory_space=pltpu.HBM)] * 8,
+        out_specs=[pl.BlockSpec(memory_space=pltpu.VMEM)] * 5,
         scratch_shapes=[
             pltpu.VMEM((tiles, height, LANES), jnp.int32),
-            pltpu.SemaphoreType.DMA((FIELDS, tiles)),
+            pltpu.VMEM(obs_step.shape, jnp.int32),
+            pltpu.VMEM((2, tiles, rows, LANES), F32),
+            pltpu.VMEM((len(SAVED), rows // 8 + 1, tiles, 8, LANES), F32),
+            pltpu.SemaphoreType.DMA((8, tiles)),
+            pltpu.SemaphoreType.DMA((7, tiles)),
         ],
+        cost_estimate=cost(WINDOW_US),
         compiler_params=pltpu.CompilerParams(vmem_limit_bytes=VMEM_BYTES),
-        name="load_tile",
-    )(*(pltpu.with_memory_space_constraint(source, pltpu.HBM) for source in sources), obs_step)
+        name="first_window",
+    )(*(pltpu.with_memory_space_constraint(source, pltpu.HBM) for source in (*sources, obs_step)))
 
 
 def window(first, rows, out_first, out_rows, fields, steps, *after):
@@ -359,7 +385,8 @@
     )(fields, steps, *after)
 
 
-def columns_kernel(fields, left_ref, right_ref):
+def columns_kernel(fields, pair_ref, other_ref):
+    rightward = is_even("ly")
     tiles, rows = fields.shape[1:3]
     lane = lax.broadcasted_iota(jnp.int32, (rows, LANES), 1)
     packed = jnp.zeros((rows, LANES), F32)
@@ -370,12 +397,14 @@
         packed = jnp.where(place < 2 * EDGE, turned, packed)
     flipped = jnp.transpose(packed)
     for field in range(FIELDS):
-        left_ref[field] = flipped[16 * field : 16 * field + EDGE]
+        left = flipped[16 * field : 16 * field + EDGE]
         start = (16 * field - EDGE) % LANES
-        right_ref[field] = flipped[start : start + EDGE]
-
-
-def in_vmem(kernel, name, out_shape, scratch=()):
+        right = flipped[start : start + EDGE]
+        pair_ref[field] = jnp.where(rightward, right, left)
+        other_ref[field] = jnp.where(rightward, left, right)
+
+
+def in_vmem(kernel, name, out_shape):
     def call(*operands):
         many = isinstance(out_shape, (list, tuple))
         space = pl.BlockSpec(memory_space=pltpu.VMEM)
@@ -384,7 +413,6 @@
             out_shape=out_shape,
             in_specs=[space] * len(operands),
             out_specs=[space] * len(out_shape) if many else space,
-            scratch_shapes=list(scratch),
             compiler_params=pltpu.CompilerParams(vmem_limit_bytes=VMEM_BYTES),
             name=name,
         )(*operands)
@@ -392,140 +420,151 @@
     return call
 
 
-def rows_kernel(fields, steps, own_left, own_right, from_left, from_right, up_ref, down_ref):
+def is_even(axis):
+    return lax.axis_index(axis) % 2 == 0
+
+
+def present(axis):
+    place = lax.axis_index(axis)
+    return (place > 0).astype(F32), (place < lax.axis_size(axis) - 1).astype(F32)
+
+
+def chosen(which, one, other):
+    return lambda index: jnp.where(which, one[index], other[index])
+
+
+def rows_kernel(fields, steps, from_pair, from_other, pair_ref, other_ref):
     tiles = fields.shape[1]
+    downward, rightward = is_even("lx"), is_even("ly")
     sub = lax.broadcasted_iota(jnp.int32, (8, LANES), 0)
     for pair in range(FIELDS // 2):
         for t in range(tiles):
             even, odd = fields.at[2 * pair, t], fields.at[2 * pair + 1, t]
-            up_ref[pair * tiles + t] = jnp.where(sub < HALO, even[:EDGE], pltpu.roll(odd[:EDGE], HALO, 0))
-            down_ref[pair * tiles + t] = jnp.where(sub < HALO, pltpu.roll(odd[-EDGE:], HALO, 0), even[-EDGE:])
+            up = jnp.where(sub < HALO, even[:EDGE], pltpu.roll(odd[:EDGE], HALO, 0))
+            down = jnp.where(sub < HALO, pltpu.roll(odd[-EDGE:], HALO, 0), even[-EDGE:])
+            pair_ref[pair * tiles + t] = jnp.where(downward, down, up)
+            other_ref[pair * tiles + t] = jnp.where(downward, up, down)
     lane = lax.broadcasted_iota(jnp.int32, (8, LANES), 1)
     base = FIELDS // 2 * tiles
-    for index, strip in enumerate((from_left, own_left, own_right, from_right)):
+    strips = chosen(rightward, from_other, from_pair), chosen(rightward, from_pair, from_other)
+    for index, strip in enumerate(strips):
         packed = jnp.zeros((8, LANES), F32)
         for field in range(FIELDS):
-            turned = pltpu.roll(strip[field], 8 * field, 1) if field else strip[field]
+            turned = pltpu.roll(strip(field), 8 * field, 1) if field else strip(field)
             place = (lane - 8 * field + HALO) % LANES
             packed = jnp.where(place < 2 * HALO, turned, packed)
-        up_ref[base + index] = packed
-        down_ref[base + index] = packed
-    up_ref[base + 4] = steps[1, :8]
-    down_ref[base + 4] = steps[1, :8]
-
-
-def pack_rows(fields, steps, strips):
-    shape = jax.ShapeDtypeStruct((FIELDS // 2 * fields.shape[1] + 5, 8, LANES), F32)
-    return in_vmem(rows_kernel, "pack_rows", [shape, shape])(fields, steps, *strips)
-
-
-def edges_kernel(place_ref, fields, steps, *refs):
-    own_left, own_right, from_left, from_right, from_above, from_below, out_ref = refs[:7]
-    row_strip, col_strip, row_step, row_grad, col_grad, row_keep, col_keep = refs[7:]
+        pair_ref[base + index] = packed
+        other_ref[base + index] = packed
+    pair_ref[base + 2] = steps[1, :8]
+    other_ref[base + 2] = steps[1, :8]
+
+
+def pack_rows(*operands):
+    fields = operands[0]
+    shape = jax.ShapeDtypeStruct((FIELDS // 2 * fields.shape[1] + 3, 8, LANES), F32)
+    return in_vmem(rows_kernel, "pack_rows", [shape, shape])(*operands)
+
+
+def outer_rows(grad, which, t):
+    sub = lax.broadcasted_iota(jnp.int32, (8, LANES), 0)
+    return jnp.where(sub < HALO, grad[which, t, 8:16, :], grad[which, t, 16:24, :])
+
+
+def edges_kernel(fields, steps, own_pair, own_other, side_pair, side_other, end_pair, end_other, *refs):
+    out_ref, strip, grad, kept, row_step = refs
     tiles = fields.shape[1]
     base = FIELDS // 2 * tiles
-    has_above, has_below, has_left, has_right = (place_ref[i] for i in range(4))
+    (has_above, has_below), (has_left, has_right) = present("lx"), present("ly")
+    downward, rightward = is_even("lx"), is_even("ly")
+    own_left, own_right = chosen(rightward, own_other, own_pair), chosen(rightward, own_pair, own_other)
+    from_left, from_right = chosen(rightward, side_other, side_pair), chosen(rightward, side_pair, side_other)
+    from_above, from_below = chosen(downward, end_other, end_pair), chosen(downward, end_pair, end_other)
     lane = lax.broadcasted_iota(jnp.int32, (8, LANES), 1)
     sub = lax.broadcasted_iota(jnp.int32, (8, LANES), 0)
-
-    corners = [
-        jnp.where((lane % 8) < HALO, from_below[base + index], from_above[base + index]) for index in range(4)
-    ]
-    beside = [[None] * 4 for _ in range(FIELDS)]
-    for field in range(FIELDS):
-        for index, strip in enumerate((from_left, own_left, own_right, from_right)):
-            value = strip[field]
-            outer = pltpu.roll(corners[index], (LANES - 8 * field) % LANES, 1) if field else corners[index]
-            if field == LAND:
-                outer = outer * jnp.where(lane < LANES // 2, has_below, has_above)
-                if index == 0:
-                    value, outer = value * has_left, outer * has_left
-                if index == 3:
-                    value, outer = value * has_right, outer * has_right
-            col_strip[field, 0, 8 * index : 8 * index + 8, :] = value
-            col_strip[field, 1, 8 * index : 8 * index + 8, :] = outer
-            beside[field][index] = (value, outer)
+    within = jnp.where(lane < LANES // 2, has_below, has_above)
 
     def lined(value, outer):
         out = jnp.where(lane < 8, pltpu.roll(outer, 8, 1), pltpu.roll(value, 8, 1))
         out = jnp.where(lane < 16, out, pltpu.roll(value, 24, 1))
         return jnp.where(lane < 24, out, pltpu.roll(outer, 24, 1))
 
+    def beside(side, index, present):
+        corners = jnp.where((lane % 8) < HALO, from_below(base + index), from_above(base + index))
+        out = []
+        for field in range(FIELDS):
+            value = side(field)
+            outer = pltpu.roll(corners, (LANES - 8 * field) % LANES, 1) if field else corners
+            if field == LAND:
+                value, outer = value * present, outer * (within * present)
+            out.append(lined(value, outer))
+        return out
+
+    lefts, rights = beside(from_left, 0, has_left), beside(from_right, 1, has_right)
     zeros = jnp.zeros((8, LANES), F32)
     stack = []
     for index in range(LANES // 8):
-        here = lined(*beside[index][3]) if index < FIELDS else zeros
         following = (index + 1) % (LANES // 8)
-        after = lined(*beside[following][0]) if following < FIELDS else zeros
+        here = rights[index] if index < FIELDS else zeros
+        after = lefts[following] if following < FIELDS else zeros
         stack.append(jnp.where(sub < HALO, here, after))
     flipped = jnp.transpose(jnp.concatenate(stack, 0))[:32]
-    own_step = steps[1, :8]
-    outer_step = jnp.where(lane < LANES // 2, from_below[base + 4], from_above[base + 4])
-    row_step[...] = step_rows(lined(own_step, outer_step))[:32]
+    outer_step = jnp.where(lane < LANES // 2, from_below(base + 2), from_above(base + 2))
+    row_step[...] = step_rows(lined(steps[1, :8], outer_step))[:32]
     for field in range(FIELDS):
         for t in range(tiles):
-            above, below = from_above[field // 2 * tiles + t], from_below[field // 2 * tiles + t]
+            above, below = from_above(field // 2 * tiles + t), from_below(field // 2 * tiles + t)
             if field % 2:
                 above, below = pltpu.roll(above, HALO, 0), pltpu.roll(below, HALO, 0)
             if field == LAND:
                 above, below = above * has_above, below * has_below
             own = fields.at[field, t]
             for index, value in enumerate((above, own[:EDGE], own[-EDGE:], below)):
-                row_strip[field, t, 8 * index : 8 * index + 8, :] = value
-        row_strip[field, tiles] = pltpu.roll(flipped, (LANES - 8 * field) % LANES, 1) if field else flipped
+                strip[field, t, 8 * index : 8 * index + 8, :] = value
+        strip[field, tiles] = pltpu.roll(flipped, (LANES - 8 * field) % LANES, 1) if field else flipped
+        left, right = from_left(field), from_right(field)
+        if field == LAND:
+            left, right = left * has_left, right * has_right
+        for index, value in enumerate((left, own_left(field), own_right(field), right)):
+            strip[field, tiles + 1, 8 * index : 8 * index + 8, :] = value
 
     slabs = 3
-    for strip, grad, kept, count in (
-        (row_strip, row_grad, row_keep, tiles + 1),
-        (col_strip, col_grad, col_keep, 2),
-    ):
-        on_rows = strip is row_strip
-
-        def load(field, k):
-            parts = [strip[field, t, pl.ds(HALO + k, 8, stride=slabs), :] for t in range(count)]
-            return jnp.stack(parts)
-
-        def steps_at(k):
-            if on_rows:
-                part = row_step[pl.ds(HALO + k, 8, stride=slabs), :]
-                return jnp.broadcast_to(part[None], (count, 8, LANES))
-            return jnp.stack([own_step, outer_step])
-
-        def put(which, k, value):
-            for t in range(count):
-                grad[which, t, pl.ds(HALO + k, 8, stride=slabs), :] = value[t]
-
-        keep = {name: kept.at[index] for index, name in enumerate(SAVED)}
-        dynamics(slabs, slabs, count, load, steps_at, keep, put)
+    count = tiles + 2
+
+    def load(field, k):
+        return jnp.stack([strip[field, t, pl.ds(HALO + k, 8, stride=slabs), :] for t in range(count)])
+
+    def steps_at(k):
+        part = row_step[pl.ds(HALO + k, 8, stride=slabs), :]
+        return jnp.stack([part] * (tiles + 1) + [steps[1, :8]])
+
+    def put(which, k, value):
+        for t in range(count):
+            grad[which, t, pl.ds(HALO + k, 8, stride=slabs), :] = value[t]
+
+    keep = {name: kept.at[index] for index, name in enumerate(SAVED)}
+    dynamics(slabs, (slabs,) * 6, (tiles + 1, 1), load, steps_at, keep, put)
     for which in range(2):
         for t in range(tiles):
-            out_ref[which, :, t * LANES : (t + 1) * LANES] = jnp.where(
-                sub < HALO, row_grad[which, t, 8:16, :], row_grad[which, t, 16:24, :]
-            )
-        out_ref[which, :, tiles * LANES :] = jnp.where(
-            sub < HALO, col_grad[which, 0, 8:16, :], col_grad[which, 0, 16:24, :]
-        )
-
-
-def edges(place, fields, steps, strips, from_above, from_below):
+            out_ref[which, :, t * LANES : (t + 1) * LANES] = outer_rows(grad, which, t)
+        out_ref[which, :, tiles * LANES :] = outer_rows(grad, which, tiles + 1)
+
+
+def edges(fields, steps, *strips):
     tiles = fields.shape[1]
-    scratch = [
-        pltpu.VMEM((FIELDS, tiles + 1, 32, LANES), F32),
-        pltpu.VMEM((FIELDS, 2, 32, LANES), F32),
-        pltpu.VMEM((32, LANES), F32),
-        pltpu.VMEM((2, tiles + 1, 32, LANES), F32),
-        pltpu.VMEM((2, 2, 32, LANES), F32),
-        pltpu.VMEM((len(SAVED), 4, tiles + 1, 8, LANES), F32),
-        pltpu.VMEM((len(SAVED), 4, 2, 8, LANES), F32),
-    ]
-    operands = [place, fields, steps, *strips, from_above, from_below]
+    count = tiles + 2
     space = pl.BlockSpec(memory_space=pltpu.VMEM)
+    operands = [fields, steps, *strips]
     return pl.pallas_call(
         edges_kernel,
         out_shape=jax.ShapeDtypeStruct((2, EDGE, (tiles + 1) * LANES), F32),
-        in_specs=[pl.BlockSpec(memory_space=pltpu.SMEM)] + [space] * (len(operands) - 1),
+        in_specs=[space] * len(operands),
         out_specs=space,
-        scratch_shapes=scratch,
+        scratch_shapes=[
+            pltpu.VMEM((FIELDS, count, 32, LANES), F32),
+            pltpu.VMEM((2, count, 32, LANES), F32),
+            pltpu.VMEM((len(SAVED), 4, count, 8, LANES), F32),
+            pltpu.VMEM((32, LANES), F32),
+        ],
         cost_estimate=cost(EDGES_US),
         compiler_params=pltpu.CompilerParams(vmem_limit_bytes=VMEM_BYTES),
         name="edges",
@@ -543,7 +582,6 @@
     strips = [edge[which, :, columns:] for which in range(2)]
     blank = jnp.zeros((LANES - 2 * EDGE, LANES), F32)
     flipped = jnp.transpose(jnp.concatenate([*strips, blank], 0))
-    height = rows // parts
     for which in range(2):
         for t in range(tiles):
             own = slice(t * LANES, (t + 1) * LANES)
@@ -551,6 +589,12 @@
                 [sum(ref[which, :, own] for ref in grads[part * terms : (part + 1) * terms]) for part in range(parts)],
                 0,
             )
+            if t == 0:
+                beside = pltpu.roll(flipped, LANES - EDGE * which, 1) if which else flipped
+                grad = jnp.where(lane < HALO, beside, grad)
+            if t == tiles - 1:
+                beside = pltpu.roll(flipped, LANES - EDGE * (which + 1), 1)
+                grad = jnp.where(lane >= LANES - HALO, beside, grad)
             outer = edge[which, :, own]
             grad = jnp.concatenate(
                 [
@@ -560,12 +604,6 @@
                 ],
                 0,
             )
-            if t == 0:
-                beside = pltpu.roll(flipped, LANES - EDGE * which, 1) if which else flipped
-                grad = jnp.where(lane < HALO, beside, grad)
-            if t == tiles - 1:
-                beside = pltpu.roll(flipped, LANES - EDGE * (which + 1), 1)
-                grad = jnp.where(lane >= LANES - HALO, beside, grad)
             first = BETA_FIRST * first_ref[which, :, own] + (1.0 - BETA_FIRST) * grad
             second = BETA_SECOND * second_ref[which, :, own] + (1.0 - BETA_SECOND) * grad * grad
             new_first[which, :, own] = first
@@ -583,10 +621,17 @@
     return in_vmem(kernel, "update", [shape] * 3)(maps, first_moment, second_moment, *flat, *edge_grads)
 
 
-def shifts(axis):
+def pairings(axis, ring):
     count = lax.axis_size(axis)
-    forward = [(i, (i + 1) % count) for i in range(count)]
-    return forward, [(target, source) for source, target in forward]
+    first = [(i, i + 1) for i in range(0, count - 1, 2)]
+    second = [(i, i + 1) for i in range(1, count - 1, 2)]
+    if ring and count % 2 == 0 and count > 2:
+        second.append((0, count - 1))
+    return [swaps + [(target, source) for source, target in swaps] for swaps in (first, second)]
+
+
+def swapped(arrays, axis, ring):
+    return [lax.ppermute(array, axis, swaps) for array, swaps in zip(arrays, pairings(axis, ring))]
 
 
 def both_scenarios(value):
@@ -610,26 +655,20 @@
 ):
     sources = (density, trait, variance, optimum, observed, land_code, maps)
     rows = maps.shape[1]
-    middle = rows // 2
-    fields, steps, own_left, own_right = load_tile(sources, obs_step)
-    rightward, leftward = shifts("ly")
-    from_left = lax.ppermute(own_right, "ly", rightward)
-    from_right = lax.ppermute(own_left, "ly", leftward)
-    upper_terms = both_scenarios(window(0, middle + EDGE, 0, middle, fields, steps))
-    strips = (own_left, own_right, from_left, from_right)
-    up, down = pack_rows(fields, steps, strips)
-    downward, upward = shifts("lx")
-    from_above = lax.ppermute(down, "lx", downward)
-    from_below = lax.ppermute(up, "lx", upward)
-    lower = window(middle - EDGE, middle + EDGE, middle, middle, fields, steps, *strips, up, down)
+    upper, fields, steps, *own_sides = first_window(CUTS[0] + EDGE, CUTS[0], sources, obs_step)
+    upper_terms = both_scenarios(upper)
+    sides = swapped(own_sides, "ly", RINGS[1])
+    middle = window(CUTS[0] - HALO, CUTS[1] - CUTS[0] + EDGE, CUTS[0], CUTS[1] - CUTS[0], fields, steps, *own_sides)
+    middle_terms = both_scenarios(middle)
+    own_ends = pack_rows(fields, steps, *sides)
+    ends = swapped(own_ends, "lx", RINGS[0])
+    last = rows - CUTS[1]
+    after = *own_sides, *sides, *own_ends, upper_terms[-1]
+    lower = window(CUTS[1] - EDGE, last + EDGE, CUTS[1], last, fields, steps, *after)
     lower_terms = both_scenarios(lower)
-    row, column = lax.axis_index("lx"), lax.axis_index("ly")
-    place = jnp.stack(
-        [row > 0, row < lax.axis_size("lx") - 1, column > 0, column < lax.axis_size("ly") - 1]
-    ).astype(F32)
-    outer = edges(place, fields, steps, strips, from_above, from_below)
+    outer = edges(fields, steps, *own_sides, *sides, *ends)
     outer_terms = both_scenarios(outer)
-    return tuple(update(maps, first_moment, second_moment, [upper_terms, lower_terms], outer_terms))
+    return tuple(update(maps, first_moment, second_moment, [upper_terms, middle_terms, lower_terms], outer_terms))
 
 
 def solution(mesh):

time: 29.8 us -> 26.7 us (0.90)
  the two profiles are of different devices: /device:TPU:0 before, /device:TPU:8 now
where the time goes in v3:
time: 26.7 us; the launch traced here: 26.6 us
  starting transfers between devices  11.5 us (43%)
  Pallas kernels  11.2 us (42%)
  waiting for transfers between devices  3.08 us (12%)
  between operations  0.73 us (3%)
    ppermute x4, starting transfers between devices, swapped(): lax.ppermute(array, axis, swaps)  6.81 us
    ppermute x4, starting transfers between devices, both_scenarios(): return [value, lax.ppermute(value, 'scen', [(0, 1), (1, 0)])]  4.71 us
    pallas_call x2, Pallas kernels, window(): pl.pallas_call(functools.partial(window_kernel, first, rows, out_first -...  4.17 us
    pallas_call x1, Pallas kernels, first_window(): pl.pallas_call(functools.partial(first_kernel, tiles, rows), out_shape=[j...  3.58 us
    ppermute x4, waiting for transfers between devices, both_scenarios(): return [value, lax.ppermute(value, 'scen', [(0, 1), (1, 0)])]  3.07 us
    pallas_call x1, Pallas kernels, edges(): pl.pallas_call(edges_kernel, out_shape=jax.ShapeDtypeStruct((2, EDGE, (ti...  1.83 us
    pallas_call x2, Pallas kernels, call(): pl.pallas_call(kernel, out_shape=out_shape, in_specs=[space] * len(operan...  1.62 us
  transfers between devices with their start and end apart: 8, of which 1 were waited for; matrix products, arithmetic and copies ran while one was open for 0% of the time, Pallas kernels for 23%

profile of v3, /device:TPU:8, one launch (start us, length us, event | category | flops | bytes accessed | tf_op | source)
XLA Modules:
  0.0 26.6 jit_solution(3033883422223814237)
XLA Ops:
  0.6 3.6 %first_window.1 = (f32[2,32,512]{2,1,0:T(8,128)S(1)}, f32[8,4,128,128]{3,2,1,0:T(8,128)S(1)}, f32[2,128,128]{2,1,0:T(8,128)S(1)}, f32[8,8,128]{2,1,0:T(8,128)S(1)}, f32[8,8,128]{2,1,0:T(8,128)S(1)}) custom-call(f32[1,128,512]{2,1,0:T(8,128)} %refs_0_.1, f32[1,128,512]{2,1,0:T(8,128)} %refs_1_.1, f32[1,128,512]{2,1,0:T(8,128)} %refs_2_.1, ...), custom_call_target="tpu_custom_call" | custom-call | flops 4000000000 | bytes 14400000 | tf_op jit(solution)/shard_map/first_window/pallas_call | solution.py:346
  4.2 0.1 collective-permute-start.2
  4.3 5.0 %collective-permute-start.3 = (f32[8,8,128]{2,1,0:T(8,128)S(1)}, f32[8,8,128]{2,1,0:T(8,128)S(1)}, u32[]{:S(2)}, u32[]{:S(2)}) collective-permute-start(f32[8,8,128]{2,1,0:T(8,128)S(1)} %get-tuple-element.14.refs_1_.own_other), channel_id=1, source_target_pairs={{1,2},{2,1},{5,6},{6,5},{9,10},{10,9},{13,14},{14,13},{17,18},{18,... | collective-permute-start | bytes 98312 | tf_op jit(solution)/shard_map/ppermute | solution.py:634
  9.3 1.6 %collective-permute-start = (f32[2,32,512]{2,1,0:T(8,128)S(1)}, f32[2,32,512]{2,1,0:T(8,128)S(1)}, u32[]{:S(2)}, u32[]{:S(2)}) collective-permute-start(f32[2,32,512]{2,1,0:T(8,128)S(1)} %get-tuple-element.10.refs_0_), channel_id=1, source_target_pairs={{0,16},{16,0},{1,17},{17,1},{2,18},{18,2},{3,19},{19,3},{4,20},{20... | collective-permute-start | bytes 393224 | tf_op jit(solution)/shard_map/ppermute | solution.py:640
  10.9 2.7 %window_32.1.refs_2_ = f32[2,64,512]{2,1,0:T(8,128)S(1)} custom-call(f32[8,4,128,128]{3,2,1,0:T(8,128)S(1)} %get-tuple-element.11.fields, f32[2,128,128]{2,1,0:T(8,128)S(1)} %get-tuple-element.12.steps, f32[8,8,128]{2,1,0:T(8,128)S(1)} %get-tuple-element.13.refs_0_.own_pair, f32[8,8,128]{2,1,0:T(8,128)S(1)} %get-tuple-element.14.refs_1_.own_other), custom_call_target="tpu_custom_call" | custom-call | flops 4000000000 | bytes 14400000 | tf_op jit(solution)/shard_map/window_32/pallas_call | solution.py:373
  13.6 0.6 %collective-permute-start.1 = (f32[2,64,512]{2,1,0:T(8,128)S(1)}, f32[2,64,512]{2,1,0:T(8,128)S(1)}, u32[]{:S(2)}, u32[]{:S(2)}) collective-permute-start(f32[2,64,512]{2,1,0:T(8,128)S(1)} %window_32.1.refs_2_), channel_id=1, source_target_pairs={{0,16},{16,0},{1,17},{17,1},{2,18},{18,2},{3,19},{19,3},{4,20},{20... | collective-permute-start | bytes 786440 | tf_op jit(solution)/shard_map/ppermute | solution.py:640
  14.2 0.0 collective-permute-done.2.from_pair.refs_2_.side_pair
  14.2 0.0 collective-permute-done.3.from_other.refs_3_.side_other
  14.2 0.1 pack_rows.1
  14.3 0.1 collective-permute-start.5
  14.4 1.6 %collective-permute-start.6 = (f32[19,8,128]{2,1,0:T(8,128)S(1)}, f32[19,8,128]{2,1,0:T(8,128)S(1)}, u32[]{:S(2)}, u32[]{:S(2)}) collective-permute-start(f32[19,8,128]{2,1,0:T(8,128)S(1)} %get-tuple-element.16.refs_5_), channel_id=1, source_target_pairs={{4,8},{0,12},{8,4},{12,0},{5,9},{1,13},{9,5},{13,1},{6,10},{2,14},... | collective-permute-start | bytes 233480 | tf_op jit(solution)/shard_map/ppermute | solution.py:634
  16.0 0.0 collective-permute-done.refs_6_.refs_1_
  16.0 1.5 %window_96.1.refs_4_ = f32[2,32,512]{2,1,0:T(8,128)S(1)} custom-call(f32[8,4,128,128]{3,2,1,0:T(8,128)S(1)} %get-tuple-element.11.fields, f32[2,128,128]{2,1,0:T(8,128)S(1)} %get-tuple-element.12.steps, f32[8,8,128]{2,1,0:T(8,128)S(1)} %get-tuple-element.13.refs_0_.own_pair, f32[8,8,128]{2,1,0:T(8,128)S(1)} %get-tuple-element.14.refs_1_.own_other, ...), custom_call_target="tpu_custom_call" | custom-call | flops 4000000000 | bytes 14400000 | tf_op jit(solution)/shard_map/window_96/pallas_call | solution.py:373
  17.5 0.0 copy-start
  17.5 0.0 copy-start.1
  17.5 0.0 copy-start.2
  17.5 1.6 %collective-permute-start.4 = (f32[2,32,512]{2,1,0:T(8,128)S(1)}, f32[2,32,512]{2,1,0:T(8,128)S(1)}, u32[]{:S(2)}, u32[]{:S(2)}) collective-permute-start(f32[2,32,512]{2,1,0:T(8,128)S(1)} %window_96.1.refs_4_), channel_id=1, source_target_pairs={{0,16},{16,0},{1,17},{17,1},{2,18},{18,2},{3,19},{19,3},{4,20},{20... | collective-permute-start | bytes 393224 | tf_op jit(solution)/shard_map/ppermute | solution.py:640
  19.1 0.0 collective-permute-done.5.end_pair
  19.1 0.0 collective-permute-done.6.end_other
  19.1 1.8 %edges.1.refs_6_ = f32[2,8,640]{2,1,0:T(8,128)S(1)} custom-call(f32[8,4,128,128]{3,2,1,0:T(8,128)S(1)} %get-tuple-element.11.fields, f32[2,128,128]{2,1,0:T(8,128)S(1)} %get-tuple-element.12.steps, f32[8,8,128]{2,1,0:T(8,128)S(1)} %get-tuple-element.13.refs_0_.own_pair, f32[8,8,128]{2,1,0:T(8,128)S(1)} %get-tuple-element.14.refs_1_.own_other, ...), custom_call_target="tpu_custom_call" | custom-call | flops 20000000000 | bytes 72000000 | tf_op jit(solution)/shard_map/edges/pallas_call | solution.py:557
  20.9 1.0 %collective-permute-start.7 = (f32[2,8,640]{2,1,0:T(8,128)S(1)}, f32[2,8,640]{2,1,0:T(8,128)S(1)}, u32[]{:S(2)}, u32[]{:S(2)}) collective-permute-start(f32[2,8,640]{2,1,0:T(8,128)S(1)} %edges.1.refs_6_), channel_id=1, source_target_pairs={{0,16},{16,0},{1,17},{17,1},{2,18},{18,2},{3,19},{19,3},{4,20},{20... | collective-permute-start | bytes 122888 | tf_op jit(solution)/shard_map/ppermute | solution.py:640
  21.9 3.1 %collective-permute-done.7.refs_7_ = f32[2,8,640]{2,1,0:T(8,128)S(1)} collective-permute-done((f32[2,8,640]{2,1,0:T(8,128)S(1)}, f32[2,8,640]{2,1,0:T(8,128)S(1)}, u32[]{:S(2)}, u32[]{:S(2)}) %collective-permute-start.7) | collective-permute-done | bytes 40992 | tf_op jit(solution)/shard_map/ppermute | solution.py:640
  25.0 0.0 collective-permute-done.4.refs_5_
  25.0 0.0 collective-permute-done.1.refs_3_
  25.0 0.0 copy-done
  25.0 0.0 copy-done.1
  25.0 0.0 copy-done.2
  25.0 1.5 %update.1 = (f32[2,128,512]{2,1,0:T(8,128)}, f32[2,128,512]{2,1,0:T(8,128)}, f32[2,128,512]{2,1,0:T(8,128)}) custom-call(f32[2,128,512]{2,1,0:T(8,128)S(1)} %copy-done, f32[2,128,512]{2,1,0:T(8,128)S(1)} %copy-done.1, f32[2,128,512]{2,1,0:T(8,128)S(1)} %copy-done.2, f32[2,32,512]{2,1,0:T(8,128)S(1)} %get-tuple-element.10.refs_0_, ...), custom_call_target="tpu_custom_call" | custom-call | tf_op jit(solution)/shard_map/update/pallas_call | solution.py:411
Async XLA Ops:
  4.2 10.0 %collective-permute-start.2 = (f32[8,8,128]{2,1,0:T(8,128)S(1)}, f32[8,8,128]{2,1,0:T(8,128)S(1)}, u32[]{:S(2)}, u32[]{:S(2)}) collective-permute-start(f32[8,8,128]{2,1,0:T(8,128)S(1)} %get-tuple-element.13.refs_0_.own_pair), channel_id=1, source_target_pairs={{0,1},{2,3},{1,0},{3,2},{4,5},{6,7},{5,4},{7,6},{8,9},{10,11},{9,8... | collective-permute-start | bytes 98312 | tf_op jit(solution)/shard_map/ppermute | solution.py:634
  4.3 9.9 %collective-permute-start.3 = (f32[8,8,128]{2,1,0:T(8,128)S(1)}, f32[8,8,128]{2,1,0:T(8,128)S(1)}, u32[]{:S(2)}, u32[]{:S(2)}) collective-permute-start(f32[8,8,128]{2,1,0:T(8,128)S(1)} %get-tuple-element.14.refs_1_.own_other), channel_id=1, source_target_pairs={{1,2},{2,1},{5,6},{6,5},{9,10},{10,9},{13,14},{14,13},{17,18},{18,... | collective-permute-start | bytes 98312 | tf_op jit(solution)/shard_map/ppermute | solution.py:634
  9.3 6.7 %collective-permute-start = (f32[2,32,512]{2,1,0:T(8,128)S(1)}, f32[2,32,512]{2,1,0:T(8,128)S(1)}, u32[]{:S(2)}, u32[]{:S(2)}) collective-permute-start(f32[2,32,512]{2,1,0:T(8,128)S(1)} %get-tuple-element.10.refs_0_), channel_id=1, source_target_pairs={{0,16},{16,0},{1,17},{17,1},{2,18},{18,2},{3,19},{19,3},{4,20},{20... | collective-permute-start | bytes 393224 | tf_op jit(solution)/shard_map/ppermute | solution.py:640
  13.6 11.4 %collective-permute-start.1 = (f32[2,64,512]{2,1,0:T(8,128)S(1)}, f32[2,64,512]{2,1,0:T(8,128)S(1)}, u32[]{:S(2)}, u32[]{:S(2)}) collective-permute-start(f32[2,64,512]{2,1,0:T(8,128)S(1)} %window_32.1.refs_2_), channel_id=1, source_target_pairs={{0,16},{16,0},{1,17},{17,1},{2,18},{18,2},{3,19},{19,3},{4,20},{20... | collective-permute-start | bytes 786440 | tf_op jit(solution)/shard_map/ppermute | solution.py:640
  14.3 4.8 %collective-permute-start.5 = (f32[19,8,128]{2,1,0:T(8,128)S(1)}, f32[19,8,128]{2,1,0:T(8,128)S(1)}, u32[]{:S(2)}, u32[]{:S(2)}) collective-permute-start(f32[19,8,128]{2,1,0:T(8,128)S(1)} %get-tuple-element.15.refs_4_), channel_id=1, source_target_pairs={{0,4},{8,12},{4,0},{12,8},{1,5},{9,13},{5,1},{13,9},{2,6},{10,14},... | collective-permute-start | bytes 233480 | tf_op jit(solution)/shard_map/ppermute | solution.py:634
  14.4 4.7 %collective-permute-start.6 = (f32[19,8,128]{2,1,0:T(8,128)S(1)}, f32[19,8,128]{2,1,0:T(8,128)S(1)}, u32[]{:S(2)}, u32[]{:S(2)}) collective-permute-start(f32[19,8,128]{2,1,0:T(8,128)S(1)} %get-tuple-element.16.refs_5_), channel_id=1, source_target_pairs={{4,8},{0,12},{8,4},{12,0},{5,9},{1,13},{9,5},{13,1},{6,10},{2,14},... | collective-permute-start | bytes 233480 | tf_op jit(solution)/shard_map/ppermute | solution.py:634
  17.5 7.5 %copy-start = (f32[2,128,512]{2,1,0:T(8,128)S(1)}, f32[2,128,512]{2,1,0:T(8,128)}, u32[]{:S(2)}) copy-start(f32[2,128,512]{2,1,0:T(8,128)} %maps_ref.1) | copy-start | bytes 1572868
  17.5 7.5 %copy-start.1 = (f32[2,128,512]{2,1,0:T(8,128)S(1)}, f32[2,128,512]{2,1,0:T(8,128)}, u32[]{:S(2)}) copy-start(f32[2,128,512]{2,1,0:T(8,128)} %first_ref.1) | copy-start | bytes 1572868
  17.5 7.5 %copy-start.2 = (f32[2,128,512]{2,1,0:T(8,128)S(1)}, f32[2,128,512]{2,1,0:T(8,128)}, u32[]{:S(2)}) copy-start(f32[2,128,512]{2,1,0:T(8,128)} %second_ref.1) | copy-start | bytes 1572868
  17.5 7.5 %collective-permute-start.4 = (f32[2,32,512]{2,1,0:T(8,128)S(1)}, f32[2,32,512]{2,1,0:T(8,128)S(1)}, u32[]{:S(2)}, u32[]{:S(2)}) collective-permute-start(f32[2,32,512]{2,1,0:T(8,128)S(1)} %window_96.1.refs_4_), channel_id=1, source_target_pairs={{0,16},{16,0},{1,17},{17,1},{2,18},{18,2},{3,19},{19,3},{4,20},{20... | collective-permute-start | bytes 393224 | tf_op jit(solution)/shard_map/ppermute | solution.py:640
  20.9 4.1 %collective-permute-start.7 = (f32[2,8,640]{2,1,0:T(8,128)S(1)}, f32[2,8,640]{2,1,0:T(8,128)S(1)}, u32[]{:S(2)}, u32[]{:S(2)}) collective-permute-start(f32[2,8,640]{2,1,0:T(8,128)S(1)} %edges.1.refs_6_), channel_id=1, source_target_pairs={{0,16},{16,0},{1,17},{17,1},{2,18},{18,2},{3,19},{19,3},{4,20},{20... | collective-permute-start | bytes 122888 | tf_op jit(solution)/shard_map/ppermute | solution.py:640

commit v4 on v3

--- a/solution.py
+++ b/solution.py
@@ -1,4 +1,5 @@
 import functools
+import math
 
 import jax
 import jax.numpy as jnp
@@ -19,24 +20,31 @@
 ADAM_EPS = 1e-08
 LOSS_WEIGHT = 2.0
 
+LOG2_E = math.log2(math.e)
+HALF_LN_2 = 0.5 * math.log(2.0)
+
 F32 = jnp.float32
 LANES = 128
 EDGE = 8
 HALO = 4
 DENSITY, TRAIT, VARIANCE, DISPERSAL, SELECTION, OPTIMUM, LAND, OBSERVED = range(8)
 FIELDS = 8
-RINGS = True, False
-GROUPS = {5: (5, 5, 5, 5, 5, 5), 9: (9, 9, 3, 3, 3, 9)}
+ENDS_MEET = {"lx": True, "ly": False}
+GROUPS = {5: (5, 5, 5, 5, 5, 5), 9: (9, 9, 3, 3, 3, 9), 10: (10, 10, 5, 5, 5, 10), 8: (8, 8, 4, 4, 4, 8), 12: (12, 12, 6, 6, 6, 12)}
 CUTS = (32, 96)
 WINDOW_US, EDGES_US = 4, 20
 VMEM_BYTES = 16 * 1024 * 1024
 SAVED = (
     "half",
     "land",
-    "select",
+    "rate",
+    "hs",
     "n0",
+    "z0",
+    "u0",
     "q0",
     "m0",
+    "ld",
     "wd",
     "wr",
     "lr",
@@ -48,6 +56,8 @@
     "vs",
     "p",
     "zs",
+    "es",
+    "misfit",
     "r",
     "n1",
     "q1",
@@ -74,12 +84,7 @@
 
 
 def reciprocal(value):
-    guess = pl.reciprocal(value, approx=True)
-    return guess * (2.0 - value * guess)
-
-
-def sigmoid(value):
-    return 0.5 + 0.5 * jnp.tanh(0.5 * value)
+    return 1.0 / value
 
 
 def dynamics(slabs, groups, cycles, load, steps_at, keep, put):
@@ -106,14 +111,30 @@
         group = groups[stage]
 
         def step(index, carry):
+            held = {}
+
+            def reader(offset):
+                def at(name, ahead=0, tile=None):
+                    if tile is not None:
+                        return keep[name][index * group + offset, tile]
+                    place = name, offset + ahead
+                    if place not in held:
+                        held[place] = keep[name][index * group + offset + ahead]
+                    return held[place]
+
+                return at
+
             for offset in range(group):
-                carry = body(index * group + offset, carry)
+                carry = body(index * group + offset, reader(offset), carry)
             return carry
 
         if group == slabs:
             return step(0, carry)
         return lax.fori_loop(0, slabs // group, step, carry)
 
+    def last(name, ahead=0):
+        return keep[name][slabs - 1 + ahead]
+
     def close(names):
         for name in names:
             keep[name][slabs] = pltpu.roll(keep[name][0], 7, 1)
@@ -121,43 +142,51 @@
     def wrapped(values):
         return tuple(pltpu.roll(value, 1, 1) for value in values)
 
-    def down_gap(name, k):
-        return keep[name][k + 1] - keep[name][k]
-
-    def row_fluxes(names, k):
-        weight = keep["wd"][k]
-        gaps = [down_gap(name, k) for name in names]
+    def down_gap(name, at):
+        return at(name, 1) - at(name)
+
+    def row_fluxes(names, at):
+        weight = at("wd")
+        gaps = [down_gap(name, at) for name in names]
         return gaps, tuple(weight * gap for gap in gaps)
 
-    def spread(names, k, above):
-        row_gaps, row_flux = row_fluxes(names, k)
-        weight = keep["wr"][k]
+    def spread(names, at, above):
+        row_gaps, row_flux = row_fluxes(names, at)
+        weight = at("wr")
         out, col_gaps = [], []
         for name, flux, before in zip(names, row_flux, above):
-            value = keep[name][k]
+            value = at(name)
             gap = right(value) - value
             col_flux = weight * gap
             out.append(value + (flux - before) + (col_flux - left(col_flux)))
             col_gaps.append(gap)
         return out, row_gaps, col_gaps, row_flux
 
-    def begin(k, _):
-        keep["half"][k] = 0.5 * REACH_MAX * sigmoid(load(DISPERSAL, k))
-        keep["land"][k] = load(LAND, k)
-        raw = load(SELECTION, k)
-        keep["select"][k] = jnp.maximum(raw, 0.0) + jnp.log(1.0 + jnp.exp(-jnp.abs(raw)))
-        n, z, v = load(DENSITY, k), load(TRAIT, k), load(VARIANCE, k)
-        keep["n0"][k] = n
-        keep["q0"][k] = n * z
-        keep["m0"][k] = n * (v + z * z)
+    def begin(k, at, _):
+        for t in range(sum(cycles)):
+            keep["half"][k, t] = 0.25 * REACH_MAX + 0.25 * REACH_MAX * jnp.tanh(0.5 * load(DISPERSAL, k, t))
+            land = load(LAND, k, t)
+            keep["land"][k, t] = land
+            keep["rate"][k, t] = LOG2_E * land
+            raw = load(SELECTION, k, t)
+            keep["hs"][k, t] = 0.5 * jnp.maximum(raw, 0.0) + HALF_LN_2 * jnp.log2(1.0 + jnp.exp2(-LOG2_E * jnp.abs(raw)))
+            n, z, v = load(DENSITY, k, t), load(TRAIT, k, t), load(VARIANCE, k, t)
+            u = v + z * z
+            keep["n0"][k, t] = n
+            keep["z0"][k, t] = z
+            keep["u0"][k, t] = u
+            keep["q0"][k, t] = n * z
+            keep["m0"][k, t] = n * u
         return ()
 
     each_slab(0, begin)
     close(("half", "land", "n0", "q0", "m0"))
 
-    def weigh(k, _):
-        half, land = keep["half"][k], keep["land"][k]
-        keep["wd"][k] = (half + keep["half"][k + 1]) * (land * keep["land"][k + 1])
+    def weigh(k, at, _):
+        half, land = at("half"), at("land")
+        pair = land * at("land", 1)
+        keep["ld"][k] = pair
+        keep["wd"][k] = (half + at("half", 1)) * pair
         pair = land * right(land)
         keep["lr"][k] = pair
         keep["wr"][k] = (half + right(half)) * pair
@@ -166,103 +195,112 @@
     each_slab(1, weigh)
     first_names, second_names = ("n0", "q0", "m0"), ("n1", "q1", "m1")
 
-    def first_step(k, above):
-        (ns, qs, ms), _, col_gaps, above = spread(first_names, k, above)
+    def first_step(k, at, above):
+        spreads, _, col_gaps, above = spread(first_names, at, above)
         for name, gap in zip(("dr0n", "dr0q", "dr0m"), col_gaps):
             keep[name][k] = gap
-        z, v = load(TRAIT, k), load(VARIANCE, k)
-        optimum, select, land = load(OPTIMUM, k), keep["select"][k], keep["land"][k]
-        r = reciprocal(ns + PRIOR_WEIGHT)
-        zs = (qs + PRIOR_WEIGHT * z) * r
-        vs = (ms + PRIOR_WEIGHT * (v + z * z)) * r - zs * zs
-        d = zs - optimum
-        p = reciprocal(1.0 + select * vs)
-        e = jnp.exp(land * (GROWTH_RATE * (1.0 - ns) - 0.5 * select * (d * d + vs)))
-        n1 = ns * e
-        z1 = optimum + p * d
-        u1 = vs * p + MUTATION_INPUT + z1 * z1
-        for name, value in zip(
-            ("e", "d", "vs", "p", "zs", "r", "n1", "q1", "m1", "z1", "u1"),
-            (e, d, vs, p, zs, r, n1, n1 * z1, n1 * u1, z1, u1),
-        ):
-            keep[name][k] = value
+        for t in range(sum(cycles)):
+            ns, qs, ms = (value[t] for value in spreads)
+            optimum, hs = load(OPTIMUM, k, t), at("hs", tile=t)
+            r = reciprocal(ns + PRIOR_WEIGHT)
+            zs = (qs + PRIOR_WEIGHT * at("z0", tile=t)) * r
+            es = (ms + PRIOR_WEIGHT * at("u0", tile=t)) * r
+            vs = es - zs * zs
+            d = zs - optimum
+            misfit = d * d + vs
+            p = reciprocal(1.0 + (hs + hs) * vs)
+            e = jnp.exp2(at("rate", tile=t) * (GROWTH_RATE - GROWTH_RATE * ns - hs * misfit))
+            n1 = ns * e
+            z1 = optimum + p * d
+            u1 = vs * p + MUTATION_INPUT + z1 * z1
+            for name, value in zip(
+                ("e", "d", "vs", "p", "zs", "es", "misfit", "r", "n1", "q1", "m1", "z1", "u1"),
+                (e, d, vs, p, zs, es, misfit, r, n1, n1 * z1, n1 * u1, z1, u1),
+            ):
+                keep[name][k, t] = value
         return above
 
-    each_slab(2, first_step, wrapped(row_fluxes(first_names, slabs - 1)[1]))
+    each_slab(2, first_step, wrapped(row_fluxes(first_names, last)[1]))
     close(second_names)
 
-    def second_step(k, above):
-        (ns, qs, ms), _, col_gaps, above = spread(second_names, k, above)
+    def second_step(k, at, above):
+        spreads, _, col_gaps, above = spread(second_names, at, above)
         for name, gap in zip(("dr1n", "dr1q", "dr1m"), col_gaps):
             keep[name][k] = gap
-        optimum, select, land = load(OPTIMUM, k), keep["select"][k], keep["land"][k]
-        r = reciprocal(ns + PRIOR_WEIGHT)
-        zs = (qs + PRIOR_WEIGHT * keep["z1"][k]) * r
-        es = (ms + PRIOR_WEIGHT * keep["u1"][k]) * r
-        vs = es - zs * zs
-        d = zs - optimum
-        misfit = d * d + vs
-        e = jnp.exp(land * (GROWTH_RATE * (1.0 - ns) - 0.5 * select * misfit))
-        n2 = ns * e
-        weight = jnp.where(steps_at(k) == 2.0, 2.0 * LOSS_WEIGHT * land, 0.0)
-        an = weight * (n2 - load(OBSERVED, k))
-        b = 0.5 * an * n2
-        av = -b * select
-        am = av * r
-        aq = -2.0 * optimum * am
-        keep["gsel"][k] = -b * misfit
-        keep["a2n"][k] = an * e - b - (aq * zs + am * es)
-        keep["a2q"][k] = aq
-        keep["a2m"][k] = am
+        for t in range(sum(cycles)):
+            ns, qs, ms = (value[t] for value in spreads)
+            optimum, hs, land = load(OPTIMUM, k, t), at("hs", tile=t), at("land", tile=t)
+            r = reciprocal(ns + PRIOR_WEIGHT)
+            zs = (qs + PRIOR_WEIGHT * at("z1", tile=t)) * r
+            es = (ms + PRIOR_WEIGHT * at("u1", tile=t)) * r
+            vs = es - zs * zs
+            d = zs - optimum
+            misfit = d * d + vs
+            e = jnp.exp2(at("rate", tile=t) * (GROWTH_RATE - GROWTH_RATE * ns - hs * misfit))
+            n2 = ns * e
+            an = jnp.where(steps_at(k, t) == 2.0, land, 0.0) * (n2 - load(OBSERVED, k, t))
+            b = an * n2
+            am = -(b * hs) * r
+            aq = (-2.0 * optimum) * am
+            keep["gsel"][k, t] = b * misfit
+            keep["a2n"][k, t] = an * e - 0.5 * b - (aq * zs + am * es)
+            keep["a2q"][k, t] = aq
+            keep["a2m"][k, t] = am
         return above
 
-    each_slab(3, second_step, wrapped(row_fluxes(second_names, slabs - 1)[1]))
+    each_slab(3, second_step, wrapped(row_fluxes(second_names, last)[1]))
     second_back, first_back = ("a2n", "a2q", "a2m"), ("a1n", "a1q", "a1m")
     close(second_back)
 
-    def back(k, above):
-        (an, aq, am), row_gaps, col_gaps, above = spread(second_back, k, above)
-        n_gap, q_gap, m_gap = [down_gap(name, k) * gap for name, gap in zip(second_names, row_gaps)]
+    def back(k, at, above):
+        spreads, row_gaps, col_gaps, above = spread(second_back, at, above)
+        n_gap, q_gap, m_gap = [down_gap(name, at) * gap for name, gap in zip(second_names, row_gaps)]
         keep["gd"][k] = n_gap + q_gap + m_gap
-        n_gap, q_gap, m_gap = [keep[f][k] * gap for f, gap in zip(("dr1n", "dr1q", "dr1m"), col_gaps)]
+        n_gap, q_gap, m_gap = [at(f) * gap for f, gap in zip(("dr1n", "dr1q", "dr1m"), col_gaps)]
         keep["gr"][k] = n_gap + q_gap + m_gap
-        n1, z1, land, select = keep["n1"][k], keep["z1"][k], keep["land"][k], keep["select"][k]
-        e, d, vs, p, zs, r = (keep[name][k] for name in ("e", "d", "vs", "p", "zs", "r"))
-        av = PRIOR_WEIGHT * keep["a2m"][k] + am * n1
-        az = PRIOR_WEIGHT * keep["a2q"][k] + aq * n1 + 2.0 * z1 * av
-        weight = jnp.where(steps_at(k) == 1.0, 2.0 * LOSS_WEIGHT * land, 0.0)
-        an = an + aq * z1 + am * keep["u1"][k] + weight * (n1 - load(OBSERVED, k))
-        b = 0.5 * an * n1 * land
-        at = -(az * d + av * vs) * (p * p)
-        gsel = keep["gsel"][k] + at * vs - b * (d * d + vs)
-        avs = av * p + select * (at - b)
-        azs = az * p - 2.0 * (b * select * d + zs * avs)
-        aqs, ams = azs * r, avs * r
-        keep["a1n"][k] = an * e - b - (aqs * zs + ams * (vs + zs * zs))
-        keep["a1q"][k] = aqs
-        keep["a1m"][k] = ams
-        put(1, k, gsel * sigmoid(load(SELECTION, k)))
+        for t in range(sum(cycles)):
+            an, aq, am = (value[t] for value in spreads)
+            n1, z1, land, hs = at("n1", tile=t), at("z1", tile=t), at("land", tile=t), at("hs", tile=t)
+            e, d, vs, p, zs, es, r = (at(name, tile=t) for name in ("e", "d", "vs", "p", "zs", "es", "r"))
+            av = PRIOR_WEIGHT * at("a2m", tile=t) + am * n1
+            az = PRIOR_WEIGHT * at("a2q", tile=t) + aq * n1 + (z1 + z1) * av
+            an = an + aq * z1 + am * at("u1", tile=t) + jnp.where(steps_at(k, t) == 1.0, land, 0.0) * (n1 - load(OBSERVED, k, t))
+            b = an * n1 * land
+            bs = b * hs
+            ar = (az * d + av * vs) * ((p + p) * p)
+            gsel = at("gsel", tile=t) + ar * vs + b * at("misfit", tile=t)
+            avs = av * p - ar * hs - bs
+            azs = az * p - 2.0 * (bs * d + zs * avs)
+            aqs, ams = azs * r, avs * r
+            keep["a1n"][k, t] = an * e - 0.5 * b - (aqs * zs + ams * es)
+            keep["a1q"][k, t] = aqs
+            keep["a1m"][k, t] = ams
+            raw = load(SELECTION, k, t)
+            put(1, k, t, gsel * (-0.5 * LOSS_WEIGHT - 0.5 * LOSS_WEIGHT * jnp.tanh(0.5 * raw)))
         return above
 
-    each_slab(4, back, wrapped(row_fluxes(second_back, slabs - 1)[1]))
+    each_slab(4, back, wrapped(row_fluxes(second_back, last)[1]))
     close(first_back)
 
-    def row_share(k):
-        n_gap, q_gap, m_gap = [down_gap(a, k) * down_gap(f, k) for a, f in zip(first_back, first_names)]
-        return (keep["gd"][k] + n_gap + q_gap + m_gap) * (keep["land"][k] * keep["land"][k + 1])
-
-    def finish(k, above):
-        here = row_share(k)
-        total = keep["gr"][k]
+    def row_share(at):
+        n_gap, q_gap, m_gap = [down_gap(a, at) * down_gap(f, at) for a, f in zip(first_back, first_names)]
+        return (at("gd") + n_gap + q_gap + m_gap) * at("ld")
+
+    def finish(k, at, above):
+        here = row_share(at)
+        total = at("gr")
         for name, field in zip(first_back, ("dr0n", "dr0q", "dr0m")):
-            value = keep[name][k]
-            total = total + (right(value) - value) * keep[field][k]
-        total = total * keep["lr"][k]
-        half = keep["half"][k]
-        put(0, k, half * (10.0 * half - 1.0) * (here + above[0] + total + left(total)))
+            value = at(name)
+            total = total + (right(value) - value) * at(field)
+        total = total * at("lr")
+        half = at("half")
+        scale = half * (2.0 * LOSS_WEIGHT / (0.5 * REACH_MAX) * half - 2.0 * LOSS_WEIGHT)
+        total = scale * (here + above[0] + total + left(total))
+        for t in range(sum(cycles)):
+            put(0, k, t, total[t])
         return (here,)
 
-    each_slab(5, finish, wrapped((row_share(slabs - 1),)))
+    each_slab(5, finish, wrapped((row_share(last),)))
 
 
 def step_rows(line):
@@ -299,16 +337,14 @@
     out_rows = out_ref.shape[1]
     slabs = rows // 8
 
-    def load(field, k):
-        return jnp.stack([fields[field, t, pl.ds(first + k, 8, stride=slabs), :] for t in range(tiles)])
-
-    def steps_at(k):
-        part = steps[0, pl.ds(first + k, 8, stride=slabs), :]
-        return jnp.broadcast_to(part[None], (tiles, 8, LANES))
-
-    def put(which, k, value):
-        for t in range(tiles):
-            grads[which, t, pl.ds(k, 8, stride=slabs), :] = value[t]
+    def load(field, k, t):
+        return fields[field, t, pl.ds(first + k, 8, stride=slabs), :]
+
+    def steps_at(k, t):
+        return steps[0, pl.ds(first + k, 8, stride=slabs), :]
+
+    def put(which, k, t, value):
+        grads[which, t, pl.ds(k, 8, stride=slabs), :] = value
 
     keep = {name: kept.at[index] for index, name in enumerate(SAVED)}
     dynamics(slabs, GROUPS[slabs], (tiles,), load, steps_at, keep, put)
@@ -530,16 +566,14 @@
     slabs = 3
     count = tiles + 2
 
-    def load(field, k):
-        return jnp.stack([strip[field, t, pl.ds(HALO + k, 8, stride=slabs), :] for t in range(count)])
-
-    def steps_at(k):
-        part = row_step[pl.ds(HALO + k, 8, stride=slabs), :]
-        return jnp.stack([part] * (tiles + 1) + [steps[1, :8]])
-
-    def put(which, k, value):
-        for t in range(count):
-            grad[which, t, pl.ds(HALO + k, 8, stride=slabs), :] = value[t]
+    def load(field, k, t):
+        return strip[field, t, pl.ds(HALO + k, 8, stride=slabs), :]
+
+    def steps_at(k, t):
+        return row_step[pl.ds(HALO + k, 8, stride=slabs), :] if t <= tiles else steps[1, :8]
+
+    def put(which, k, t, value):
+        grad[which, t, pl.ds(HALO + k, 8, stride=slabs), :] = value
 
     keep = {name: kept.at[index] for index, name in enumerate(SAVED)}
     dynamics(slabs, (slabs,) * 6, (tiles + 1, 1), load, steps_at, keep, put)
@@ -621,17 +655,22 @@
     return in_vmem(kernel, "update", [shape] * 3)(maps, first_moment, second_moment, *flat, *edge_grads)
 
 
-def pairings(axis, ring):
-    count = lax.axis_size(axis)
-    first = [(i, i + 1) for i in range(0, count - 1, 2)]
-    second = [(i, i + 1) for i in range(1, count - 1, 2)]
-    if ring and count % 2 == 0 and count > 2:
-        second.append((0, count - 1))
-    return [swaps + [(target, source) for source, target in swaps] for swaps in (first, second)]
-
-
-def swapped(arrays, axis, ring):
-    return [lax.ppermute(array, axis, swaps) for array, swaps in zip(arrays, pairings(axis, ring))]
+def swapped(arrays, axis, other):
+    count, beside, columns = lax.axis_size(axis), lax.axis_size(other), lax.axis_size("ly")
+    out = []
+    for array, start in zip(arrays, (0, 1)):
+        swaps = [(i, i + 1) for i in range(start, count - 1, 2)]
+        alone = sorted(set(range(count)) - {i for swap in swaps for i in swap})
+        pairs = [((i, k), (j, k)) for i, j in swaps for k in range(beside)]
+        if ENDS_MEET[axis] and len(alone) == 2:
+            pairs += [((alone[0], k), (alone[1], k)) for k in range(beside)]
+        else:
+            pairs += [((i, k), (i, k + 1)) for i in alone for k in range(0, beside - 1, 2)]
+        if axis == "ly":
+            pairs = [tuple(place[::-1] for place in pair) for pair in pairs]
+        flat = [tuple(row * columns + column for row, column in pair) for pair in pairs]
+        out.append(lax.ppermute(array, ("lx", "ly"), flat + [pair[::-1] for pair in flat]))
+    return out
 
 
 def both_scenarios(value):
@@ -657,11 +696,11 @@
     rows = maps.shape[1]
     upper, fields, steps, *own_sides = first_window(CUTS[0] + EDGE, CUTS[0], sources, obs_step)
     upper_terms = both_scenarios(upper)
-    sides = swapped(own_sides, "ly", RINGS[1])
-    middle = window(CUTS[0] - HALO, CUTS[1] - CUTS[0] + EDGE, CUTS[0], CUTS[1] - CUTS[0], fields, steps, *own_sides)
+    sides = swapped(own_sides, "ly", "lx")
+    middle = window(CUTS[0] - EDGE, CUTS[1] - CUTS[0] + 2 * EDGE, CUTS[0], CUTS[1] - CUTS[0], fields, steps, *own_sides)
     middle_terms = both_scenarios(middle)
     own_ends = pack_rows(fields, steps, *sides)
-    ends = swapped(own_ends, "lx", RINGS[0])
+    ends = swapped(own_ends, "lx", "ly")
     last = rows - CUTS[1]
     after = *own_sides, *sides, *own_ends, upper_terms[-1]
     lower = window(CUTS[1] - EDGE, last + EDGE, CUTS[1], last, fields, steps, *after)

time: 26.7 us -> 25.4 us (0.951)
  the two profiles are of different devices: /device:TPU:8 before, /device:TPU:0 now
where the time goes in v4:
time: 25.4 us; the launch traced here: 25.2 us
  Pallas kernels  11.3 us (44%)
  starting transfers between devices  9.4 us (37%)
  waiting for transfers between devices  3.85 us (15%)
  between operations  0.72 us (3%)
    ppermute x4, starting transfers between devices, swapped(): lax.ppermute(array, ('lx', 'ly'), flat + [pair[::-1] for pair in flat])  4.8 us
    ppermute x4, starting transfers between devices, both_scenarios(): return [value, lax.ppermute(value, 'scen', [(0, 1), (1, 0)])]  4.6 us
    pallas_call x2, Pallas kernels, window(): pl.pallas_call(functools.partial(window_kernel, first, rows, out_first -...  4.05 us
    ppermute x4, waiting for transfers between devices, both_scenarios(): return [value, lax.ppermute(value, 'scen', [(0, 1), (1, 0)])]  3.83 us
    pallas_call x1, Pallas kernels, first_window(): pl.pallas_call(functools.partial(first_kernel, tiles, rows), out_shape=[j...  3.74 us
    pallas_call x1, Pallas kernels, edges(): pl.pallas_call(edges_kernel, out_shape=jax.ShapeDtypeStruct((2, EDGE, (ti...  1.88 us
    pallas_call x2, Pallas kernels, call(): pl.pallas_call(kernel, out_shape=out_shape, in_specs=[space] * len(operan...  1.6 us
  transfers between devices with their start and end apart: 8, of which 1 were waited for; matrix products, arithmetic and copies ran while one was open for 0% of the time, Pallas kernels for 24%

profile of v4, /device:TPU:0, one launch (start us, length us, event | category | flops | bytes accessed | tf_op | source)
XLA Modules:
  0.0 25.2 jit_solution(1536948480238596424)
XLA Ops:
  0.6 3.7 %first_window.1 = (f32[2,32,512]{2,1,0:T(8,128)S(1)}, f32[8,4,128,128]{3,2,1,0:T(8,128)S(1)}, f32[2,128,128]{2,1,0:T(8,128)S(1)}, f32[8,8,128]{2,1,0:T(8,128)S(1)}, f32[8,8,128]{2,1,0:T(8,128)S(1)}) custom-call(f32[1,128,512]{2,1,0:T(8,128)} %refs_0_.1, f32[1,128,512]{2,1,0:T(8,128)} %refs_1_.1, f32[1,128,512]{2,1,0:T(8,128)} %refs_2_.1, ...), custom_call_target="tpu_custom_call" | custom-call | flops 4000000000 | bytes 14400000 | tf_op jit(solution)/shard_map/first_window/pallas_call | solution.py:382
  4.4 3.1 %collective-permute-start.2 = (f32[8,8,128]{2,1,0:T(8,128)S(1)}, f32[8,8,128]{2,1,0:T(8,128)S(1)}, u32[]{:S(2)}, u32[]{:S(2)}) collective-permute-start(f32[8,8,128]{2,1,0:T(8,128)S(1)} %get-tuple-element.13.refs_0_.own_pair), channel_id=1, source_target_pairs={{0,1},{4,5},{8,9},{12,13},{2,3},{6,7},{10,11},{14,15},{1,0},{5,4},... | collective-permute-start | bytes 98312 | tf_op jit(solution)/shard_map/ppermute | solution.py:672
  7.5 0.0 collective-permute-start.3
  7.5 1.5 %collective-permute-start = (f32[2,32,512]{2,1,0:T(8,128)S(1)}, f32[2,32,512]{2,1,0:T(8,128)S(1)}, u32[]{:S(2)}, u32[]{:S(2)}) collective-permute-start(f32[2,32,512]{2,1,0:T(8,128)S(1)} %get-tuple-element.10.refs_0_), channel_id=1, source_target_pairs={{0,16},{16,0},{1,17},{17,1},{2,18},{18,2},{3,19},{19,3},{4,20},{20... | collective-permute-start | bytes 393224 | tf_op jit(solution)/shard_map/ppermute | solution.py:679
  9.0 2.5 %window_32.1.refs_2_ = f32[2,64,512]{2,1,0:T(8,128)S(1)} custom-call(f32[8,4,128,128]{3,2,1,0:T(8,128)S(1)} %get-tuple-element.11.fields, f32[2,128,128]{2,1,0:T(8,128)S(1)} %get-tuple-element.12.steps, f32[8,8,128]{2,1,0:T(8,128)S(1)} %get-tuple-element.13.refs_0_.own_pair, f32[8,8,128]{2,1,0:T(8,128)S(1)} %get-tuple-element.14.refs_1_.own_other), custom_call_target="tpu_custom_call" | custom-call | flops 4000000000 | bytes 14400000 | tf_op jit(solution)/shard_map/window_32/pallas_call | solution.py:409
  11.5 0.6 %collective-permute-start.1 = (f32[2,64,512]{2,1,0:T(8,128)S(1)}, f32[2,64,512]{2,1,0:T(8,128)S(1)}, u32[]{:S(2)}, u32[]{:S(2)}) collective-permute-start(f32[2,64,512]{2,1,0:T(8,128)S(1)} %window_32.1.refs_2_), channel_id=1, source_target_pairs={{0,16},{16,0},{1,17},{17,1},{2,18},{18,2},{3,19},{19,3},{4,20},{20... | collective-permute-start | bytes 786440 | tf_op jit(solution)/shard_map/ppermute | solution.py:679
  12.1 0.0 collective-permute-done.2.from_pair.refs_2_.side_pair
  12.1 0.0 collective-permute-done.3.from_other.refs_3_.side_other
  12.1 0.1 pack_rows.1
  12.2 0.1 collective-permute-start.5
  12.3 1.6 %collective-permute-start.6 = (f32[19,8,128]{2,1,0:T(8,128)S(1)}, f32[19,8,128]{2,1,0:T(8,128)S(1)}, u32[]{:S(2)}, u32[]{:S(2)}) collective-permute-start(f32[19,8,128]{2,1,0:T(8,128)S(1)} %get-tuple-element.16.refs_5_), channel_id=1, source_target_pairs={{4,8},{5,9},{6,10},{7,11},{0,12},{1,13},{2,14},{3,15},{8,4},{9,5},... | collective-permute-start | bytes 233480 | tf_op jit(solution)/shard_map/ppermute | solution.py:672
  13.9 0.0 collective-permute-done.refs_6_.refs_1_
  13.9 1.5 %window_96.1.refs_4_ = f32[2,32,512]{2,1,0:T(8,128)S(1)} custom-call(f32[8,4,128,128]{3,2,1,0:T(8,128)S(1)} %get-tuple-element.11.fields, f32[2,128,128]{2,1,0:T(8,128)S(1)} %get-tuple-element.12.steps, f32[8,8,128]{2,1,0:T(8,128)S(1)} %get-tuple-element.13.refs_0_.own_pair, f32[8,8,128]{2,1,0:T(8,128)S(1)} %get-tuple-element.14.refs_1_.own_other, ...), custom_call_target="tpu_custom_call" | custom-call | flops 4000000000 | bytes 14400000 | tf_op jit(solution)/shard_map/window_96/pallas_call | solution.py:409
  15.4 0.0 copy-start
  15.5 0.0 copy-start.1
  15.5 0.0 copy-start.2
  15.5 1.6 %collective-permute-start.4 = (f32[2,32,512]{2,1,0:T(8,128)S(1)}, f32[2,32,512]{2,1,0:T(8,128)S(1)}, u32[]{:S(2)}, u32[]{:S(2)}) collective-permute-start(f32[2,32,512]{2,1,0:T(8,128)S(1)} %window_96.1.refs_4_), channel_id=1, source_target_pairs={{0,16},{16,0},{1,17},{17,1},{2,18},{18,2},{3,19},{19,3},{4,20},{20... | collective-permute-start | bytes 393224 | tf_op jit(solution)/shard_map/ppermute | solution.py:679
  17.0 0.0 collective-permute-done.5.end_pair
  17.0 0.0 collective-permute-done.6.end_other
  17.0 1.9 %edges.1.refs_6_ = f32[2,8,640]{2,1,0:T(8,128)S(1)} custom-call(f32[8,4,128,128]{3,2,1,0:T(8,128)S(1)} %get-tuple-element.11.fields, f32[2,128,128]{2,1,0:T(8,128)S(1)} %get-tuple-element.12.steps, f32[8,8,128]{2,1,0:T(8,128)S(1)} %get-tuple-element.13.refs_0_.own_pair, f32[8,8,128]{2,1,0:T(8,128)S(1)} %get-tuple-element.14.refs_1_.own_other, ...), custom_call_target="tpu_custom_call" | custom-call | flops 20000000000 | bytes 72000000 | tf_op jit(solution)/shard_map/edges/pallas_call | solution.py:591
  18.9 1.0 %collective-permute-start.7 = (f32[2,8,640]{2,1,0:T(8,128)S(1)}, f32[2,8,640]{2,1,0:T(8,128)S(1)}, u32[]{:S(2)}, u32[]{:S(2)}) collective-permute-start(f32[2,8,640]{2,1,0:T(8,128)S(1)} %edges.1.refs_6_), channel_id=1, source_target_pairs={{0,16},{16,0},{1,17},{17,1},{2,18},{18,2},{3,19},{19,3},{4,20},{20... | collective-permute-start | bytes 122888 | tf_op jit(solution)/shard_map/ppermute | solution.py:679
  19.9 3.8 %collective-permute-done.7.refs_7_ = f32[2,8,640]{2,1,0:T(8,128)S(1)} collective-permute-done((f32[2,8,640]{2,1,0:T(8,128)S(1)}, f32[2,8,640]{2,1,0:T(8,128)S(1)}, u32[]{:S(2)}, u32[]{:S(2)}) %collective-permute-start.7) | collective-permute-done | bytes 40992 | tf_op jit(solution)/shard_map/ppermute | solution.py:679
  23.7 0.0 collective-permute-done.4.refs_5_
  23.7 0.0 collective-permute-done.1.refs_3_
  23.7 0.0 copy-done
  23.7 0.0 copy-done.1
  23.7 0.0 copy-done.2
  23.7 1.5 %update.1 = (f32[2,128,512]{2,1,0:T(8,128)}, f32[2,128,512]{2,1,0:T(8,128)}, f32[2,128,512]{2,1,0:T(8,128)}) custom-call(f32[2,128,512]{2,1,0:T(8,128)S(1)} %copy-done, f32[2,128,512]{2,1,0:T(8,128)S(1)} %copy-done.1, f32[2,128,512]{2,1,0:T(8,128)S(1)} %copy-done.2, f32[2,32,512]{2,1,0:T(8,128)S(1)} %get-tuple-element.10.refs_0_, ...), custom_call_target="tpu_custom_call" | custom-call | tf_op jit(solution)/shard_map/update/pallas_call | solution.py:447
Async XLA Ops:
  4.4 7.7 %collective-permute-start.2 = (f32[8,8,128]{2,1,0:T(8,128)S(1)}, f32[8,8,128]{2,1,0:T(8,128)S(1)}, u32[]{:S(2)}, u32[]{:S(2)}) collective-permute-start(f32[8,8,128]{2,1,0:T(8,128)S(1)} %get-tuple-element.13.refs_0_.own_pair), channel_id=1, source_target_pairs={{0,1},{4,5},{8,9},{12,13},{2,3},{6,7},{10,11},{14,15},{1,0},{5,4},... | collective-permute-start | bytes 98312 | tf_op jit(solution)/shard_map/ppermute | solution.py:672
  7.5 4.6 %collective-permute-start.3 = (f32[8,8,128]{2,1,0:T(8,128)S(1)}, f32[8,8,128]{2,1,0:T(8,128)S(1)}, u32[]{:S(2)}, u32[]{:S(2)}) collective-permute-start(f32[8,8,128]{2,1,0:T(8,128)S(1)} %get-tuple-element.14.refs_1_.own_other), channel_id=1, source_target_pairs={{1,2},{5,6},{9,10},{13,14},{0,4},{8,12},{3,7},{11,15},{2,1},{6,5},... | collective-permute-start | bytes 98312 | tf_op jit(solution)/shard_map/ppermute | solution.py:672
  7.5 6.5 %collective-permute-start = (f32[2,32,512]{2,1,0:T(8,128)S(1)}, f32[2,32,512]{2,1,0:T(8,128)S(1)}, u32[]{:S(2)}, u32[]{:S(2)}) collective-permute-start(f32[2,32,512]{2,1,0:T(8,128)S(1)} %get-tuple-element.10.refs_0_), channel_id=1, source_target_pairs={{0,16},{16,0},{1,17},{17,1},{2,18},{18,2},{3,19},{19,3},{4,20},{20... | collective-permute-start | bytes 393224 | tf_op jit(solution)/shard_map/ppermute | solution.py:679
  11.5 12.2 %collective-permute-start.1 = (f32[2,64,512]{2,1,0:T(8,128)S(1)}, f32[2,64,512]{2,1,0:T(8,128)S(1)}, u32[]{:S(2)}, u32[]{:S(2)}) collective-permute-start(f32[2,64,512]{2,1,0:T(8,128)S(1)} %window_32.1.refs_2_), channel_id=1, source_target_pairs={{0,16},{16,0},{1,17},{17,1},{2,18},{18,2},{3,19},{19,3},{4,20},{20... | collective-permute-start | bytes 786440 | tf_op jit(solution)/shard_map/ppermute | solution.py:679
  12.2 4.8 %collective-permute-start.5 = (f32[19,8,128]{2,1,0:T(8,128)S(1)}, f32[19,8,128]{2,1,0:T(8,128)S(1)}, u32[]{:S(2)}, u32[]{:S(2)}) collective-permute-start(f32[19,8,128]{2,1,0:T(8,128)S(1)} %get-tuple-element.15.refs_4_), channel_id=1, source_target_pairs={{0,4},{1,5},{2,6},{3,7},{8,12},{9,13},{10,14},{11,15},{4,0},{5,1},... | collective-permute-start | bytes 233480 | tf_op jit(solution)/shard_map/ppermute | solution.py:672
  12.3 4.7 %collective-permute-start.6 = (f32[19,8,128]{2,1,0:T(8,128)S(1)}, f32[19,8,128]{2,1,0:T(8,128)S(1)}, u32[]{:S(2)}, u32[]{:S(2)}) collective-permute-start(f32[19,8,128]{2,1,0:T(8,128)S(1)} %get-tuple-element.16.refs_5_), channel_id=1, source_target_pairs={{4,8},{5,9},{6,10},{7,11},{0,12},{1,13},{2,14},{3,15},{8,4},{9,5},... | collective-permute-start | bytes 233480 | tf_op jit(solution)/shard_map/ppermute | solution.py:672
  15.4 8.3 %copy-start = (f32[2,128,512]{2,1,0:T(8,128)S(1)}, f32[2,128,512]{2,1,0:T(8,128)}, u32[]{:S(2)}) copy-start(f32[2,128,512]{2,1,0:T(8,128)} %maps_ref.1) | copy-start | bytes 1572868
  15.5 8.3 %copy-start.1 = (f32[2,128,512]{2,1,0:T(8,128)S(1)}, f32[2,128,512]{2,1,0:T(8,128)}, u32[]{:S(2)}) copy-start(f32[2,128,512]{2,1,0:T(8,128)} %first_ref.1) | copy-start | bytes 1572868
  15.5 8.3 %copy-start.2 = (f32[2,128,512]{2,1,0:T(8,128)S(1)}, f32[2,128,512]{2,1,0:T(8,128)}, u32[]{:S(2)}) copy-start(f32[2,128,512]{2,1,0:T(8,128)} %second_ref.1) | copy-start | bytes 1572868
  15.5 8.2 %collective-permute-start.4 = (f32[2,32,512]{2,1,0:T(8,128)S(1)}, f32[2,32,512]{2,1,0:T(8,128)S(1)}, u32[]{:S(2)}, u32[]{:S(2)}) collective-permute-start(f32[2,32,512]{2,1,0:T(8,128)S(1)} %window_96.1.refs_4_), channel_id=1, source_target_pairs={{0,16},{16,0},{1,17},{17,1},{2,18},{18,2},{3,19},{19,3},{4,20},{20... | collective-permute-start | bytes 393224 | tf_op jit(solution)/shard_map/ppermute | solution.py:679
  18.9 4.8 %collective-permute-start.7 = (f32[2,8,640]{2,1,0:T(8,128)S(1)}, f32[2,8,640]{2,1,0:T(8,128)S(1)}, u32[]{:S(2)}, u32[]{:S(2)}) collective-permute-start(f32[2,8,640]{2,1,0:T(8,128)S(1)} %edges.1.refs_6_), channel_id=1, source_target_pairs={{0,16},{16,0},{1,17},{17,1},{2,18},{18,2},{3,19},{19,3},{4,20},{20... | collective-permute-start | bytes 122888 | tf_op jit(solution)/shard_map/ppermute | solution.py:679

commit v5 on v4

--- a/solution.py
+++ b/solution.py
@@ -30,8 +30,19 @@
 DENSITY, TRAIT, VARIANCE, DISPERSAL, SELECTION, OPTIMUM, LAND, OBSERVED = range(8)
 FIELDS = 8
 ENDS_MEET = {"lx": True, "ly": False}
-GROUPS = {5: (5, 5, 5, 5, 5, 5), 9: (9, 9, 3, 3, 3, 9), 10: (10, 10, 5, 5, 5, 10), 8: (8, 8, 4, 4, 4, 8), 12: (12, 12, 6, 6, 6, 12)}
-CUTS = (32, 96)
+GROUPS = {
+    3: (3, 3, 3, 3, 3, 3),
+    4: (4, 4, 4, 4, 4, 4),
+    5: (5, 5, 5, 5, 5, 5),
+    6: (6, 6, 6, 6, 6, 6),
+    7: (7, 7, 7, 7, 7, 7),
+    8: (8, 8, 4, 4, 4, 8),
+    9: (9, 9, 3, 3, 3, 9),
+    10: (10, 10, 5, 5, 5, 10),
+    12: (12, 12, 6, 6, 6, 12),
+}
+APART = (6, 7)
+CUTS = (40, 112)
 WINDOW_US, EDGES_US = 4, 20
 VMEM_BYTES = 16 * 1024 * 1024
 SAVED = (
@@ -88,6 +99,8 @@
 
 
 def dynamics(slabs, groups, cycles, load, steps_at, keep, put):
+    apart = slabs in APART
+    once = (lax.axis_index("lx") >= 0).astype(jnp.int32) if apart else 1
     lane = lax.broadcasted_iota(jnp.int32, (sum(cycles), 8, LANES), 2)
     at_last, at_first = lane == LANES - 1, lane == 0
 
@@ -128,9 +141,9 @@
                 carry = body(index * group + offset, reader(offset), carry)
             return carry
 
-        if group == slabs:
+        if not apart and group == slabs:
             return step(0, carry)
-        return lax.fori_loop(0, slabs // group, step, carry)
+        return lax.fori_loop(0, slabs // group * once, step, carry)
 
     def last(name, ahead=0):
         return keep[name][slabs - 1 + ahead]
@@ -697,7 +710,7 @@
     upper, fields, steps, *own_sides = first_window(CUTS[0] + EDGE, CUTS[0], sources, obs_step)
     upper_terms = both_scenarios(upper)
     sides = swapped(own_sides, "ly", "lx")
-    middle = window(CUTS[0] - EDGE, CUTS[1] - CUTS[0] + 2 * EDGE, CUTS[0], CUTS[1] - CUTS[0], fields, steps, *own_sides)
+    middle = window(CUTS[0] - HALO, CUTS[1] - CUTS[0] + EDGE, CUTS[0], CUTS[1] - CUTS[0], fields, steps, *own_sides)
     middle_terms = both_scenarios(middle)
     own_ends = pack_rows(fields, steps, *sides)
     ends = swapped(own_ends, "lx", "ly")

time: 25.4 us -> 24.7 us (0.972)
  Pallas kernels: 11.3 us -> 10.6 us
  waiting for transfers between devices: 3.85 us -> 3.3 us
  starting transfers between devices: 9.4 us -> 9.9 us
    pallas_call x2, Pallas kernels: 4.05 us -> 3.39 us  [window(): pl.pallas_call(functools.partial(window_kernel, first, rows, out_first -...]
    ppermute x4, waiting for transfers between devices: 3.83 us -> 3.28 us  [both_scenarios(): return [value, lax.ppermute(value, 'scen', [(0, 1), (1, 0)])]]
    ppermute x4, starting transfers between devices: 4.6 us -> 5.1 us  [both_scenarios(): return [value, lax.ppermute(value, 'scen', [(0, 1), (1, 0)])]]
  transfers between devices with their start and end apart: 8 -> 8, of which waited for: 1 -> 2; matrix products, arithmetic and copies ran while one was open for 0% -> 0% of each run, Pallas kernels for 24% -> 22%
where the time goes in v5:
time: 24.7 us; the launch traced here: 24.5 us
  Pallas kernels  10.6 us (43%)
  starting transfers between devices  9.9 us (40%)
  waiting for transfers between devices  3.3 us (13%)
  between operations  0.71 us (3%)
    ppermute x4, starting transfers between devices, both_scenarios(): return [value, lax.ppermute(value, 'scen', [(0, 1), (1, 0)])]  5.1 us
    ppermute x4, starting transfers between devices, swapped(): lax.ppermute(array, ('lx', 'ly'), flat + [pair[::-1] for pair in flat])  4.8 us
    pallas_call x1, Pallas kernels, first_window(): pl.pallas_call(functools.partial(first_kernel, tiles, rows), out_shape=[j...  3.69 us
    pallas_call x2, Pallas kernels, window(): pl.pallas_call(functools.partial(window_kernel, first, rows, out_first -...  3.39 us
    ppermute x4, waiting for transfers between devices, both_scenarios(): return [value, lax.ppermute(value, 'scen', [(0, 1), (1, 0)])]  3.28 us
    pallas_call x1, Pallas kernels, edges(): pl.pallas_call(edges_kernel, out_shape=jax.ShapeDtypeStruct((2, EDGE, (ti...  1.88 us
    pallas_call x2, Pallas kernels, call(): pl.pallas_call(kernel, out_shape=out_shape, in_specs=[space] * len(operan...  1.6 us
  transfers between devices with their start and end apart: 8, of which 2 were waited for; matrix products, arithmetic and copies ran while one was open for 0% of the time, Pallas kernels for 22%

profile of v5, /device:TPU:0, one launch (start us, length us, event | category | flops | bytes accessed | tf_op | source)
XLA Modules:
  0.0 24.5 jit_solution(15943747052391471475)
XLA Ops:
  0.6 3.7 %first_window.1 = (f32[2,40,512]{2,1,0:T(8,128)S(1)}, f32[8,4,128,128]{3,2,1,0:T(8,128)S(1)}, f32[2,128,128]{2,1,0:T(8,128)S(1)}, f32[8,8,128]{2,1,0:T(8,128)S(1)}, f32[8,8,128]{2,1,0:T(8,128)S(1)}) custom-call(f32[1,128,512]{2,1,0:T(8,128)} %refs_0_.1, f32[1,128,512]{2,1,0:T(8,128)} %refs_1_.1, f32[1,128,512]{2,1,0:T(8,128)} %refs_2_.1, ...), custom_call_target="tpu_custom_call" | custom-call | flops 4000000000 | bytes 14400000 | tf_op jit(solution)/shard_map/first_window/pallas_call | solution.py:395
  4.3 3.1 %collective-permute-start.2 = (f32[8,8,128]{2,1,0:T(8,128)S(1)}, f32[8,8,128]{2,1,0:T(8,128)S(1)}, u32[]{:S(2)}, u32[]{:S(2)}) collective-permute-start(f32[8,8,128]{2,1,0:T(8,128)S(1)} %get-tuple-element.13.refs_0_.own_pair), channel_id=1, source_target_pairs={{0,1},{4,5},{8,9},{12,13},{2,3},{6,7},{10,11},{14,15},{1,0},{5,4},... | collective-permute-start | bytes 98312 | tf_op jit(solution)/shard_map/ppermute | solution.py:685
  7.4 0.0 collective-permute-start.3
  7.4 1.5 %collective-permute-start = (f32[2,40,512]{2,1,0:T(8,128)S(1)}, f32[2,40,512]{2,1,0:T(8,128)S(1)}, u32[]{:S(2)}, u32[]{:S(2)}) collective-permute-start(f32[2,40,512]{2,1,0:T(8,128)S(1)} %get-tuple-element.10.refs_0_), channel_id=1, source_target_pairs={{0,16},{16,0},{1,17},{17,1},{2,18},{18,2},{3,19},{19,3},{4,20},{20... | collective-permute-start | bytes 491528 | tf_op jit(solution)/shard_map/ppermute | solution.py:692
  8.9 2.5 %window_40.1.refs_2_ = f32[2,72,512]{2,1,0:T(8,128)S(1)} custom-call(f32[8,4,128,128]{3,2,1,0:T(8,128)S(1)} %get-tuple-element.11.fields, f32[2,128,128]{2,1,0:T(8,128)S(1)} %get-tuple-element.12.steps, f32[8,8,128]{2,1,0:T(8,128)S(1)} %get-tuple-element.13.refs_0_.own_pair, f32[8,8,128]{2,1,0:T(8,128)S(1)} %get-tuple-element.14.refs_1_.own_other), custom_call_target="tpu_custom_call" | custom-call | flops 4000000000 | bytes 14400000 | tf_op jit(solution)/shard_map/window_40/pallas_call | solution.py:422
  11.5 0.6 %collective-permute-start.1 = (f32[2,72,512]{2,1,0:T(8,128)S(1)}, f32[2,72,512]{2,1,0:T(8,128)S(1)}, u32[]{:S(2)}, u32[]{:S(2)}) collective-permute-start(f32[2,72,512]{2,1,0:T(8,128)S(1)} %window_40.1.refs_2_), channel_id=1, source_target_pairs={{0,16},{16,0},{1,17},{17,1},{2,18},{18,2},{3,19},{19,3},{4,20},{20... | collective-permute-start | bytes 884744 | tf_op jit(solution)/shard_map/ppermute | solution.py:692
  12.1 0.0 collective-permute-done.2.from_pair.refs_2_.side_pair
  12.1 0.0 collective-permute-done.3.from_other.refs_3_.side_other
  12.1 0.1 pack_rows.1
  12.2 0.1 collective-permute-start.5
  12.2 1.6 %collective-permute-start.6 = (f32[19,8,128]{2,1,0:T(8,128)S(1)}, f32[19,8,128]{2,1,0:T(8,128)S(1)}, u32[]{:S(2)}, u32[]{:S(2)}) collective-permute-start(f32[19,8,128]{2,1,0:T(8,128)S(1)} %get-tuple-element.16.refs_5_), channel_id=1, source_target_pairs={{4,8},{5,9},{6,10},{7,11},{0,12},{1,13},{2,14},{3,15},{8,4},{9,5},... | collective-permute-start | bytes 233480 | tf_op jit(solution)/shard_map/ppermute | solution.py:685
  13.9 0.2 collective-permute-done.refs_6_.refs_1_
  14.0 0.9 %window_112.1.refs_4_ = f32[2,16,512]{2,1,0:T(8,128)S(1)} custom-call(f32[8,4,128,128]{3,2,1,0:T(8,128)S(1)} %get-tuple-element.11.fields, f32[2,128,128]{2,1,0:T(8,128)S(1)} %get-tuple-element.12.steps, f32[8,8,128]{2,1,0:T(8,128)S(1)} %get-tuple-element.13.refs_0_.own_pair, f32[8,8,128]{2,1,0:T(8,128)S(1)} %get-tuple-element.14.refs_1_.own_other, ...), custom_call_target="tpu_custom_call" | custom-call | flops 4000000000 | bytes 14400000 | tf_op jit(solution)/shard_map/window_112/pallas_call | solution.py:422
  14.9 0.0 copy-start
  14.9 0.0 copy-start.1
  14.9 0.0 copy-start.2
  14.9 1.9 %collective-permute-start.4 = (f32[2,16,512]{2,1,0:T(8,128)S(1)}, f32[2,16,512]{2,1,0:T(8,128)S(1)}, u32[]{:S(2)}, u32[]{:S(2)}) collective-permute-start(f32[2,16,512]{2,1,0:T(8,128)S(1)} %window_112.1.refs_4_), channel_id=1, source_target_pairs={{0,16},{16,0},{1,17},{17,1},{2,18},{18,2},{3,19},{19,3},{4,20},{20... | collective-permute-start | bytes 196616 | tf_op jit(solution)/shard_map/ppermute | solution.py:692
  16.9 0.0 collective-permute-done.5.end_pair
  16.9 0.0 collective-permute-done.6.end_other
  16.9 1.9 %edges.1.refs_6_ = f32[2,8,640]{2,1,0:T(8,128)S(1)} custom-call(f32[8,4,128,128]{3,2,1,0:T(8,128)S(1)} %get-tuple-element.11.fields, f32[2,128,128]{2,1,0:T(8,128)S(1)} %get-tuple-element.12.steps, f32[8,8,128]{2,1,0:T(8,128)S(1)} %get-tuple-element.13.refs_0_.own_pair, f32[8,8,128]{2,1,0:T(8,128)S(1)} %get-tuple-element.14.refs_1_.own_other, ...), custom_call_target="tpu_custom_call" | custom-call | flops 20000000000 | bytes 72000000 | tf_op jit(solution)/shard_map/edges/pallas_call | solution.py:604
  18.8 1.1 %collective-permute-start.7 = (f32[2,8,640]{2,1,0:T(8,128)S(1)}, f32[2,8,640]{2,1,0:T(8,128)S(1)}, u32[]{:S(2)}, u32[]{:S(2)}) collective-permute-start(f32[2,8,640]{2,1,0:T(8,128)S(1)} %edges.1.refs_6_), channel_id=1, source_target_pairs={{0,16},{16,0},{1,17},{17,1},{2,18},{18,2},{3,19},{19,3},{4,20},{20... | collective-permute-start | bytes 122888 | tf_op jit(solution)/shard_map/ppermute | solution.py:692
  19.8 3.1 %collective-permute-done.7.refs_7_ = f32[2,8,640]{2,1,0:T(8,128)S(1)} collective-permute-done((f32[2,8,640]{2,1,0:T(8,128)S(1)}, f32[2,8,640]{2,1,0:T(8,128)S(1)}, u32[]{:S(2)}, u32[]{:S(2)}) %collective-permute-start.7) | collective-permute-done | bytes 40992 | tf_op jit(solution)/shard_map/ppermute | solution.py:692
  23.0 0.0 collective-permute-done.4.refs_5_
  23.0 0.0 collective-permute-done.1.refs_3_
  23.0 0.0 copy-done
  23.0 0.0 copy-done.1
  23.0 0.0 copy-done.2
  23.0 1.5 %update.1 = (f32[2,128,512]{2,1,0:T(8,128)}, f32[2,128,512]{2,1,0:T(8,128)}, f32[2,128,512]{2,1,0:T(8,128)}) custom-call(f32[2,128,512]{2,1,0:T(8,128)S(1)} %copy-done, f32[2,128,512]{2,1,0:T(8,128)S(1)} %copy-done.1, f32[2,128,512]{2,1,0:T(8,128)S(1)} %copy-done.2, f32[2,40,512]{2,1,0:T(8,128)S(1)} %get-tuple-element.10.refs_0_, ...), custom_call_target="tpu_custom_call" | custom-call | tf_op jit(solution)/shard_map/update/pallas_call | solution.py:460
Async XLA Ops:
  4.3 7.7 %collective-permute-start.2 = (f32[8,8,128]{2,1,0:T(8,128)S(1)}, f32[8,8,128]{2,1,0:T(8,128)S(1)}, u32[]{:S(2)}, u32[]{:S(2)}) collective-permute-start(f32[8,8,128]{2,1,0:T(8,128)S(1)} %get-tuple-element.13.refs_0_.own_pair), channel_id=1, source_target_pairs={{0,1},{4,5},{8,9},{12,13},{2,3},{6,7},{10,11},{14,15},{1,0},{5,4},... | collective-permute-start | bytes 98312 | tf_op jit(solution)/shard_map/ppermute | solution.py:685
  7.4 4.6 %collective-permute-start.3 = (f32[8,8,128]{2,1,0:T(8,128)S(1)}, f32[8,8,128]{2,1,0:T(8,128)S(1)}, u32[]{:S(2)}, u32[]{:S(2)}) collective-permute-start(f32[8,8,128]{2,1,0:T(8,128)S(1)} %get-tuple-element.14.refs_1_.own_other), channel_id=1, source_target_pairs={{1,2},{5,6},{9,10},{13,14},{0,4},{8,12},{3,7},{11,15},{2,1},{6,5},... | collective-permute-start | bytes 98312 | tf_op jit(solution)/shard_map/ppermute | solution.py:685
  7.4 6.6 %collective-permute-start = (f32[2,40,512]{2,1,0:T(8,128)S(1)}, f32[2,40,512]{2,1,0:T(8,128)S(1)}, u32[]{:S(2)}, u32[]{:S(2)}) collective-permute-start(f32[2,40,512]{2,1,0:T(8,128)S(1)} %get-tuple-element.10.refs_0_), channel_id=1, source_target_pairs={{0,16},{16,0},{1,17},{17,1},{2,18},{18,2},{3,19},{19,3},{4,20},{20... | collective-permute-start | bytes 491528 | tf_op jit(solution)/shard_map/ppermute | solution.py:692
  11.5 11.5 %collective-permute-start.1 = (f32[2,72,512]{2,1,0:T(8,128)S(1)}, f32[2,72,512]{2,1,0:T(8,128)S(1)}, u32[]{:S(2)}, u32[]{:S(2)}) collective-permute-start(f32[2,72,512]{2,1,0:T(8,128)S(1)} %window_40.1.refs_2_), channel_id=1, source_target_pairs={{0,16},{16,0},{1,17},{17,1},{2,18},{18,2},{3,19},{19,3},{4,20},{20... | collective-permute-start | bytes 884744 | tf_op jit(solution)/shard_map/ppermute | solution.py:692
  12.2 4.7 %collective-permute-start.5 = (f32[19,8,128]{2,1,0:T(8,128)S(1)}, f32[19,8,128]{2,1,0:T(8,128)S(1)}, u32[]{:S(2)}, u32[]{:S(2)}) collective-permute-start(f32[19,8,128]{2,1,0:T(8,128)S(1)} %get-tuple-element.15.refs_4_), channel_id=1, source_target_pairs={{0,4},{1,5},{2,6},{3,7},{8,12},{9,13},{10,14},{11,15},{4,0},{5,1},... | collective-permute-start | bytes 233480 | tf_op jit(solution)/shard_map/ppermute | solution.py:685
  12.2 4.6 %collective-permute-start.6 = (f32[19,8,128]{2,1,0:T(8,128)S(1)}, f32[19,8,128]{2,1,0:T(8,128)S(1)}, u32[]{:S(2)}, u32[]{:S(2)}) collective-permute-start(f32[19,8,128]{2,1,0:T(8,128)S(1)} %get-tuple-element.16.refs_5_), channel_id=1, source_target_pairs={{4,8},{5,9},{6,10},{7,11},{0,12},{1,13},{2,14},{3,15},{8,4},{9,5},... | collective-permute-start | bytes 233480 | tf_op jit(solution)/shard_map/ppermute | solution.py:685
  14.9 8.1 %copy-start = (f32[2,128,512]{2,1,0:T(8,128)S(1)}, f32[2,128,512]{2,1,0:T(8,128)}, u32[]{:S(2)}) copy-start(f32[2,128,512]{2,1,0:T(8,128)} %maps_ref.1) | copy-start | bytes 1572868
  14.9 8.1 %copy-start.1 = (f32[2,128,512]{2,1,0:T(8,128)S(1)}, f32[2,128,512]{2,1,0:T(8,128)}, u32[]{:S(2)}) copy-start(f32[2,128,512]{2,1,0:T(8,128)} %first_ref.1) | copy-start | bytes 1572868
  14.9 8.1 %copy-start.2 = (f32[2,128,512]{2,1,0:T(8,128)S(1)}, f32[2,128,512]{2,1,0:T(8,128)}, u32[]{:S(2)}) copy-start(f32[2,128,512]{2,1,0:T(8,128)} %second_ref.1) | copy-start | bytes 1572868
  14.9 8.0 %collective-permute-start.4 = (f32[2,16,512]{2,1,0:T(8,128)S(1)}, f32[2,16,512]{2,1,0:T(8,128)S(1)}, u32[]{:S(2)}, u32[]{:S(2)}) collective-permute-start(f32[2,16,512]{2,1,0:T(8,128)S(1)} %window_112.1.refs_4_), channel_id=1, source_target_pairs={{0,16},{16,0},{1,17},{17,1},{2,18},{18,2},{3,19},{19,3},{4,20},{20... | collective-permute-start | bytes 196616 | tf_op jit(solution)/shard_map/ppermute | solution.py:692
  18.8 4.2 %collective-permute-start.7 = (f32[2,8,640]{2,1,0:T(8,128)S(1)}, f32[2,8,640]{2,1,0:T(8,128)S(1)}, u32[]{:S(2)}, u32[]{:S(2)}) collective-permute-start(f32[2,8,640]{2,1,0:T(8,128)S(1)} %edges.1.refs_6_), channel_id=1, source_target_pairs={{0,16},{16,0},{1,17},{17,1},{2,18},{18,2},{3,19},{19,3},{4,20},{20... | collective-permute-start | bytes 122888 | tf_op jit(solution)/shard_map/ppermute | solution.py:692

commit v6 on v5

--- a/solution.py
+++ b/solution.py
@@ -372,15 +372,16 @@
     height = fields.shape[2]
     early = tile_copies(tiles, 0, rows, sources, fields, codes, sems)
     late = tile_copies(tiles, rows, height - rows, sources, fields, codes, late_sems)
-    early.append(pltpu.make_async_copy(step_ref, line, sems.at[7, 0]))
-    for copy in early + late:
+    steps_copy = pltpu.make_async_copy(step_ref, line, sems.at[7, 0])
+    for copy in [steps_copy] + early + late:
         copy.start()
+    steps_copy.wait()
+    wide = jnp.broadcast_to(line[0:1, :].astype(F32), (8, LANES))
+    steps[0] = step_rows(wide)
+    steps[1] = jnp.broadcast_to(wide[0:1], (LANES, LANES))
     for copy in early:
         copy.wait()
     fields[LAND, :, :rows] = codes[:, :rows].astype(F32)
-    wide = jnp.broadcast_to(line[0:1, :].astype(F32), (8, LANES))
-    steps[0] = step_rows(wide)
-    steps[1] = jnp.broadcast_to(wide[0:1], (LANES, LANES))
     window_kernel(0, rows, 0, fields, steps, out_ref, grads, kept)
     for copy in late:
         copy.wait()
@@ -556,9 +557,10 @@
         here = rights[index] if index < FIELDS else zeros
         after = lefts[following] if following < FIELDS else zeros
         stack.append(jnp.where(sub < HALO, here, after))
+    outer_step = jnp.where(lane < LANES // 2, from_below(base + 2), from_above(base + 2))
+    stack[FIELDS] = lined(steps[1, :8], outer_step)
     flipped = jnp.transpose(jnp.concatenate(stack, 0))[:32]
-    outer_step = jnp.where(lane < LANES // 2, from_below(base + 2), from_above(base + 2))
-    row_step[...] = step_rows(lined(steps[1, :8], outer_step))[:32]
+    row_step[...] = jnp.broadcast_to(flipped[:, 8 * FIELDS : 8 * FIELDS + 1], (32, LANES))
     for field in range(FIELDS):
         for t in range(tiles):
             above, below = from_above(field // 2 * tiles + t), from_below(field // 2 * tiles + t)

time: 24.7 us -> 24.6 us (level)
  no operation moved by 1% of the time
where the time goes in v6:
time: 24.6 us; the launch traced here: 24.4 us
  Pallas kernels  10.5 us (43%)
  starting transfers between devices  9.9 us (40%)
  waiting for transfers between devices  3.3 us (13%)
  between operations  0.71 us (3%)
    ppermute x4, starting transfers between devices, both_scenarios(): return [value, lax.ppermute(value, 'scen', [(0, 1), (1, 0)])]  5.11 us
    ppermute x4, starting transfers between devices, swapped(): lax.ppermute(array, ('lx', 'ly'), flat + [pair[::-1] for pair in flat])  4.8 us
    pallas_call x1, Pallas kernels, first_window(): pl.pallas_call(functools.partial(first_kernel, tiles, rows), out_shape=[j...  3.61 us
    pallas_call x2, Pallas kernels, window(): pl.pallas_call(functools.partial(window_kernel, first, rows, out_first -...  3.39 us
    ppermute x4, waiting for transfers between devices, both_scenarios(): return [value, lax.ppermute(value, 'scen', [(0, 1), (1, 0)])]  3.29 us
    pallas_call x1, Pallas kernels, edges(): pl.pallas_call(edges_kernel, out_shape=jax.ShapeDtypeStruct((2, EDGE, (ti...  1.87 us
    pallas_call x2, Pallas kernels, call(): pl.pallas_call(kernel, out_shape=out_shape, in_specs=[space] * len(operan...  1.6 us
  transfers between devices with their start and end apart: 8, of which 2 were waited for; matrix products, arithmetic and copies ran while one was open for 0% of the time, Pallas kernels for 22%

profile of v6, /device:TPU:0, one launch (start us, length us, event | category | flops | bytes accessed | tf_op | source)
XLA Modules:
  0.0 24.4 jit_solution(395988188122141499)
XLA Ops:
  0.6 3.6 %first_window.1 = (f32[2,40,512]{2,1,0:T(8,128)S(1)}, f32[8,4,128,128]{3,2,1,0:T(8,128)S(1)}, f32[2,128,128]{2,1,0:T(8,128)S(1)}, f32[8,8,128]{2,1,0:T(8,128)S(1)}, f32[8,8,128]{2,1,0:T(8,128)S(1)}) custom-call(f32[1,128,512]{2,1,0:T(8,128)} %refs_0_.1, f32[1,128,512]{2,1,0:T(8,128)} %refs_1_.1, f32[1,128,512]{2,1,0:T(8,128)} %refs_2_.1, ...), custom_call_target="tpu_custom_call" | custom-call | flops 4000000000 | bytes 14400000 | tf_op jit(solution)/shard_map/first_window/pallas_call | solution.py:396
  4.2 3.1 %collective-permute-start.2 = (f32[8,8,128]{2,1,0:T(8,128)S(1)}, f32[8,8,128]{2,1,0:T(8,128)S(1)}, u32[]{:S(2)}, u32[]{:S(2)}) collective-permute-start(f32[8,8,128]{2,1,0:T(8,128)S(1)} %get-tuple-element.13.refs_0_.own_pair), channel_id=1, source_target_pairs={{0,1},{4,5},{8,9},{12,13},{2,3},{6,7},{10,11},{14,15},{1,0},{5,4},... | collective-permute-start | bytes 98312 | tf_op jit(solution)/shard_map/ppermute | solution.py:687
  7.3 0.0 collective-permute-start.3
  7.3 1.5 %collective-permute-start = (f32[2,40,512]{2,1,0:T(8,128)S(1)}, f32[2,40,512]{2,1,0:T(8,128)S(1)}, u32[]{:S(2)}, u32[]{:S(2)}) collective-permute-start(f32[2,40,512]{2,1,0:T(8,128)S(1)} %get-tuple-element.10.refs_0_), channel_id=1, source_target_pairs={{0,16},{16,0},{1,17},{17,1},{2,18},{18,2},{3,19},{19,3},{4,20},{20... | collective-permute-start | bytes 491528 | tf_op jit(solution)/shard_map/ppermute | solution.py:694
  8.8 2.5 %window_40.1.refs_2_ = f32[2,72,512]{2,1,0:T(8,128)S(1)} custom-call(f32[8,4,128,128]{3,2,1,0:T(8,128)S(1)} %get-tuple-element.11.fields, f32[2,128,128]{2,1,0:T(8,128)S(1)} %get-tuple-element.12.steps, f32[8,8,128]{2,1,0:T(8,128)S(1)} %get-tuple-element.13.refs_0_.own_pair, f32[8,8,128]{2,1,0:T(8,128)S(1)} %get-tuple-element.14.refs_1_.own_other), custom_call_target="tpu_custom_call" | custom-call | flops 4000000000 | bytes 14400000 | tf_op jit(solution)/shard_map/window_40/pallas_call | solution.py:423
  11.4 0.6 %collective-permute-start.1 = (f32[2,72,512]{2,1,0:T(8,128)S(1)}, f32[2,72,512]{2,1,0:T(8,128)S(1)}, u32[]{:S(2)}, u32[]{:S(2)}) collective-permute-start(f32[2,72,512]{2,1,0:T(8,128)S(1)} %window_40.1.refs_2_), channel_id=1, source_target_pairs={{0,16},{16,0},{1,17},{17,1},{2,18},{18,2},{3,19},{19,3},{4,20},{20... | collective-permute-start | bytes 884744 | tf_op jit(solution)/shard_map/ppermute | solution.py:694
  12.0 0.0 collective-permute-done.2.from_pair.refs_2_.side_pair
  12.0 0.0 collective-permute-done.3.from_other.refs_3_.side_other
  12.0 0.1 pack_rows.1
  12.1 0.1 collective-permute-start.5
  12.2 1.6 %collective-permute-start.6 = (f32[19,8,128]{2,1,0:T(8,128)S(1)}, f32[19,8,128]{2,1,0:T(8,128)S(1)}, u32[]{:S(2)}, u32[]{:S(2)}) collective-permute-start(f32[19,8,128]{2,1,0:T(8,128)S(1)} %get-tuple-element.16.refs_5_), channel_id=1, source_target_pairs={{4,8},{5,9},{6,10},{7,11},{0,12},{1,13},{2,14},{3,15},{8,4},{9,5},... | collective-permute-start | bytes 233480 | tf_op jit(solution)/shard_map/ppermute | solution.py:687
  13.8 0.2 collective-permute-done.refs_6_.refs_1_
  14.0 0.9 %window_112.1.refs_4_ = f32[2,16,512]{2,1,0:T(8,128)S(1)} custom-call(f32[8,4,128,128]{3,2,1,0:T(8,128)S(1)} %get-tuple-element.11.fields, f32[2,128,128]{2,1,0:T(8,128)S(1)} %get-tuple-element.12.steps, f32[8,8,128]{2,1,0:T(8,128)S(1)} %get-tuple-element.13.refs_0_.own_pair, f32[8,8,128]{2,1,0:T(8,128)S(1)} %get-tuple-element.14.refs_1_.own_other, ...), custom_call_target="tpu_custom_call" | custom-call | flops 4000000000 | bytes 14400000 | tf_op jit(solution)/shard_map/window_112/pallas_call | solution.py:423
  14.8 0.0 copy-start
  14.8 0.0 copy-start.1
  14.8 0.0 copy-start.2
  14.8 1.9 %collective-permute-start.4 = (f32[2,16,512]{2,1,0:T(8,128)S(1)}, f32[2,16,512]{2,1,0:T(8,128)S(1)}, u32[]{:S(2)}, u32[]{:S(2)}) collective-permute-start(f32[2,16,512]{2,1,0:T(8,128)S(1)} %window_112.1.refs_4_), channel_id=1, source_target_pairs={{0,16},{16,0},{1,17},{17,1},{2,18},{18,2},{3,19},{19,3},{4,20},{20... | collective-permute-start | bytes 196616 | tf_op jit(solution)/shard_map/ppermute | solution.py:694
  16.8 0.0 collective-permute-done.5.end_pair
  16.8 0.0 collective-permute-done.6.end_other
  16.8 1.9 %edges.1.refs_6_ = f32[2,8,640]{2,1,0:T(8,128)S(1)} custom-call(f32[8,4,128,128]{3,2,1,0:T(8,128)S(1)} %get-tuple-element.11.fields, f32[2,128,128]{2,1,0:T(8,128)S(1)} %get-tuple-element.12.steps, f32[8,8,128]{2,1,0:T(8,128)S(1)} %get-tuple-element.13.refs_0_.own_pair, f32[8,8,128]{2,1,0:T(8,128)S(1)} %get-tuple-element.14.refs_1_.own_other, ...), custom_call_target="tpu_custom_call" | custom-call | flops 20000000000 | bytes 72000000 | tf_op jit(solution)/shard_map/edges/pallas_call | solution.py:606
  18.7 1.1 %collective-permute-start.7 = (f32[2,8,640]{2,1,0:T(8,128)S(1)}, f32[2,8,640]{2,1,0:T(8,128)S(1)}, u32[]{:S(2)}, u32[]{:S(2)}) collective-permute-start(f32[2,8,640]{2,1,0:T(8,128)S(1)} %edges.1.refs_6_), channel_id=1, source_target_pairs={{0,16},{16,0},{1,17},{17,1},{2,18},{18,2},{3,19},{19,3},{4,20},{20... | collective-permute-start | bytes 122888 | tf_op jit(solution)/shard_map/ppermute | solution.py:694
  19.7 3.1 %collective-permute-done.7.refs_7_ = f32[2,8,640]{2,1,0:T(8,128)S(1)} collective-permute-done((f32[2,8,640]{2,1,0:T(8,128)S(1)}, f32[2,8,640]{2,1,0:T(8,128)S(1)}, u32[]{:S(2)}, u32[]{:S(2)}) %collective-permute-start.7) | collective-permute-done | bytes 40992 | tf_op jit(solution)/shard_map/ppermute | solution.py:694
  22.9 0.0 collective-permute-done.4.refs_5_
  22.9 0.0 collective-permute-done.1.refs_3_
  22.9 0.0 copy-done
  22.9 0.0 copy-done.1
  22.9 0.0 copy-done.2
  22.9 1.5 %update.1 = (f32[2,128,512]{2,1,0:T(8,128)}, f32[2,128,512]{2,1,0:T(8,128)}, f32[2,128,512]{2,1,0:T(8,128)}) custom-call(f32[2,128,512]{2,1,0:T(8,128)S(1)} %copy-done, f32[2,128,512]{2,1,0:T(8,128)S(1)} %copy-done.1, f32[2,128,512]{2,1,0:T(8,128)S(1)} %copy-done.2, f32[2,40,512]{2,1,0:T(8,128)S(1)} %get-tuple-element.10.refs_0_, ...), custom_call_target="tpu_custom_call" | custom-call | tf_op jit(solution)/shard_map/update/pallas_call | solution.py:461
Async XLA Ops:
  4.2 7.7 %collective-permute-start.2 = (f32[8,8,128]{2,1,0:T(8,128)S(1)}, f32[8,8,128]{2,1,0:T(8,128)S(1)}, u32[]{:S(2)}, u32[]{:S(2)}) collective-permute-start(f32[8,8,128]{2,1,0:T(8,128)S(1)} %get-tuple-element.13.refs_0_.own_pair), channel_id=1, source_target_pairs={{0,1},{4,5},{8,9},{12,13},{2,3},{6,7},{10,11},{14,15},{1,0},{5,4},... | collective-permute-start | bytes 98312 | tf_op jit(solution)/shard_map/ppermute | solution.py:687
  7.3 4.6 %collective-permute-start.3 = (f32[8,8,128]{2,1,0:T(8,128)S(1)}, f32[8,8,128]{2,1,0:T(8,128)S(1)}, u32[]{:S(2)}, u32[]{:S(2)}) collective-permute-start(f32[8,8,128]{2,1,0:T(8,128)S(1)} %get-tuple-element.14.refs_1_.own_other), channel_id=1, source_target_pairs={{1,2},{5,6},{9,10},{13,14},{0,4},{8,12},{3,7},{11,15},{2,1},{6,5},... | collective-permute-start | bytes 98312 | tf_op jit(solution)/shard_map/ppermute | solution.py:687
  7.3 6.6 %collective-permute-start = (f32[2,40,512]{2,1,0:T(8,128)S(1)}, f32[2,40,512]{2,1,0:T(8,128)S(1)}, u32[]{:S(2)}, u32[]{:S(2)}) collective-permute-start(f32[2,40,512]{2,1,0:T(8,128)S(1)} %get-tuple-element.10.refs_0_), channel_id=1, source_target_pairs={{0,16},{16,0},{1,17},{17,1},{2,18},{18,2},{3,19},{19,3},{4,20},{20... | collective-permute-start | bytes 491528 | tf_op jit(solution)/shard_map/ppermute | solution.py:694
  11.4 11.5 %collective-permute-start.1 = (f32[2,72,512]{2,1,0:T(8,128)S(1)}, f32[2,72,512]{2,1,0:T(8,128)S(1)}, u32[]{:S(2)}, u32[]{:S(2)}) collective-permute-start(f32[2,72,512]{2,1,0:T(8,128)S(1)} %window_40.1.refs_2_), channel_id=1, source_target_pairs={{0,16},{16,0},{1,17},{17,1},{2,18},{18,2},{3,19},{19,3},{4,20},{20... | collective-permute-start | bytes 884744 | tf_op jit(solution)/shard_map/ppermute | solution.py:694
  12.1 4.7 %collective-permute-start.5 = (f32[19,8,128]{2,1,0:T(8,128)S(1)}, f32[19,8,128]{2,1,0:T(8,128)S(1)}, u32[]{:S(2)}, u32[]{:S(2)}) collective-permute-start(f32[19,8,128]{2,1,0:T(8,128)S(1)} %get-tuple-element.15.refs_4_), channel_id=1, source_target_pairs={{0,4},{1,5},{2,6},{3,7},{8,12},{9,13},{10,14},{11,15},{4,0},{5,1},... | collective-permute-start | bytes 233480 | tf_op jit(solution)/shard_map/ppermute | solution.py:687
  12.2 4.6 %collective-permute-start.6 = (f32[19,8,128]{2,1,0:T(8,128)S(1)}, f32[19,8,128]{2,1,0:T(8,128)S(1)}, u32[]{:S(2)}, u32[]{:S(2)}) collective-permute-start(f32[19,8,128]{2,1,0:T(8,128)S(1)} %get-tuple-element.16.refs_5_), channel_id=1, source_target_pairs={{4,8},{5,9},{6,10},{7,11},{0,12},{1,13},{2,14},{3,15},{8,4},{9,5},... | collective-permute-start | bytes 233480 | tf_op jit(solution)/shard_map/ppermute | solution.py:687
  14.8 8.1 %copy-start = (f32[2,128,512]{2,1,0:T(8,128)S(1)}, f32[2,128,512]{2,1,0:T(8,128)}, u32[]{:S(2)}) copy-start(f32[2,128,512]{2,1,0:T(8,128)} %maps_ref.1) | copy-start | bytes 1572868
  14.8 8.1 %copy-start.1 = (f32[2,128,512]{2,1,0:T(8,128)S(1)}, f32[2,128,512]{2,1,0:T(8,128)}, u32[]{:S(2)}) copy-start(f32[2,128,512]{2,1,0:T(8,128)} %first_ref.1) | copy-start | bytes 1572868
  14.8 8.1 %copy-start.2 = (f32[2,128,512]{2,1,0:T(8,128)S(1)}, f32[2,128,512]{2,1,0:T(8,128)}, u32[]{:S(2)}) copy-start(f32[2,128,512]{2,1,0:T(8,128)} %second_ref.1) | copy-start | bytes 1572868
  14.8 8.0 %collective-permute-start.4 = (f32[2,16,512]{2,1,0:T(8,128)S(1)}, f32[2,16,512]{2,1,0:T(8,128)S(1)}, u32[]{:S(2)}, u32[]{:S(2)}) collective-permute-start(f32[2,16,512]{2,1,0:T(8,128)S(1)} %window_112.1.refs_4_), channel_id=1, source_target_pairs={{0,16},{16,0},{1,17},{17,1},{2,18},{18,2},{3,19},{19,3},{4,20},{20... | collective-permute-start | bytes 196616 | tf_op jit(solution)/shard_map/ppermute | solution.py:694
  18.7 4.2 %collective-permute-start.7 = (f32[2,8,640]{2,1,0:T(8,128)S(1)}, f32[2,8,640]{2,1,0:T(8,128)S(1)}, u32[]{:S(2)}, u32[]{:S(2)}) collective-permute-start(f32[2,8,640]{2,1,0:T(8,128)S(1)} %edges.1.refs_6_), channel_id=1, source_target_pairs={{0,16},{16,0},{1,17},{17,1},{2,18},{18,2},{3,19},{19,3},{4,20},{20... | collective-permute-start | bytes 122888 | tf_op jit(solution)/shard_map/ppermute | solution.py:694
